TPU v7x, 32 devices: a whole 2x2x4 slice. The times are simulated.
32 devices in a mesh: dp: 8 (over z, x), tensor: 4 (over y, core).
Axes of the slice: x: 2, y: 2, z: 4, core: 2. Of those that a mesh axis runs over, the one named last changes fastest.
Arguments:
- hidden_in: bfloat16 [2, 8, 64, 1600], P(None, 'dp'), may hold values from -6 to 6
- out_grad: bfloat16 [2, 8, 64, 1600], P(None, 'dp'), may hold values from -6 to 6
- lengths: int32 [2, 8], P(None, 'dp'), may hold values from 16 to 64, as said below
- norm_gains: float32 [2, 4, 1600], replicated, may hold values from 0.5 to 1.5
- q_weight: bfloat16 [2, 1600, 1600], P(None, 'dp'), may hold values from -0.15625 to 0.15625
- kv_weight: bfloat16 [2, 1600, 2, 320], P(None, 'dp'), may hold values from -0.15625 to 0.15625
- o_weight: bfloat16 [2, 1600, 1600], P(None, None, 'dp'), may hold values from -0.15625 to 0.15625
- in_weight: bfloat16 [2, 1600, 2, 3200], P(None, 'dp', None, 'tensor'), may hold values from -0.15625 to 0.15625
- conv_weight: float32 [2, 4, 3200], P(None, None, 'tensor'), may hold values from -3 to 3
- conv_bias: float32 [2, 3200], P(None, 'tensor'), may hold values from -3 to 3
- step_bias: float32 [2, 3200], P(None, 'tensor'), may hold values from -6 to -2
- decay_log: float32 [2, 3200, 16], P(None, 'tensor'), may hold values from 0 to 2.77
- skip_gain: float32 [2, 3200], P(None, 'tensor'), may hold values from 0.5 to 1.5
- scan_weight: bfloat16 [2, 3200, 132], P(None, 'tensor'), may hold values from -0.109375 to 0.109375
- step_weight: bfloat16 [2, 100, 3200], P(None, None, 'tensor'), may hold values from -0.625 to 0.625
- ssm_weight: bfloat16 [2, 3200, 1600], P(None, 'tensor', 'dp'), may hold values from -0.109375 to 0.109375
- gate_weight: bfloat16 [2, 1600, 2, 5504], P(None, 'dp', None, 'tensor'), may hold values from -0.15625 to 0.15625
- down_weight: bfloat16 [2, 5504, 1600], P(None, 'tensor', 'dp'), may hold values from -0.078125 to 0.078125
Outputs:
- output: bfloat16 [2, 8, 64, 1600], P(None, 'dp')
- input_grad: float32 [2, 8, 64, 1600], P(None, 'dp')
- grad_norm_gains: float32 [2, 4, 1600], replicated
- grad_q_weight: float32 [2, 1600, 1600], P(None, 'dp')
- grad_kv_weight: float32 [2, 1600, 2, 320], P(None, 'dp')
- grad_o_weight: float32 [2, 1600, 1600], P(None, None, 'dp')
- grad_in_weight: float32 [2, 1600, 2, 3200], P(None, 'dp', None, 'tensor')
- grad_conv_weight: float32 [2, 4, 3200], P(None, None, 'tensor')
- grad_conv_bias: float32 [2, 3200], P(None, 'tensor')
- grad_step_bias: float32 [2, 3200], P(None, 'tensor')
- grad_decay_log: float32 [2, 3200, 16], P(None, 'tensor')
- grad_skip_gain: float32 [2, 3200], P(None, 'tensor')
- grad_scan_weight: float32 [2, 3200, 132], P(None, 'tensor')
- grad_step_weight: float32 [2, 100, 3200], P(None, None, 'tensor')
- grad_ssm_weight: float32 [2, 3200, 1600], P(None, 'tensor', 'dp')
- grad_gate_weight: float32 [2, 1600, 2, 5504], P(None, 'dp', None, 'tensor')
- grad_down_weight: float32 [2, 5504, 1600], P(None, 'tensor', 'dp')
Inputs may be any that keep to these rules, and one draw needn't show every extreme that they name: `lengths`: positions from a sequence's length to 64 are padding; in every draw some sequence has 16 tokens and some has 64.
All inputs are finite; a program needn't handle non-finite values.
Results may differ from a plain program's by a relative error of at most 0.035.
Values may be sent and summed in bfloat16 or wider, within the bound.
No kernel may reach another device: no remote copies, remote signals or barrier semaphores. Data moves between devices by JAX's collectives and lax.ppermute only.
A program may use at most 448 MiB of HBM per device.

v0:
```python
import jax
import jax.numpy as jnp
from jax import lax
from jax.sharding import PartitionSpec as P

KVH = 5
HEAD = 64
CONV = 4
WINDOW = 1024
SCAN_BLOCK = 64
GQ = 5
QD = 1600
KVD = 320


EPSILON = 1e-06


def rms_scale(values, gain_vec):
    return (
        values * lax.rsqrt(jnp.mean(values * values, axis=-1, keepdims=True) + EPSILON) * gain_vec
    )


def conv_silu(inner_in, conv_taps, conv_shift):
    length = inner_in.shape[0]
    padded = jnp.pad(inner_in, ((CONV - 1, 0), (0, 0)))
    running = conv_shift
    for offset in range(CONV):
        running = running + padded[offset : offset + length] * conv_taps[offset]
    return jax.nn.silu(running)


def combine_steps(earlier, later):
    return (earlier[0] * later[0], later[0] * earlier[1] + later[1])


def ssm_tail(step_raw, conv_out, drive_in, read_out, gate_in, step_shift, log_rates, skip_scale):
    step_size = jax.nn.softplus(step_raw + step_shift)
    rate_mat = -jnp.exp(log_rates).T
    length = conv_out.shape[0]
    blocks = length // SCAN_BLOCK

    def advance(state_in, block_in):
        conv_blk, step_blk, drive_blk, read_blk = block_in
        decay_step = jnp.exp(step_blk[:, None, :] * rate_mat[None])
        source = (step_blk * conv_blk)[:, None, :] * drive_blk[:, :, None]
        acc_decay, acc_source = lax.associative_scan(combine_steps, (decay_step, source), axis=0)
        states = acc_decay * state_in[None] + acc_source
        return (states[-1], jnp.sum(states * read_blk[:, :, None], axis=1))

    def shaped(values):
        return values.reshape((blocks, SCAN_BLOCK) + values.shape[1:])

    initial = jnp.zeros(rate_mat.shape, jnp.float32)
    _, outputs = lax.scan(
        jax.checkpoint(advance),
        initial,
        (shaped(conv_out), shaped(step_size), shaped(drive_in), shaped(read_out)),
    )
    scanned = outputs.reshape(length, -1) + skip_scale * conv_out
    return scanned * jax.nn.silu(gate_in)


def mix_branches(resid_in, attn_out, ssm_out, gain_attn, gain_ssm, gain_ffn):
    residual = resid_in + 0.5 * (rms_scale(attn_out, gain_attn) + rms_scale(ssm_out, gain_ssm))
    return (residual, rms_scale(residual, gain_ffn))


def gate_product(gate_out):
    return jax.nn.silu(gate_out[:, 0]) * gate_out[:, 1]


def score_block(query_blk, key_rows, first_row):
    row_count = query_blk.shape[0]
    scores = jnp.einsum(
        "qrd,kd->rqk", query_blk, key_rows, preferred_element_type=jnp.float32
    ) * HEAD ** (-0.5)
    query_pos = first_row + jnp.arange(row_count)
    key_pos = jnp.arange(key_rows.shape[0])
    allowed = (key_pos[None, :] <= query_pos[:, None]) & (
        key_pos[None, :] > query_pos[:, None] - WINDOW
    )
    return jnp.where(allowed[None], scores, -jnp.inf)


def attend_forward(queries, keyval):
    length = queries.shape[0]
    block_rows = min(length, 512)
    count_blk = length // block_rows
    query_blocks = queries.reshape(count_blk, block_rows, GQ, HEAD)
    key_rows = keyval[:, 0]
    value_rows = keyval[:, 1]

    def one_block(block_in):
        query_blk, first_row = block_in
        scores = score_block(query_blk, key_rows, first_row)
        row_max = jnp.max(scores, axis=-1, keepdims=True)
        weights = jnp.exp(scores - row_max)
        norm_sum = jnp.sum(weights, axis=-1, keepdims=True)
        probability = (weights / norm_sum).astype(jnp.bfloat16)
        heads_out = jnp.einsum(
            "rqk,kd->qrd", probability, value_rows, preferred_element_type=jnp.float32
        )
        return (
            heads_out.astype(jnp.bfloat16).reshape(block_rows, GQ * HEAD),
            (row_max + jnp.log(norm_sum))[..., 0],
        )

    outputs, log_sums = lax.map(one_block, (query_blocks, jnp.arange(count_blk) * block_rows))
    return (outputs.reshape(length, GQ * HEAD), log_sums)


def attend_backward(queries, keyval, log_sums, grad_heads):
    length = queries.shape[0]
    block_rows = min(length, 512)
    count_blk = length // block_rows
    query_blocks = queries.reshape(count_blk, block_rows, GQ, HEAD)
    grad_blocks = grad_heads.reshape(count_blk, block_rows, GQ, HEAD)
    key_rows = keyval[:, 0]
    value_rows = keyval[:, 1]

    def one_block(sums_in, block_in):
        query_blk, grad_blk, lse_blk, first_row = block_in
        scores = score_block(query_blk, key_rows, first_row)
        probability = jnp.exp(scores - lse_blk[..., None])
        grad_prob = jnp.einsum(
            "qrd,kd->rqk", grad_blk, value_rows, preferred_element_type=jnp.float32
        )
        grad_scores = (
            probability
            * (grad_prob - jnp.sum(grad_prob * probability, axis=-1, keepdims=True))
            * HEAD ** (-0.5)
        ).astype(jnp.bfloat16)
        grad_query = jnp.einsum(
            "rqk,kd->qrd", grad_scores, key_rows, preferred_element_type=jnp.float32
        )
        grad_key = jnp.einsum(
            "rqk,qrd->kd", grad_scores, query_blk, preferred_element_type=jnp.float32
        )
        grad_value = jnp.einsum(
            "rqk,qrd->kd",
            probability.astype(jnp.bfloat16),
            grad_blk,
            preferred_element_type=jnp.float32,
        )
        return (
            (sums_in[0] + grad_key, sums_in[1] + grad_value),
            grad_query.reshape(block_rows, GQ * HEAD),
        )

    zero_rows = jnp.zeros((length, HEAD), jnp.float32)
    sums_out, grad_query = lax.scan(
        one_block,
        (zero_rows, zero_rows),
        (query_blocks, grad_blocks, log_sums, jnp.arange(count_blk) * block_rows),
    )
    return (grad_query.reshape(length, GQ * HEAD), jnp.stack(sums_out, axis=1))


def per_device(
    hidden_in,
    out_grad,
    lengths,
    norm_gains,
    q_weight,
    kv_weight,
    o_weight,
    in_weight,
    conv_weight,
    conv_bias,
    step_bias,
    decay_log,
    skip_gain,
    scan_weight,
    step_weight,
    ssm_weight,
    gate_weight,
    down_weight,
):
    layer_count = q_weight.shape[0]
    batches = hidden_in.shape[0]
    length = hidden_in.shape[2]
    model_width = hidden_in.shape[3]
    rank_cols = step_weight.shape[1]
    state_cols = decay_log.shape[2]
    group_cols = GQ * HEAD
    block_rows = min(length, 512)
    count_blk = length // block_rows
    tensor_idx = lax.axis_index("tensor")
    first_group = jnp.where(tensor_idx == 0, 0, tensor_idx + 1)
    group_count = jnp.where(tensor_idx == 0, 2, 1)
    window_start = jnp.minimum(first_group, KVH - 2)
    slot_offset = first_group - window_start

    def fetch_layer(layer_idx):
        query_cols = lax.dynamic_slice_in_dim(
            q_weight[layer_idx], window_start * group_cols, 2 * group_cols, 1
        )
        keyval_cols = lax.dynamic_slice_in_dim(
            kv_weight[layer_idx], window_start * HEAD, 2 * HEAD, 2
        )
        output_rows = lax.dynamic_slice_in_dim(
            o_weight[layer_idx], window_start * group_cols, 2 * group_cols, 0
        )
        return (
            lax.all_gather(query_cols, "dp", axis=0, tiled=True),
            lax.all_gather(keyval_cols, "dp", axis=0, tiled=True),
            lax.all_gather(output_rows, "dp", axis=1, tiled=True),
            lax.all_gather(in_weight[layer_idx], "dp", axis=0, tiled=True),
            lax.all_gather(ssm_weight[layer_idx], "dp", axis=1, tiled=True),
            lax.all_gather(gate_weight[layer_idx], "dp", axis=0, tiled=True),
            lax.all_gather(down_weight[layer_idx], "dp", axis=1, tiled=True),
        )

    def settle(big_part):
        shares = (
            lax.psum_scatter(
                big_part[0].astype(jnp.bfloat16), "dp", scatter_dimension=0, tiled=True
            ).astype(jnp.float32),
            lax.psum_scatter(
                big_part[1].astype(jnp.bfloat16), "dp", scatter_dimension=0, tiled=True
            ).astype(jnp.float32),
            lax.psum_scatter(
                big_part[2].astype(jnp.bfloat16), "dp", scatter_dimension=1, tiled=True
            ).astype(jnp.float32),
            lax.psum_scatter(
                big_part[3].astype(jnp.bfloat16), "dp", scatter_dimension=0, tiled=True
            ).astype(jnp.float32),
            lax.psum_scatter(
                big_part[4].astype(jnp.bfloat16), "dp", scatter_dimension=1, tiled=True
            ).astype(jnp.float32),
            lax.psum_scatter(
                big_part[5].astype(jnp.bfloat16), "dp", scatter_dimension=0, tiled=True
            ).astype(jnp.float32),
            lax.psum_scatter(
                big_part[6].astype(jnp.bfloat16), "dp", scatter_dimension=1, tiled=True
            ).astype(jnp.float32),
        )
        rows_here = shares[0].shape[0]
        full_query = lax.dynamic_update_slice_in_dim(
            jnp.zeros((rows_here, QD), jnp.float32), shares[0], window_start * group_cols, 1
        )
        full_keyval = lax.dynamic_update_slice_in_dim(
            jnp.zeros((rows_here, 2, KVD), jnp.float32), shares[1], window_start * HEAD, 2
        )
        full_heads = lax.dynamic_update_slice_in_dim(
            jnp.zeros((QD, shares[2].shape[1]), jnp.float32),
            shares[2],
            window_start * group_cols,
            0,
        )
        summed = (
            lax.psum(full_query.astype(jnp.bfloat16), "tensor").astype(jnp.float32),
            lax.psum(full_keyval.astype(jnp.bfloat16), "tensor").astype(jnp.float32),
            lax.psum(full_heads.astype(jnp.bfloat16), "tensor").astype(jnp.float32),
        )
        return (summed[0], summed[1], summed[2], shares[3], shares[4], shares[5], shares[6])

    fetched = [fetch_layer(layer_idx) for layer_idx in range(layer_count)]
    big_sums = [None] * layer_count
    small_sums = [None] * layer_count
    outputs = []
    input_grads = []
    for batch_idx in range(batches):
        running = hidden_in[batch_idx, 0].astype(jnp.float32)
        kept_list = []
        weight_list = []
        for layer_idx in range(layer_count):
            weights_now = fetched[layer_idx]
            query_mat, keyval_mat, heads_mat, inner_mat, ssm_mat, gate_mat, down_mat = weights_now
            gains = norm_gains[layer_idx]
            normed, pull_input = jax.vjp(rms_scale, running, gains[0])
            normed_b16 = normed.astype(jnp.bfloat16)

            def group_forward(group_idx, state_in):
                attn_acc, saved_query, saved_keyval, saved_heads, saved_lse = state_in
                slot_pos = slot_offset + group_idx
                query_slice = lax.dynamic_slice_in_dim(
                    query_mat, slot_pos * group_cols, group_cols, 1
                )
                keyval_slice = lax.dynamic_slice_in_dim(keyval_mat, slot_pos * HEAD, HEAD, 2)
                heads_slice = lax.dynamic_slice_in_dim(
                    heads_mat, slot_pos * group_cols, group_cols, 0
                )
                queries = jnp.dot(
                    normed_b16, query_slice, preferred_element_type=jnp.float32
                ).astype(jnp.bfloat16)
                keyval = jnp.einsum(
                    "sd,dkc->skc", normed_b16, keyval_slice, preferred_element_type=jnp.float32
                ).astype(jnp.bfloat16)
                heads_out, log_sums = attend_forward(queries, keyval)
                attn_acc = attn_acc + jnp.dot(
                    heads_out, heads_slice, preferred_element_type=jnp.float32
                )
                return (
                    attn_acc,
                    saved_query.at[group_idx].set(queries),
                    saved_keyval.at[group_idx].set(keyval),
                    saved_heads.at[group_idx].set(heads_out),
                    saved_lse.at[group_idx].set(log_sums),
                )

            start_state = (
                jnp.zeros((length, model_width), jnp.float32),
                jnp.zeros((2, length, group_cols), jnp.bfloat16),
                jnp.zeros((2, length, 2, HEAD), jnp.bfloat16),
                jnp.zeros((2, length, group_cols), jnp.bfloat16),
                jnp.zeros((2, count_blk, GQ, block_rows), jnp.float32),
            )
            attn_part, saved_query, saved_keyval, saved_heads, saved_lse = lax.fori_loop(
                0, group_count, group_forward, start_state
            )
            inner_out = jnp.einsum(
                "sd,dkc->skc", normed_b16, inner_mat, preferred_element_type=jnp.float32
            )
            conv_out, pull_conv = jax.vjp(
                conv_silu, inner_out[:, 0], conv_weight[layer_idx], conv_bias[layer_idx]
            )
            conv_b16 = conv_out.astype(jnp.bfloat16)
            scan_proj = lax.psum(
                jnp.dot(
                    conv_b16, scan_weight[layer_idx], preferred_element_type=jnp.float32
                ).astype(jnp.bfloat16),
                "tensor",
            ).astype(jnp.float32)
            step_low = scan_proj[:, :rank_cols].astype(jnp.bfloat16)
            step_raw = jnp.dot(step_low, step_weight[layer_idx], preferred_element_type=jnp.float32)
            gated, pull_tail = jax.vjp(
                ssm_tail,
                step_raw,
                conv_b16.astype(jnp.float32),
                scan_proj[:, rank_cols : rank_cols + state_cols],
                scan_proj[:, rank_cols + state_cols :],
                inner_out[:, 1],
                step_bias[layer_idx],
                decay_log[layer_idx],
                skip_gain[layer_idx],
            )
            gated_b16 = gated.astype(jnp.bfloat16)
            ssm_part = jnp.dot(gated_b16, ssm_mat, preferred_element_type=jnp.float32)
            attn_out = lax.psum(attn_part.astype(jnp.bfloat16), "tensor").astype(jnp.float32)
            ssm_out = lax.psum(ssm_part.astype(jnp.bfloat16), "tensor").astype(jnp.float32)
            (residual, ffn_in), pull_mix = jax.vjp(
                mix_branches, running, attn_out, ssm_out, gains[1], gains[2], gains[3]
            )
            ffn_b16 = ffn_in.astype(jnp.bfloat16)
            gate_out = jnp.einsum(
                "sd,dkf->skf", ffn_b16, gate_mat, preferred_element_type=jnp.float32
            )
            activ, pull_act = jax.vjp(gate_product, gate_out)
            activ_b16 = activ.astype(jnp.bfloat16)
            ffn_out = lax.psum(
                jnp.dot(activ_b16, down_mat, preferred_element_type=jnp.float32).astype(
                    jnp.bfloat16
                ),
                "tensor",
            ).astype(jnp.float32)
            kept_state = (
                normed_b16,
                pull_input,
                saved_query,
                saved_keyval,
                saved_heads,
                saved_lse,
                pull_conv,
                conv_b16,
                step_low,
                pull_tail,
                gated_b16,
                pull_mix,
                ffn_b16,
                pull_act,
                activ_b16,
            )
            running, kept_state = (residual + ffn_out, kept_state)
            kept_list.append(kept_state)
            weight_list.append(weights_now)
        pad_mask = (jnp.arange(length) < lengths[batch_idx, 0]).astype(jnp.float32)[:, None]
        outputs.append((running * pad_mask).astype(jnp.bfloat16))
        grad_run = out_grad[batch_idx, 0].astype(jnp.float32) * pad_mask
        for layer_idx in reversed(range(layer_count)):
            backward_kept_state = kept_list[layer_idx]
            backward_weights = weight_list[layer_idx]
            (
                backward_query_mat,
                backward_keyval_mat,
                backward_heads_mat,
                backward_inner_mat,
                backward_ssm_mat,
                backward_gate_mat,
                backward_down_mat,
            ) = backward_weights
            (
                backward_normed_b16,
                backward_pull_input,
                backward_saved_query,
                backward_saved_keyval,
                backward_saved_heads,
                backward_saved_lse,
                backward_pull_conv,
                backward_conv_b16,
                backward_step_low,
                backward_pull_tail,
                backward_gated_b16,
                backward_pull_mix,
                backward_ffn_b16,
                backward_pull_act,
                backward_activ_b16,
            ) = backward_kept_state
            grad_ffn = grad_run.astype(jnp.bfloat16)
            grad_down = jnp.dot(backward_activ_b16.T, grad_ffn, preferred_element_type=jnp.float32)
            grad_activ = jnp.dot(grad_ffn, backward_down_mat.T, preferred_element_type=jnp.float32)
            (grad_gate_out,) = backward_pull_act(grad_activ)
            gate_b16 = grad_gate_out.astype(jnp.bfloat16)
            grad_gate = jnp.einsum(
                "sd,skf->dkf", backward_ffn_b16, gate_b16, preferred_element_type=jnp.float32
            )
            grad_ffn_in = lax.psum(
                jnp.einsum(
                    "skf,dkf->sd", gate_b16, backward_gate_mat, preferred_element_type=jnp.float32
                ).astype(jnp.bfloat16),
                "tensor",
            ).astype(jnp.float32)
            grad_resid, grad_attn, grad_ssm, grad_gain_attn, grad_gain_ssm, grad_gain_ffn = (
                backward_pull_mix((grad_run, grad_ffn_in))
            )
            attn_b16 = grad_attn.astype(jnp.bfloat16)
            ssm_b16 = grad_ssm.astype(jnp.bfloat16)
            grad_ssm_mat = jnp.dot(
                backward_gated_b16.T, ssm_b16, preferred_element_type=jnp.float32
            )
            grad_gated = jnp.dot(ssm_b16, backward_ssm_mat.T, preferred_element_type=jnp.float32)
            (
                grad_step_raw,
                grad_conv_scan,
                grad_drive,
                grad_read,
                grad_gate_in,
                grad_step_bias,
                grad_decay,
                grad_skip,
            ) = backward_pull_tail(grad_gated)
            step_b16 = grad_step_raw.astype(jnp.bfloat16)
            grad_step_mat = jnp.dot(
                backward_step_low.T, step_b16, preferred_element_type=jnp.float32
            )
            grad_low = jnp.dot(
                step_b16, step_weight[layer_idx].T, preferred_element_type=jnp.float32
            )
            grad_proj = lax.psum(
                jnp.concatenate([grad_low, grad_drive, grad_read], axis=1).astype(jnp.bfloat16),
                "tensor",
            )
            grad_scan_mat = jnp.dot(
                backward_conv_b16.T, grad_proj, preferred_element_type=jnp.float32
            )
            grad_conv_out = grad_conv_scan + jnp.dot(
                grad_proj, scan_weight[layer_idx].T, preferred_element_type=jnp.float32
            )
            grad_inner_x, grad_conv_taps, grad_conv_shift = backward_pull_conv(grad_conv_out)
            inner_b16 = jnp.stack([grad_inner_x, grad_gate_in], axis=1).astype(jnp.bfloat16)
            grad_inner_mat = jnp.einsum(
                "sd,skc->dkc", backward_normed_b16, inner_b16, preferred_element_type=jnp.float32
            )
            grad_normed = jnp.einsum(
                "skc,dkc->sd", inner_b16, backward_inner_mat, preferred_element_type=jnp.float32
            )

            def group_backward(group_idx, state_in):
                grad_acc, grad_query_mat, grad_keyval_mat, grad_heads_mat = state_in
                slot_pos = slot_offset + group_idx
                query_slice = lax.dynamic_slice_in_dim(
                    backward_query_mat, slot_pos * group_cols, group_cols, 1
                )
                keyval_slice = lax.dynamic_slice_in_dim(
                    backward_keyval_mat, slot_pos * HEAD, HEAD, 2
                )
                heads_slice = lax.dynamic_slice_in_dim(
                    backward_heads_mat, slot_pos * group_cols, group_cols, 0
                )
                grad_heads = jnp.dot(
                    attn_b16, heads_slice.T, preferred_element_type=jnp.float32
                ).astype(jnp.bfloat16)
                heads_part = jnp.dot(
                    backward_saved_heads[group_idx].T, attn_b16, preferred_element_type=jnp.float32
                )
                grad_query, grad_keyval = attend_backward(
                    backward_saved_query[group_idx],
                    backward_saved_keyval[group_idx],
                    backward_saved_lse[group_idx],
                    grad_heads,
                )
                query_b16 = grad_query.astype(jnp.bfloat16)
                keyval_b16 = grad_keyval.astype(jnp.bfloat16)
                grad_acc = grad_acc + jnp.dot(
                    query_b16, query_slice.T, preferred_element_type=jnp.float32
                )
                grad_acc = grad_acc + jnp.einsum(
                    "skc,dkc->sd", keyval_b16, keyval_slice, preferred_element_type=jnp.float32
                )
                query_part = jnp.dot(
                    backward_normed_b16.T, query_b16, preferred_element_type=jnp.float32
                )
                keyval_part = jnp.einsum(
                    "sd,skc->dkc",
                    backward_normed_b16,
                    keyval_b16,
                    preferred_element_type=jnp.float32,
                )
                grad_query_mat = lax.dynamic_update_slice_in_dim(
                    grad_query_mat, query_part, slot_pos * group_cols, 1
                )
                grad_keyval_mat = lax.dynamic_update_slice_in_dim(
                    grad_keyval_mat, keyval_part, slot_pos * HEAD, 2
                )
                grad_heads_mat = lax.dynamic_update_slice_in_dim(
                    grad_heads_mat, heads_part, slot_pos * group_cols, 0
                )
                return (grad_acc, grad_query_mat, grad_keyval_mat, grad_heads_mat)

            backward_start_state = (
                grad_normed,
                jnp.zeros((model_width, 2 * group_cols), jnp.float32),
                jnp.zeros((model_width, 2, 2 * HEAD), jnp.float32),
                jnp.zeros((2 * group_cols, model_width), jnp.float32),
            )
            grad_normed, grad_query_mat, grad_keyval_mat, grad_heads_mat = lax.fori_loop(
                0, group_count, group_backward, backward_start_state
            )
            grad_normed = lax.psum(grad_normed.astype(jnp.bfloat16), "tensor").astype(jnp.float32)
            grad_lower, grad_gain_input = backward_pull_input(grad_normed)
            backward_big_part = (
                grad_query_mat,
                grad_keyval_mat,
                grad_heads_mat,
                grad_inner_mat,
                grad_ssm_mat,
                grad_gate,
                grad_down,
            )
            small_part = (
                jnp.stack([grad_gain_input, grad_gain_attn, grad_gain_ssm, grad_gain_ffn]),
                grad_conv_taps,
                grad_conv_shift,
                grad_step_bias,
                grad_decay,
                grad_skip,
                grad_scan_mat,
                grad_step_mat,
            )
            grad_run, big_part, small_part = (
                grad_resid + grad_lower,
                backward_big_part,
                small_part,
            )
            big_sums[layer_idx] = (
                big_part if batch_idx == 0 else jax.tree.map(jnp.add, big_sums[layer_idx], big_part)
            )
            small_sums[layer_idx] = (
                small_part
                if batch_idx == 0
                else jax.tree.map(jnp.add, small_sums[layer_idx], small_part)
            )
        input_grads.append(grad_run)
    big_sums = [settle(big_part) for big_part in big_sums]

    def stacked(member):
        return jnp.stack([small_sums[layer_idx][member] for layer_idx in range(layer_count)])

    def big_stack(member):
        return jnp.stack([big_sums[layer_idx][member] for layer_idx in range(layer_count)])

    small_total = (
        lax.psum(stacked(0).astype(jnp.bfloat16), "dp").astype(jnp.float32),
        lax.psum(stacked(1).astype(jnp.bfloat16), "dp").astype(jnp.float32),
        lax.psum(stacked(2).astype(jnp.bfloat16), "dp").astype(jnp.float32),
        lax.psum(stacked(3).astype(jnp.bfloat16), "dp").astype(jnp.float32),
        lax.psum(stacked(4).astype(jnp.bfloat16), "dp").astype(jnp.float32),
        lax.psum(stacked(5).astype(jnp.bfloat16), "dp").astype(jnp.float32),
        lax.psum(stacked(6).astype(jnp.bfloat16), "dp").astype(jnp.float32),
        lax.psum(stacked(7).astype(jnp.bfloat16), "dp").astype(jnp.float32),
    )
    output = jnp.stack(outputs)[:, None]
    input_grad = jnp.stack(input_grads)[:, None]
    return (
        output,
        input_grad,
        small_total[0],
        big_stack(0),
        big_stack(1),
        big_stack(2),
        big_stack(3),
        small_total[1],
        small_total[2],
        small_total[3],
        small_total[4],
        small_total[5],
        small_total[6],
        small_total[7],
        big_stack(4),
        big_stack(5),
        big_stack(6),
    )


def solution(mesh):
    return jax.shard_map(
        per_device,
        mesh=mesh,
        in_specs=(
            P(None, "dp", None, None),
            P(None, "dp", None, None),
            P(None, "dp"),
            P(),
            P(None, "dp", None),
            P(None, "dp", None, None),
            P(None, None, "dp"),
            P(None, "dp", None, "tensor"),
            P(None, None, "tensor"),
            P(None, "tensor"),
            P(None, "tensor"),
            P(None, "tensor", None),
            P(None, "tensor"),
            P(None, "tensor", None),
            P(None, None, "tensor"),
            P(None, "tensor", "dp"),
            P(None, "dp", None, "tensor"),
            P(None, "tensor", "dp"),
        ),
        out_specs=(
            P(None, "dp", None, None),
            P(None, "dp", None, None),
            P(),
            P(None, "dp", None),
            P(None, "dp", None, None),
            P(None, None, "dp"),
            P(None, "dp", None, "tensor"),
            P(None, None, "tensor"),
            P(None, "tensor"),
            P(None, "tensor"),
            P(None, "tensor", None),
            P(None, "tensor"),
            P(None, "tensor", None),
            P(None, None, "tensor"),
            P(None, "tensor", "dp"),
            P(None, "dp", None, "tensor"),
            P(None, "tensor", "dp"),
        ),
        check_vma=False,
    )
```

profile of v0, /device:TPU:0, one launch (start us, length us, event | category | flops | bytes accessed | tf_op | source)
XLA Modules:
  0.0 5468.0 jit_solution(4633568901307685865)
XLA Ops:
  25.2 35.3 all-gather
  73.1 48.6 all-gather.27.cloned.1.call-done
  125.0 30.1 while.140
  160.2 30.6 while.142
  192.9 22.3 all-gather.31.cloned.1.call-done
  591.7 25.4 all-reduce.507.cloned.1.call-done
  623.5 129.6 %all-gather.35.cloned.1.call-done = bf16[1,1600,2,1376]{3,1,2,0:T(8,128)(2,1)} async-done(((bf16[1,200,2,1376]{3,1,2,0:T(8,128)(2,1)}), bf16[1,1600,2,1376]{3,1,2,0:T(8,128)(2,1)}) %all-gather.35.cloned.1.call-update) | async-done | bytes 8806416 | tf_op jit(solution)/shard_map/all_gather | solution.py:212
  758.3 73.3 %all-gather.37.cloned.1.call-done = bf16[1,1376,1600]{1,2,0:T(8,128)(2,1)} async-done(((bf16[1,1376,200]{1,2,0:T(8,128)(2,1)}), bf16[1,1376,1600]{1,2,0:T(8,128)(2,1)}) %all-gather.37.cloned.1.call-update) | async-done | bytes 4403216 | tf_op jit(solution)/shard_map/all_gather | solution.py:213
  850.1 33.9 all-gather.7
  893.8 91.4 %all-gather.43.cloned.1.call-done = bf16[1,1600,2,800]{3,2,0,1:T(2,128)(2,1)} async-done(((bf16[1,200,2,800]{3,2,0,1:T(2,128)(2,1)}), bf16[1,1600,2,800]{3,2,0,1:T(2,128)(2,1)}) %all-gather.43.cloned.1.call-update) | async-done | bytes 5120016 | tf_op jit(solution)/shard_map/all_gather | solution.py:210
  1141.8 27.7 while.141
  1172.2 27.6 while.143
  1471.1 30.0 all-reduce.503.cloned.1.call-done
  1508.3 128.8 %all-gather.47.cloned.1.call-done = bf16[1,1600,2,1376]{3,1,2,0:T(8,128)(2,1)} async-done(((bf16[1,200,2,1376]{3,1,2,0:T(8,128)(2,1)}), bf16[1,1600,2,1376]{3,1,2,0:T(8,128)(2,1)}) %all-gather.47.cloned.1.call-update) | async-done | bytes 8806416 | tf_op jit(solution)/shard_map/all_gather | solution.py:212
  1645.6 69.2 %all-gather.49.cloned.1.call-done = bf16[1,1376,1600]{1,2,0:T(8,128)(2,1)} async-done(((bf16[1,1376,200]{1,2,0:T(8,128)(2,1)}), bf16[1,1376,1600]{1,2,0:T(8,128)(2,1)}) %all-gather.49.cloned.1.call-update) | async-done | bytes 4403216 | tf_op jit(solution)/shard_map/all_gather | solution.py:213
  1731.7 31.1 all-reduce.501.cloned.1.call-done
  2678.5 37.0 while.144
  2730.3 36.9 while.146
  2780.7 21.6 all-reduce.499.cloned.1.call-done
  3771.9 37.1 while.147
  3822.0 57.6 %while.145 = (s32[]{:T(128)}, f32[64,1600]{1,0:T(8,128)}, f32[1600,640]{0,1:T(8,128)}, f32[1600,2,128]{0,2,1:T(8,128)}, f32[640,1600]{1,0:T(8,128)}, /*index=5*/...) while((s32[]{:T(128)}, f32[64,1600]{1,0:T(8,128)}, ...), condition=%wide.region_85.87_spmd, body=%wide.region_83.86_spmd.sunk | while | flops 328250176 | bytes 58676044 | solution.py:528
  3983.5 62.7 %reduce-scatter.41.cloned.1.call-done = bf16[640,200]{0,1:T(8,128)(2,1)} async-done(((bf16[640,1600]{0,1:T(8,128)(2,1)}), bf16[640,200]{0,1:T(8,128)(2,1)}) %reduce-scatter.41.cloned.1.call-update) | async-done | bytes 256016
  4049.9 440.2 %all-reduce.493.cloned.1.call-done = (bf16[2,800,132]{1,2,0:T(8,128)(2,1)}, bf16[2,100,800]{2,1,0:T(8,128)(2,1)}, bf16[1600,2,128]{2,1,0:T(2,128)(2,1)}, bf16[16...) async-done(((bf16[2,800,132]{1,2,0:T(8,128)(2,1)}, bf16[2,100,800]{2,1,0:T(8,128)(2,1)}, bf16[1600,2,128]{2,1,0:T(2,128)(2,1)}, ...) | async-done | bytes 12620816 | tf_op jit(solution)/shard_map/psum | solution.py:581
  4558.9 90.9 %all-reduce.495.cloned.1.call-done = (bf16[64,1600]{1,0:T(8,128)(2,1)}, bf16[64,1600]{1,0:T(8,128)(2,1)}, bf16[64,1600]{1,0:T(8,128)(2,1)}, bf16[64,1600]{1,0:T(...) async-done(((bf16[64,1600]{1,0:T(8,128)(2,1)}, ...) | async-done | bytes 3891216 | tf_op jit(solution)/shard_map/psum | solution.py:353
  4661.8 29.2 copy.565
  4729.1 29.3 copy.563
  4777.5 48.4 reduce-scatter.45.cloned.1.call-done
  4828.2 112.8 %reduce-scatter.51.cloned.1.call-done = bf16[1376,200]{0,1:T(8,128)(2,1)} async-done(((bf16[1376,1600]{0,1:T(8,128)(2,1)}), bf16[1376,200]{0,1:T(8,128)(2,1)}) %reduce-scatter.51.cloned.1.call-update) | async-done | bytes 550416
  4941.0 114.2 %reduce-scatter.49.cloned.1.call-done = bf16[1376,200]{0,1:T(8,128)(2,1)} async-done(((bf16[1376,1600]{0,1:T(8,128)(2,1)}), bf16[1376,200]{0,1:T(8,128)(2,1)}) %reduce-scatter.49.cloned.1.call-update) | async-done | bytes 550416
  5074.0 56.9 %all-reduce.491.cloned.1.call-done = (bf16[2,4,1600]{2,1,0:T(4,128)(2,1)}, bf16[2,4,800]{2,1,0:T(4,128)(2,1)}, bf16[2,800]{1,0:T(2,128)(2,1)}, bf16[2,800]{1,0:T...) async-done(((bf16[2,4,1600]{2,1,0:T(4,128)(2,1)}, bf16[2,4,800]{2,1,0:T(4,128)(2,1)}, bf16[2,800]{1,0:T(2,128)(2,1)}, bf16[2,800]{1,0:T(2,128)(2,1)}, ...) | async-done | bytes 99216 | tf_op jit(solution)/shard_map/psum | solution.py:575
  5138.9 153.1 %reduce-scatter.35.cloned.1.call-done = bf16[200,2752]{1,0:T(8,128)(2,1)} async-done(((bf16[1600,2752]{1,0:T(8,128)(2,1)}), bf16[200,2752]{1,0:T(8,128)(2,1)}) %reduce-scatter.35.cloned.1.call-update) | async-done | bytes 1100816
  5295.2 157.4 %reduce-scatter.33.cloned.1.call-done = bf16[200,2752]{1,0:T(8,128)(2,1)} async-done(((bf16[1600,2752]{1,0:T(8,128)(2,1)}), bf16[200,2752]{1,0:T(8,128)(2,1)}) %reduce-scatter.33.cloned.1.call-update) | async-done | bytes 1100816
  (3389 shorter events, 3406.5 us)
Async XLA Ops:
  7.2 62.8 %all-gather.29.cloned.1.call-start = ((), (), s32[]{:S(2)}) async-start(), calls=%async_computation.11 | async-start | bytes 2304000 | tf_op jit(solution)/shard_map/all_gather | solution.py:209
  10.5 111.2 %all-gather.27.cloned.1.call-start = ((), (), s32[]{:S(2)}) async-start(), calls=%async_computation.10 | async-start | bytes 2304000 | tf_op jit(solution)/shard_map/all_gather | solution.py:207
  12.3 202.9 %all-gather.31.cloned.1.call-start = ((), (), s32[]{:S(2)}) async-start(), calls=%async_computation.12 | async-start | bytes 6451200 | tf_op jit(solution)/shard_map/all_gather | solution.py:210
  14.5 563.4 %all-gather.33.cloned.1.call-start = ((), (), s32[]{:S(2)}) async-start(), calls=%async_computation.13 | async-start | bytes 3225600 | tf_op jit(solution)/shard_map/all_gather | solution.py:211
  15.6 601.5 %all-reduce.507.cloned.1.call-start = ((), (), s32[]{:S(2)}) async-start(), calls=%async_computation.40 | async-start | bytes 1703936 | tf_op jit(solution)/shard_map/psum | solution.py:343
  16.4 819.7 %copy-start.540 = (f32[1600]{0:T(1024)}, f32[1600]{0:T(1024)S(1)}, u32[]{:S(2)}) copy-start(f32[1600]{0:T(1024)S(1)} %get-tuple-element.2849) | copy-start | bytes 19204
  583.3 169.8 %all-gather.35.cloned.1.call-start = ((), (), s32[]{:S(2)}) async-start(), calls=%async_computation.14 | async-start | bytes 10137600 | tf_op jit(solution)/shard_map/all_gather | solution.py:212
  586.9 244.6 %all-gather.37.cloned.1.call-start = ((), (), s32[]{:S(2)}) async-start(), calls=%async_computation.15 | async-start | bytes 5068800 | tf_op jit(solution)/shard_map/all_gather | solution.py:213
  588.6 302.1 %all-gather.41.cloned.1.call-start = ((), (), s32[]{:S(2)}) async-start(), calls=%async_computation.17 | async-start | bytes 2304000 | tf_op jit(solution)/shard_map/all_gather | solution.py:209
  590.5 394.6 %all-gather.43.cloned.1.call-start = ((), (), s32[]{:S(2)}) async-start(), calls=%async_computation.18 | async-start | bytes 6451200 | tf_op jit(solution)/shard_map/all_gather | solution.py:210
  591.3 428.5 %all-reduce.505.cloned.1.call-start = ((), (), s32[]{:S(2)}) async-start(), calls=%async_computation.39 | async-start | bytes 851968 | tf_op jit(solution)/shard_map/psum | solution.py:353
  845.0 294.0 %all-gather.39.cloned.1.call-start = ((), (), s32[]{:S(2)}) async-start(), calls=%async_computation.16 | async-start | bytes 2304000 | tf_op jit(solution)/shard_map/all_gather | solution.py:207
  846.9 613.3 %all-gather.45.cloned.1.call-start = ((), (), s32[]{:S(2)}) async-start(), calls=%async_computation.19 | async-start | bytes 3225600 | tf_op jit(solution)/shard_map/all_gather | solution.py:211
  847.5 653.6 %all-reduce.503.cloned.1.call-start = ((), (), s32[]{:S(2)}) async-start(), calls=%async_computation.38 | async-start | bytes 1703936 | tf_op jit(solution)/shard_map/psum | solution.py:343
  1465.6 171.5 %all-gather.47.cloned.1.call-start = ((), (), s32[]{:S(2)}) async-start(), calls=%async_computation.20 | async-start | bytes 10137600 | tf_op jit(solution)/shard_map/all_gather | solution.py:212
  1468.1 246.7 %all-gather.49.cloned.1.call-start = ((), (), s32[]{:S(2)}) async-start(), calls=%async_computation.21 | async-start | bytes 5068800 | tf_op jit(solution)/shard_map/all_gather | solution.py:213
  1468.7 294.2 %all-reduce.501.cloned.1.call-start = ((), (), s32[]{:S(2)}) async-start(), calls=%async_computation.37 | async-start | bytes 851968 | tf_op jit(solution)/shard_map/psum | solution.py:419
  1731.7 1070.6 %all-reduce.499.cloned.1.call-start = ((), (), s32[]{:S(2)}) async-start(), calls=%async_computation.36 | async-start | bytes 851968 | tf_op jit(solution)/shard_map/psum | solution.py:531
  2769.0 85.7 %all-reduce.497.cloned.1.call-start = ((), (), s32[]{:S(2)}) async-start(), calls=%async_computation.35 | async-start | bytes 851968 | tf_op jit(solution)/shard_map/psum | solution.py:419
  2821.6 1150.0 %reduce-scatter.39.cloned.1.call-start = ((), (), s32[]{:S(2)}) async-start(), calls=%async_computation.25 | async-start | bytes 2304000
  2826.8 1148.5 %reduce-scatter.43.cloned.1.call-start = ((), (), s32[]{:S(2)}) async-start(), calls=%async_computation.27 | async-start | bytes 2304000
  2843.7 1135.3 %reduce-scatter.37.cloned.1.call-start = ((), (), s32[]{:S(2)}) async-start(), calls=%async_computation.24 | async-start | bytes 2304000
  3895.7 150.6 %reduce-scatter.41.cloned.1.call-start = ((), (), s32[]{:S(2)}) async-start(), calls=%async_computation.26 | async-start | bytes 2304000
  3921.3 568.8 %all-reduce.493.cloned.1.call-start = ((), (), s32[]{:S(2)}) async-start(), calls=%async_computation.33 | async-start | bytes 27934720 | tf_op jit(solution)/shard_map/psum | solution.py:581
  3959.3 690.5 %all-reduce.495.cloned.1.call-start = ((), (), s32[]{:S(2)}) async-start(), calls=%async_computation.34 | async-start | bytes 8257536 | tf_op jit(solution)/shard_map/psum | solution.py:353
  4512.9 264.6 %reduce-scatter.47.cloned.1.call-start = ((), (), s32[]{:S(2)}) async-start(), calls=%async_computation.29 | async-start | bytes 3225600
  4516.9 309.1 %reduce-scatter.45.cloned.1.call-start = ((), (), s32[]{:S(2)}) async-start(), calls=%async_computation.28 | async-start | bytes 3225600
  4521.4 419.6 %reduce-scatter.51.cloned.1.call-start = ((), (), s32[]{:S(2)}) async-start(), calls=%async_computation.31 | async-start | bytes 5068800
  4527.6 527.6 %reduce-scatter.49.cloned.1.call-start = ((), (), s32[]{:S(2)}) async-start(), calls=%async_computation.30 | async-start | bytes 5068800
  4533.8 597.0 %all-reduce.491.cloned.1.call-start = ((), (), s32[]{:S(2)}) async-start(), calls=%async_computation.32 | async-start | bytes 218112 | tf_op jit(solution)/shard_map/psum | solution.py:575
  4652.5 639.4 %reduce-scatter.35.cloned.1.call-start = ((), (), s32[]{:S(2)}) async-start(), calls=%async_computation.23 | async-start | bytes 10137600
  4710.0 742.6 %reduce-scatter.33.cloned.1.call-start = ((), (), s32[]{:S(2)}) async-start(), calls=%async_computation.22 | async-start | bytes 10137600
  (940 other events, 13427.7 us)
Sparse Core Ops, SparseCore 0:
  10.8 59.0 all-gather.28
  72.7 48.9 all-gather.26
  124.4 90.7 all-gather.30
  217.2 55.6 all-gather.32
  583.5 33.6 all-reduce.506
  620.0 133.0 all-gather.34
  756.1 75.4 all-gather.36
  834.6 56.0 all-gather.40
  893.6 91.4 all-gather.42
  988.7 31.0 all-reduce.504
  1022.0 48.8 all-gather.38
  1072.9 56.0 all-gather.44
  1465.7 35.3 all-reduce.502
  1504.0 133.0 all-gather.46
  1639.3 75.4 all-gather.48
  1731.8 31.0 all-reduce.500
  2769.1 33.1 all-reduce.498
  2821.7 32.9 all-reduce.496
  2858.8 73.0 reduce-scatter.38
  2935.9 72.4 reduce-scatter.42
  3895.8 73.2 reduce-scatter.36
  3973.2 72.9 reduce-scatter.40
  4052.9 437.1 all-reduce.492
  4513.0 136.7 all-reduce.494
  4654.1 84.5 reduce-scatter.46
  4742.0 83.8 reduce-scatter.44
  4830.2 110.8 reduce-scatter.50
  4944.9 110.2 reduce-scatter.48
  5061.0 69.7 all-reduce.490
  5134.2 157.6 reduce-scatter.34
  5295.8 156.7 reduce-scatter.32
where the time goes:
time: 5560 us; the launch traced here: 5470 us
  local copies, waits for them, and re-layouts  2310 us (42%)
  waiting for transfers between devices  1950 us (35%)
  other arithmetic  685 us (12%)
  matrix products  377 us (7%)
  blocking collectives  116 us (2%)
    pad x312, local copies, waits for them, and re-layouts, advance(): lax.associative_scan(combine_steps, (decay_step, source), axis=0)  1720 us
    unnamed x41, waiting for transfers between devices  651 us
    psum x1, waiting for transfers between devices, per_device(): lax.psum(stacked(6).astype(jnp.bfloat16), 'dp').astype(jnp.float32)  440 us
    all_gather x2, waiting for transfers between devices, fetch_layer(): lax.all_gather(gate_weight[layer_idx], 'dp', axis=0, tiled=True)  258 us
    unnamed x1732, local copies, waits for them, and re-layouts  244 us
    all_gather x2, waiting for transfers between devices, fetch_layer(): lax.all_gather(down_weight[layer_idx], 'dp', axis=1, tiled=True)  142 us
    mul x108, other arithmetic, combine_steps(): return (earlier[0] * later[0], later[0] * earlier[1] + later[1])  130 us
    add x80, other arithmetic, advance(): lax.associative_scan(combine_steps, (decay_step, source), axis=0)  114 us
  transfers between devices with their start and end apart: 31, of which 24 were waited for; matrix products, arithmetic and copies ran while one was open for 40% of the time, Pallas kernels for 0%

commit v1 on v0

v1 whole, which is shorter than its diff:
```python
import functools

import jax
import jax.numpy as jnp
from jax import lax
from jax.experimental import pallas as pl
from jax.experimental.pallas import tpu as pltpu
from jax.sharding import PartitionSpec as P

KVH = 5
HEAD = 64
GQ = 5
CONV = 4
WINDOW = 1024
EPSILON = 1e-06
GROUP = 4
LANES = 128
F32 = jnp.float32
BF16 = jnp.bfloat16
NN = (((1,), (0,)), ((), ()))
NT = (((1,), (1,)), ((), ()))
TN = (((0,), (0,)), ((), ()))


def mm(left, right, dims=NN):
    return lax.dot_general(left, right, dims, preferred_element_type=F32)


def sigmoid(v):
    return 1.0 / (1.0 + jnp.exp(-v))


def softplus(v):
    return jnp.maximum(v, 0.0) + jnp.log(1.0 + jnp.exp(-jnp.abs(v)))


def params(megabytes=56):
    return pltpu.CompilerParams(vmem_limit_bytes=megabytes * 2**20)


def cost(flops, moved):
    return pl.CostEstimate(flops=int(flops), bytes_accessed=int(moved), transcendentals=0)


def call(kernel, outs, args, flops, scratch=()):
    moved = sum(a.size * a.dtype.itemsize for a in args)
    moved += sum(o.size * o.dtype.itemsize for o in outs)
    vmem = pl.BlockSpec(memory_space=pltpu.VMEM)
    return pl.pallas_call(
        kernel,
        out_shape=outs,
        in_specs=[vmem] * len(args),
        out_specs=[vmem] * len(outs),
        scratch_shapes=list(scratch),
        compiler_params=params(),
        cost_estimate=cost(flops, moved),
    )(*args)


def out(shape, dtype):
    return jax.ShapeDtypeStruct(shape, dtype)


def widen(values, width):
    rows, have = values.shape
    if have == width:
        return values
    return jnp.concatenate([values, jnp.zeros((rows, width - have), values.dtype)], axis=1)


def shift_rows(values, amount, length):
    if amount == 0:
        return values
    rows = values.shape[0]
    place = lax.broadcasted_iota(jnp.int32, values.shape, 0) % length
    moved = pltpu.roll(values, amount % rows, 0)
    inside = place >= amount if amount > 0 else place < length + amount
    return jnp.where(inside, moved, 0.0)


def conv_pre(inner_x, taps, bias, length):
    running = bias
    for k in range(CONV):
        running = running + shift_rows(inner_x, CONV - 1 - k, length) * taps[k : k + 1]
    return running


def scores_of(queries, keys, length):
    scores = lax.dot_general(
        queries, keys, (((2,), (2,)), ((0,), (0,))), preferred_element_type=F32
    ) * HEAD ** (-0.5)
    shape = scores.shape
    query_pos = lax.broadcasted_iota(jnp.int32, shape, 1)
    key_pos = lax.broadcasted_iota(jnp.int32, shape, 2)
    allowed = (key_pos <= query_pos) & (key_pos > query_pos - WINDOW)
    scores = jnp.where(allowed, scores, -1e30)
    weights = jnp.exp(scores - jnp.max(scores, axis=-1, keepdims=True))
    return weights / jnp.sum(weights, axis=-1, keepdims=True)


class Mix:
    def __init__(self, chan):
        self.q = 0
        self.kv = 2 * HEAD
        self.o = 4 * HEAD
        self.x = 6 * HEAD
        self.z = self.x + chan
        self.s = self.z + chan
        self.end = self.s + chan


def mix_forward_kernel(cols, chan, wide, length, n, w, taps, bias, scan_w, xi, z, conv, qkv, heads, proj, attn):
    normed = n[...]
    both = mm(normed, w[:, : cols.o]).astype(BF16)
    qkv[...] = both
    inner = mm(normed, w[:, cols.x : cols.s])
    inner_x = widen(inner[:, :chan], wide)
    xi[...] = inner_x
    z[...] = widen(inner[:, chan:], wide)
    running = conv_pre(inner_x, taps[...], bias[...], length)
    conv_low = (running * sigmoid(running)).astype(BF16)
    conv[...] = conv_low
    proj[...] = mm(scan_w[...], conv_low, NT).astype(BF16)
    seqs = normed.shape[0] // length
    keys = both[:, cols.kv : cols.kv + HEAD].reshape(seqs, length, HEAD)
    values = both[:, cols.kv + HEAD : cols.o].reshape(seqs, length, HEAD)
    outs = []
    for h in range(2):
        queries = both[:, h * HEAD : (h + 1) * HEAD].reshape(seqs, length, HEAD)
        probs = scores_of(queries, keys, length).astype(BF16)
        mixed = lax.dot_general(
            probs, values, (((2,), (1,)), ((0,), (0,))), preferred_element_type=F32
        )
        outs.append(mixed.reshape(seqs * length, HEAD))
    heads_out = jnp.concatenate(outs, axis=1).astype(BF16)
    heads[...] = heads_out
    attn[...] = mm(heads_out, w[:, cols.o : cols.x], NT).astype(BF16)


def spread(state, wide):
    row = lax.broadcasted_iota(jnp.int32, (state, wide), 0)
    col = lax.broadcasted_iota(jnp.int32, (state, wide), 1) // LANES
    return (row == col).astype(BF16)


def lane(n):
    return slice(n * LANES, (n + 1) * LANES)


def tiles_in(ref, values):
    for n in range(ref.shape[0]):
        ref[n] = values[:, lane(n)]


def tiles_out(ref):
    return jnp.concatenate([ref[n] for n in range(ref.shape[0])], axis=1)


def scan_setup(rank, state, seqs, proj, conv, step_w, step_b, dlog, dt_s, dtx_s, drive_s, read_s, rate_s):
    pre = mm(proj[:rank], step_w[...], TN) + step_b[...]
    dt = softplus(pre)
    tiles_in(dt_s, dt)
    tiles_in(dtx_s, dt * conv)
    table = spread(state, state * LANES)
    tiles_in(drive_s, mm(proj[rank : rank + state], table, TN))
    tiles_in(read_s, mm(proj[rank + state :], table, TN))
    rates = -jnp.exp(dlog[...])
    for n in range(state):
        rate_s[n] = jnp.broadcast_to(rates[n : n + 1], (seqs, rates.shape[1]))
    return pre


def scan_forward_loop(state, seqs, length, tile, dt_s, dtx_s, drive_s, read_s, rate_s, y_s, keep_s):
    def step(t, held):
        rows = pl.ds(t, seqs, stride=length)
        dt = dt_s[tile, rows]
        dtx = dtx_s[tile, rows]
        total = jnp.zeros_like(dt)
        fresh = []
        for n in range(state):
            now = jnp.exp(dt * rate_s[n, :, lane(tile)]) * held[n] + dtx * drive_s[n, rows]
            total = total + now * read_s[n, rows]
            if keep_s is not None:
                keep_s[t, n] = now
            fresh.append(now)
        y_s[tile, rows] = total
        return tuple(fresh)

    zero = jnp.zeros((seqs, LANES), F32)
    lax.fori_loop(0, length, step, (zero,) * state)


def scan_forward_kernel(cols, chan, wide, rank, state, seqs, length, proj, conv, z, step_w, step_b, dlog, skip, w, gated, ssm, dt_s, dtx_s, drive_s, read_s, rate_s, y_s):
    conv32 = conv[...].astype(F32)
    scan_setup(rank, state, seqs, proj, conv32, step_w, step_b, dlog, dt_s, dtx_s, drive_s, read_s, rate_s)
    for tile in range(wide // LANES):
        scan_forward_loop(state, seqs, length, tile, dt_s, dtx_s, drive_s, read_s, rate_s, y_s, None)
    gate = z[...]
    low = ((tiles_out(y_s) + skip[...] * conv32) * (gate * sigmoid(gate))).astype(BF16)
    gated[...] = low
    ssm[...] = mm(low[:, :chan], w[:, cols.s :], NT).astype(BF16)


def split_sum(table, values):
    high = values.astype(BF16)
    rest = (values - high.astype(F32)).astype(BF16)
    return mm(table, high, NT) + mm(table, rest, NT)


def scan_backward_kernel(cols, chan, wide, rank, state, seqs, length, grad, proj, conv, z, step_w, step_b, dlog, skip, w, d_proj, d_conv, d_z, small, d_step_w, dt_s, dtx_s, drive_s, read_s, rate_s, y_s, keep_s, ds_s, ddt_s, pd_s, pr_s, dr_s):
    conv32 = conv[...].astype(F32)
    pre = scan_setup(rank, state, seqs, proj, conv32, step_w, step_b, dlog, dt_s, dtx_s, drive_s, read_s, rate_s)
    d_gated = widen(mm(grad[...], w[:, cols.s :]), wide)
    gate = z[...]
    sig = sigmoid(gate)
    d_scanned = d_gated * (gate * sig)
    tiles_in(ds_s, d_scanned)
    d_rates = []
    for tile in range(wide // LANES):
        scan_forward_loop(state, seqs, length, tile, dt_s, dtx_s, drive_s, read_s, rate_s, y_s, keep_s)
        for n in range(state):
            dr_s[n] = jnp.zeros((seqs, LANES), F32)

        def step(back, carry):
            t = length - 1 - back
            rows = pl.ds(t, seqs, stride=length)
            dt = dt_s[tile, rows]
            dtx = dtx_s[tile, rows]
            ds = ds_s[tile, rows]
            earlier = jnp.maximum(t - 1, 0)
            alive = jnp.where(t > 0, 1.0, 0.0)
            d_src = jnp.zeros_like(dt)
            d_dt = jnp.zeros_like(dt)
            fresh = []
            for n in range(state):
                rate = rate_s[n, :, lane(tile)]
                lam = carry[n] + read_s[n, rows] * ds
                prod_read = keep_s[t, n] * ds
                prod_drive = lam * dtx
                if tile == 0:
                    pr_s[n, rows] = prod_read
                    pd_s[n, rows] = prod_drive
                else:
                    pr_s[n, rows] = pr_s[n, rows] + prod_read
                    pd_s[n, rows] = pd_s[n, rows] + prod_drive
                d_src = d_src + lam * drive_s[n, rows]
                passed = jnp.exp(dt * rate) * lam
                d_log = passed * (keep_s[earlier, n] * alive)
                d_dt = d_dt + d_log * rate
                dr_s[n] = dr_s[n] + d_log * dt
                fresh.append(passed)
            ddt_s[tile, rows] = d_dt
            dtx_s[tile, rows] = d_src
            return tuple(fresh)

        zero = jnp.zeros((seqs, LANES), F32)
        lax.fori_loop(0, length, step, (zero,) * state)
        d_rates.append(
            jnp.concatenate(
                [jnp.sum(dr_s[n], axis=0, keepdims=True) for n in range(state)], axis=0
            )
        )
    d_src = tiles_out(dtx_s)
    dt = tiles_out(dt_s)
    d_dt = tiles_out(ddt_s) + d_src * conv32
    d_conv[...] = skip[...] * d_scanned + d_src * dt
    scanned = tiles_out(y_s) + skip[...] * conv32
    d_z[...] = (d_gated * scanned * (sig * (1.0 + gate * (1.0 - sig)))).astype(BF16)
    d_pre = d_dt * sigmoid(pre)
    rates = -jnp.exp(dlog[...])
    d_log = jnp.concatenate(d_rates, axis=1) * rates
    small[0:1] = jnp.sum(d_pre, axis=0, keepdims=True)
    small[1:2] = jnp.sum(d_scanned * conv32, axis=0, keepdims=True)
    small[2:8] = jnp.zeros((6, wide), F32)
    small[8:] = d_log
    low = d_pre.astype(BF16)
    d_step_w[...] = mm(proj[:rank], low)
    table = spread(state, state * LANES)
    d_proj[:rank] = mm(step_w[...], low, NT).astype(BF16)
    d_proj[rank : rank + state] = split_sum(table, tiles_out(pd_s)).astype(BF16)
    d_proj[rank + state :] = split_sum(table, tiles_out(pr_s)).astype(BF16)


def attend_backward_kernel(cols, length, grad, w, qkv, d_qkv):
    d_heads = mm(grad[...], w[:, cols.o : cols.x]).astype(BF16)
    both = qkv[...]
    seqs = both.shape[0] // length
    keys = both[:, cols.kv : cols.kv + HEAD].reshape(seqs, length, HEAD)
    values = both[:, cols.kv + HEAD : cols.o].reshape(seqs, length, HEAD)
    parts = []
    d_keys = 0.0
    d_values = 0.0
    for h in range(2):
        queries = both[:, h * HEAD : (h + 1) * HEAD].reshape(seqs, length, HEAD)
        d_out = d_heads[:, h * HEAD : (h + 1) * HEAD].reshape(seqs, length, HEAD)
        probs = scores_of(queries, keys, length)
        d_probs = lax.dot_general(
            d_out, values, (((2,), (2,)), ((0,), (0,))), preferred_element_type=F32
        )
        d_scores = (
            probs
            * (d_probs - jnp.sum(d_probs * probs, axis=-1, keepdims=True))
            * HEAD ** (-0.5)
        ).astype(BF16)
        d_query = lax.dot_general(
            d_scores, keys, (((2,), (1,)), ((0,), (0,))), preferred_element_type=F32
        )
        parts.append(d_query.reshape(seqs * length, HEAD))
        d_keys = d_keys + lax.dot_general(
            d_scores, queries, (((1,), (1,)), ((0,), (0,))), preferred_element_type=F32
        )
        d_values = d_values + lax.dot_general(
            probs.astype(BF16), d_out, (((1,), (1,)), ((0,), (0,))), preferred_element_type=F32
        )
    parts.append(d_keys.reshape(seqs * length, HEAD))
    parts.append(d_values.reshape(seqs * length, HEAD))
    d_qkv[...] = jnp.concatenate(parts, axis=1).astype(BF16)


def mix_backward_kernel(cols, chan, length, proj, conv, xi, d_conv, d_z, d_qkv, w, taps, bias, scan_w, d_x, part, d_scan_w, small):
    d_out = d_conv[...] + mm(proj[...], scan_w[...], TN)
    inner_x = xi[...]
    running = conv_pre(inner_x, taps[...], bias[...], length)
    sig = sigmoid(running)
    d_run = d_out * (sig * (1.0 + running * (1.0 - sig)))
    d_in = 0.0
    for k in range(CONV):
        back = CONV - 1 - k
        d_in = d_in + shift_rows(d_run, -back, length) * taps[k : k + 1]
        small[k : k + 1] = jnp.sum(d_run * shift_rows(inner_x, back, length), axis=0, keepdims=True)
    small[CONV : CONV + 1] = jnp.sum(d_run, axis=0, keepdims=True)
    small[CONV + 1 :] = jnp.zeros((8 - CONV - 1, inner_x.shape[1]), F32)
    low = d_in.astype(BF16)
    d_x[...] = low
    inner = jnp.concatenate([low[:, :chan], d_z[:, :chan]], axis=1)
    part[...] = (
        mm(inner, w[:, cols.x : cols.s], NT) + mm(d_qkv[...], w[:, : cols.o], NT)
    ).astype(BF16)
    d_scan_w[...] = mm(proj[...], conv[...])


def mix_weights_kernel(cols, chan, n, d_attn, d_ssm, d_qkv, heads, d_x, d_z, gated, d_w):
    normed = n[...]
    d_w[:, : cols.o] = mm(normed, d_qkv[...], TN).astype(BF16)
    d_w[:, cols.o : cols.x] = mm(d_attn[...], heads[...], TN).astype(BF16)
    d_w[:, cols.x : cols.z] = mm(normed, d_x[:, :chan], TN).astype(BF16)
    d_w[:, cols.z : cols.s] = mm(normed, d_z[:, :chan], TN).astype(BF16)
    d_w[:, cols.s :] = mm(d_ssm[...], gated[:, :chan], TN).astype(BF16)


def ffn_forward_kernel(units, f, w, hidden, part):
    both = mm(f[...], w[:, : 2 * units])
    hidden[...] = both
    gate = both[:, :units]
    activ = (gate * sigmoid(gate) * both[:, units:]).astype(BF16)
    part[...] = mm(activ, w[:, 2 * units :], NT).astype(BF16)


def ffn_backward_kernel(units, d_out, hidden, w, d_hidden, activ, part):
    d_activ = mm(d_out[...], w[:, 2 * units :])
    gate = hidden[:, :units]
    up = hidden[:, units:]
    sig = sigmoid(gate)
    swish = gate * sig
    activ[...] = (swish * up).astype(BF16)
    low = jnp.concatenate(
        [d_activ * up * (sig * (1.0 + gate * (1.0 - sig))), d_activ * swish], axis=1
    ).astype(BF16)
    d_hidden[...] = low
    part[...] = mm(low, w[:, : 2 * units], NT).astype(BF16)


def ffn_weights_kernel(units, f, d_out, d_hidden, activ, d_w):
    d_w[:, : 2 * units] = mm(f[...], d_hidden[...], TN).astype(BF16)
    d_w[:, 2 * units :] = mm(d_out[...], activ[...], TN).astype(BF16)


def rms_scale(values, gain_vec):
    return (
        values * lax.rsqrt(jnp.mean(values * values, axis=-1, keepdims=True) + EPSILON) * gain_vec
    )


def mix_branches(resid_in, attn_out, ssm_out, gain_attn, gain_ssm, gain_ffn):
    residual = resid_in + 0.5 * (rms_scale(attn_out, gain_attn) + rms_scale(ssm_out, gain_ssm))
    return (residual, rms_scale(residual, gain_ffn))


def per_device(
    dp_size,
    tensor_size,
    hidden_in,
    out_grad,
    lengths,
    norm_gains,
    q_weight,
    kv_weight,
    o_weight,
    in_weight,
    conv_weight,
    conv_bias,
    step_bias,
    decay_log,
    skip_gain,
    scan_weight,
    step_weight,
    ssm_weight,
    gate_weight,
    down_weight,
):
    layers = q_weight.shape[0]
    batches, _, length, width = hidden_in.shape
    fast = dp_size // GROUP
    share = width // dp_size
    chan = in_weight.shape[3] // GROUP
    wide = -(-chan // LANES) * LANES
    units = gate_weight.shape[3] // GROUP
    rank_true = step_weight.shape[1]
    state = decay_log.shape[2]
    rank = -(-rank_true // 16) * 16
    proj_rows = rank + 2 * state
    cols = Mix(chan)
    ffn_cols = 3 * units
    dp_idx = lax.axis_index("dp")
    slow_idx = dp_idx // fast
    fast_idx = dp_idx % fast
    tensor_idx = lax.axis_index("tensor")
    rows_here = batches * length // tensor_size
    seqs = GROUP * batches
    tokens = seqs * length
    half = tensor_size // 2

    def slow_perm(by):
        return [
            (s * fast + f, ((s + by) % GROUP) * fast + f) for s in range(GROUP) for f in range(fast)
        ]

    def fast_perm(by):
        return [
            (s * fast + f, s * fast + (f + by) % fast) for s in range(GROUP) for f in range(fast)
        ]

    core_perm = [(t, t ^ 1) for t in range(tensor_size)]
    chip_perm = [(t, t ^ 2) for t in range(tensor_size)]
    core_idx = tensor_idx % 2
    chip_idx = tensor_idx // 2

    def slow(values, by):
        return lax.ppermute(values, "dp", slow_perm(by)) if by % GROUP else values

    def other_fast(values, by):
        return lax.ppermute(values, "dp", fast_perm(by)) if by % fast else values

    def add_low(*terms):
        total = terms[0].astype(F32)
        for term in terms[1:]:
            total = total + term.astype(F32)
        return total.astype(BF16)

    def gather_tokens(own):
        parts = jnp.stack([slow(own, by) for by in range(GROUP)])
        moved = lax.ppermute(parts, "tensor", chip_perm)
        parts = jnp.where(chip_idx == 0, jnp.stack([parts, moved], 1), jnp.stack([moved, parts], 1))
        moved = lax.ppermute(parts, "tensor", core_perm)
        parts = jnp.where(core_idx == 0, jnp.stack([parts, moved], 2), jnp.stack([moved, parts], 2))
        return parts.reshape(tokens, own.shape[1])

    def scatter_tokens(full):
        parts = full.reshape(GROUP, half, 2, rows_here, full.shape[1])
        mine = lax.dynamic_index_in_dim(parts, core_idx, 2, False)
        theirs = lax.dynamic_index_in_dim(parts, 1 - core_idx, 2, False)
        parts = add_low(mine, lax.ppermute(theirs, "tensor", core_perm))
        mine = lax.dynamic_index_in_dim(parts, chip_idx, 1, False)
        theirs = lax.dynamic_index_in_dim(parts, 1 - chip_idx, 1, False)
        parts = add_low(mine, lax.ppermute(theirs, "tensor", chip_perm))
        total = parts[0].astype(F32)
        for by in range(1, GROUP):
            total = total + slow(parts[by], GROUP - by).astype(F32)
        return total

    def sum_group(values):
        values = add_low(values, lax.ppermute(values, "tensor", core_perm))
        values = add_low(values, lax.ppermute(values, "tensor", chip_perm))
        chunk = tokens // GROUP
        parts = [values[:, k * chunk : (k + 1) * chunk] for k in range(GROUP)]
        total = add_low(parts[0], *[slow(parts[by], GROUP - by) for by in range(1, GROUP)])
        return jnp.concatenate([slow(total, by) for by in range(GROUP)], axis=1)

    def fetch(packed):
        columns = packed.shape[2]
        place = lax.dynamic_index_in_dim
        full = jnp.zeros((GROUP, fast, share, columns), BF16)
        for by in range(GROUP):
            got = slow(place(packed, (slow_idx + by) % GROUP, 0, False), by)
            source = (slow_idx - by) % GROUP
            for turn in range(fast):
                piece = other_fast(got, turn)
                full = lax.dynamic_update_slice(
                    full, piece[None, None], (source, (fast_idx - turn) % fast, 0, 0)
                )
        return full.reshape(width, columns)

    def settle(grad):
        columns = grad.shape[1]
        grad = grad.reshape(GROUP, fast, share, columns)
        pieces = []
        for by in range(GROUP):
            target = lax.dynamic_index_in_dim(grad, (slow_idx + by) % GROUP, 0, False)
            terms = [
                other_fast(
                    lax.dynamic_index_in_dim(target, (fast_idx + turn) % fast, 0, False), turn
                )
                for turn in range(fast)
            ]
            pieces.append(slow(add_low(*terms), by))
        stacked = jnp.stack(pieces)
        return [
            lax.dynamic_index_in_dim(stacked, (slow_idx - source) % GROUP, 0, False)
            for source in range(GROUP)
        ]

    def pack_mix(layer):
        padded_q = jnp.pad(q_weight[layer], ((0, 0), (0, 2 * HEAD)))
        padded_o = jnp.pad(o_weight[layer], ((0, 2 * HEAD), (0, 0)))
        ssm_t = ssm_weight[layer].T
        pieces = []
        for s in range(GROUP):
            unit = s * tensor_size + tensor_idx
            group = unit // 3
            sub = unit % 3
            start = group * GQ * HEAD + sub * 2 * HEAD
            valid = jnp.where(group >= KVH, 0, jnp.where(sub == 2, HEAD, 2 * HEAD))
            keep = jnp.arange(2 * HEAD) < valid
            query = lax.dynamic_slice_in_dim(padded_q, start, 2 * HEAD, 1)
            query = jnp.where(keep[None], query, 0)
            output = lax.dynamic_slice_in_dim(padded_o, start, 2 * HEAD, 0)
            output = jnp.where(keep[:, None], output, 0).T
            keyval = lax.dynamic_slice_in_dim(
                kv_weight[layer], jnp.minimum(group, KVH - 1) * HEAD, HEAD, 2
            )
            inner = in_weight[layer, :, :, s * chan : (s + 1) * chan]
            pieces.append(
                jnp.concatenate(
                    [
                        query,
                        keyval[:, 0],
                        keyval[:, 1],
                        output,
                        inner[:, 0],
                        inner[:, 1],
                        ssm_t[:, s * chan : (s + 1) * chan],
                    ],
                    axis=1,
                )
            )
        return jnp.stack(pieces)

    def pack_ffn(layer):
        down_t = down_weight[layer].T
        return jnp.stack(
            [
                jnp.concatenate(
                    [
                        gate_weight[layer, :, 0, s * units : (s + 1) * units],
                        gate_weight[layer, :, 1, s * units : (s + 1) * units],
                        down_t[:, s * units : (s + 1) * units],
                    ],
                    axis=1,
                )
                for s in range(GROUP)
            ]
        )

    def after(values, *earlier):
        return lax.optimization_barrier((values,) + earlier)[0]

    pad_chan = ((0, 0), (0, wide - chan))

    def channels(values, axis):
        return lax.dynamic_slice_in_dim(values, slow_idx * chan, chan, axis)

    small_weights = []
    for layer in range(layers):
        scan_t = channels(scan_weight[layer], 0).T
        scan_t = jnp.concatenate(
            [
                scan_t[:rank_true],
                jnp.zeros((rank - rank_true, chan), BF16),
                scan_t[rank_true:],
            ],
            axis=0,
        )
        step_mat = jnp.pad(channels(step_weight[layer], 1), ((0, rank - rank_true), (0, 0)))
        small_weights.append(
            (
                jnp.pad(channels(conv_weight[layer], 1), pad_chan),
                jnp.pad(channels(conv_bias[layer][None], 1), pad_chan),
                jnp.pad(scan_t, pad_chan),
                jnp.pad(step_mat, pad_chan),
                jnp.pad(channels(step_bias[layer][None], 1), pad_chan),
                jnp.pad(channels(decay_log[layer], 0).T, pad_chan),
                jnp.pad(channels(skip_gain[layer][None], 1), pad_chan),
            )
        )

    fetched = []
    for layer in range(layers):
        fetched.append((fetch(pack_mix(layer)), fetch(pack_ffn(layer))))

    bf_rows = lambda columns: out((tokens, columns), BF16)
    f_rows = lambda columns: out((tokens, columns), F32)
    tiled = pltpu.VMEM((wide // LANES, tokens, LANES), F32)
    state_tiled = pltpu.VMEM((state, tokens, LANES), F32)
    scan_scratch = [
        tiled,
        tiled,
        state_tiled,
        state_tiled,
        pltpu.VMEM((state, seqs, wide), F32),
        tiled,
    ]

    def own_rows(values):
        flat = values.reshape(batches * length, width)
        return lax.dynamic_slice_in_dim(flat, tensor_idx * rows_here, rows_here, 0)

    running = own_rows(hidden_in).astype(F32)
    kept = []
    for layer in range(layers):
        mix_w, ffn_w = fetched[layer]
        gains = norm_gains[layer]
        taps, bias, scan_w, step_w, step_b, dlog, skip = small_weights[layer]
        normed, pull_input = jax.vjp(rms_scale, running, gains[0])
        n = gather_tokens(normed.astype(BF16))
        xi, z, conv, qkv, heads, proj_part, attn_part = call(
            functools.partial(mix_forward_kernel, cols, chan, wide, length),
            [
                f_rows(wide),
                f_rows(wide),
                bf_rows(wide),
                bf_rows(cols.o),
                bf_rows(2 * HEAD),
                out((proj_rows, tokens), BF16),
                bf_rows(width),
            ],
            [n, mix_w, taps, bias, scan_w],
            2 * tokens * width * (cols.s),
        )
        proj = sum_group(proj_part)
        attn_out = scatter_tokens(attn_part)
        gated, ssm_part = call(
            functools.partial(
                scan_forward_kernel, cols, chan, wide, rank, state, seqs, length
            ),
            [bf_rows(wide), bf_rows(width)],
            [proj, conv, z, step_w, step_b, dlog, skip, mix_w],
            2 * tokens * width * chan + 100 * tokens * wide * state,
            scan_scratch,
        )
        ssm_out = scatter_tokens(ssm_part)
        (residual, ffn_in), pull_mix = jax.vjp(
            mix_branches, running, attn_out, ssm_out, gains[1], gains[2], gains[3]
        )
        f = gather_tokens(ffn_in.astype(BF16))
        hidden, ffn_part = call(
            functools.partial(ffn_forward_kernel, units),
            [f_rows(2 * units), bf_rows(width)],
            [f, ffn_w],
            2 * tokens * width * ffn_cols,
        )
        running = residual + scatter_tokens(ffn_part)
        kept.append((n, pull_input, xi, z, conv, qkv, heads, proj, gated, pull_mix, f, hidden))

    place = tensor_idx * rows_here + jnp.arange(rows_here)
    mask = (place % length < lengths[place // length, 0]).astype(F32)[:, None]
    output = (running * mask).astype(BF16)
    grad_run = own_rows(out_grad).astype(F32) * mask

    def all_rows(own):
        moved = lax.all_gather(own, "tensor", axis=0, tiled=True)
        return moved.reshape(batches, 1, length, width)

    output = all_rows(output)

    big_grads = [None] * layers
    small_grads = [None] * layers
    gain_grads = [None] * layers
    for layer in reversed(range(layers)):
        mix_w, ffn_w = fetched[layer]
        taps, bias, scan_w, step_w, step_b, dlog, skip = small_weights[layer]
        n, pull_input, xi, z, conv, qkv, heads, proj, gated, pull_mix, f, hidden = kept[layer]
        d_out = gather_tokens(grad_run.astype(BF16))
        d_hidden, activ, part = call(
            functools.partial(ffn_backward_kernel, units),
            [bf_rows(2 * units), bf_rows(units), bf_rows(width)],
            [d_out, hidden, ffn_w],
            2 * tokens * width * ffn_cols,
        )
        d_ffn_in = scatter_tokens(part)
        (d_ffn_w,) = call(
            functools.partial(ffn_weights_kernel, units),
            [out((width, ffn_cols), BF16)],
            [f, d_out, d_hidden, activ],
            2 * tokens * width * ffn_cols,
        )
        ffn_pieces = settle(d_ffn_w)
        grad_resid, d_attn, d_ssm, d_gain_attn, d_gain_ssm, d_gain_ffn = pull_mix(
            (grad_run, d_ffn_in)
        )
        d_attn = gather_tokens(d_attn.astype(BF16))
        d_ssm = gather_tokens(d_ssm.astype(BF16))
        d_proj, d_conv, d_z, small_scan, d_step_w = call(
            functools.partial(
                scan_backward_kernel, cols, chan, wide, rank, state, seqs, length
            ),
            [
                out((proj_rows, tokens), BF16),
                f_rows(wide),
                bf_rows(wide),
                out((8 + state, wide), F32),
                out((rank, wide), F32),
            ],
            [d_ssm, proj, conv, z, step_w, step_b, dlog, skip, mix_w],
            2 * tokens * width * chan + 400 * tokens * wide * state,
            scan_scratch
            + [
                pltpu.VMEM((length, state, seqs, LANES), F32),
                tiled,
                tiled,
                state_tiled,
                state_tiled,
                pltpu.VMEM((state, seqs, LANES), F32),
            ],
        )
        d_proj = sum_group(d_proj)
        (d_qkv,) = call(
            functools.partial(attend_backward_kernel, cols, length),
            [bf_rows(cols.o)],
            [d_attn, mix_w, qkv],
            2 * tokens * width * 2 * HEAD,
        )
        d_x, part, d_scan_w, small_conv = call(
            functools.partial(mix_backward_kernel, cols, chan, length),
            [
                bf_rows(wide),
                bf_rows(width),
                out((proj_rows, wide), F32),
                out((8, wide), F32),
            ],
            [d_proj, conv, xi, d_conv, d_z, d_qkv, mix_w, taps, bias, scan_w],
            2 * tokens * width * (cols.s),
        )
        d_normed = scatter_tokens(part)
        (d_mix_w,) = call(
            functools.partial(mix_weights_kernel, cols, chan),
            [out((width, cols.end), BF16)],
            [n, d_attn, d_ssm, d_qkv, heads, d_x, d_z, gated],
            2 * tokens * width * cols.end,
        )
        mix_pieces = settle(d_mix_w)
        grad_lower, d_gain_input = pull_input(d_normed)
        grad_run = grad_resid + grad_lower
        big_grads[layer] = (mix_pieces, ffn_pieces)
        small_grads[layer] = jnp.concatenate([small_scan, small_conv, d_step_w, d_scan_w], axis=0)
        gain_grads[layer] = jnp.stack([d_gain_input, d_gain_attn, d_gain_ssm, d_gain_ffn])

    input_grad = all_rows(grad_run.astype(BF16)).astype(F32)
    grad_gains = lax.psum(jnp.stack(gain_grads).astype(BF16), ("dp", "tensor")).astype(F32)

    small = jnp.stack(small_grads)[:, :, :chan].astype(BF16)
    small = add_low(*[other_fast(small, turn) for turn in range(fast)])
    turned = jnp.stack([slow(small, by) for by in range(GROUP)])
    small = jnp.concatenate(
        [
            lax.dynamic_index_in_dim(turned, (slow_idx - source) % GROUP, 0, False)
            for source in range(GROUP)
        ],
        axis=2,
    ).astype(F32)
    base = 8 + state
    grad_step_bias = small[:, 0]
    grad_skip = small[:, 1]
    grad_decay = small[:, 8:base].transpose(0, 2, 1)
    grad_conv_weight = small[:, base : base + CONV]
    grad_conv_bias = small[:, base + CONV]
    base = base + 8
    grad_step_weight = small[:, base : base + rank_true]
    base = base + rank
    scan_rows = jnp.concatenate(
        [small[:, base : base + rank_true], small[:, base + rank :]], axis=1
    )
    grad_scan = scan_rows.transpose(0, 2, 1)

    def joined(pieces, start, stop):
        return jnp.concatenate([p[:, start:stop] for p in pieces], axis=1).astype(F32)

    def by_unit(pieces, start, stop):
        mine = jnp.stack([p[:, start:stop] for p in pieces])
        every = lax.all_gather(mine, "tensor", axis=1)
        return every.reshape((GROUP * tensor_size,) + mine.shape[1:])

    grads = {name: [] for name in ("q", "kv", "o", "in", "ssm", "gate", "down")}
    for layer in range(layers):
        mix_pieces, ffn_pieces = big_grads[layer]
        every = by_unit(mix_pieces, 0, cols.x)

        def heads_of(start):
            parts = []
            for group in range(KVH):
                parts.append(every[3 * group, :, start : start + 2 * HEAD])
                parts.append(every[3 * group + 1, :, start : start + 2 * HEAD])
                parts.append(every[3 * group + 2, :, start : start + HEAD])
            return jnp.concatenate(parts, axis=1).astype(F32)

        def group_sum(start):
            parts = [
                sum(every[3 * group + i, :, start : start + HEAD].astype(F32) for i in range(3))
                for group in range(KVH)
            ]
            return jnp.concatenate(parts, axis=1)

        grads["q"].append(heads_of(cols.q))
        grads["kv"].append(jnp.stack([group_sum(cols.kv), group_sum(cols.kv + HEAD)], axis=1))
        grads["o"].append(heads_of(cols.o).T)
        grads["in"].append(
            jnp.stack(
                [joined(mix_pieces, cols.x, cols.z), joined(mix_pieces, cols.z, cols.s)], axis=1
            )
        )
        grads["ssm"].append(joined(mix_pieces, cols.s, cols.end).T)
        grads["gate"].append(
            jnp.stack(
                [joined(ffn_pieces, 0, units), joined(ffn_pieces, units, 2 * units)], axis=1
            )
        )
        grads["down"].append(joined(ffn_pieces, 2 * units, 3 * units).T)
    grads = {name: jnp.stack(parts) for name, parts in grads.items()}
    return (
        output,
        input_grad,
        grad_gains,
        grads["q"],
        grads["kv"],
        grads["o"],
        grads["in"],
        grad_conv_weight,
        grad_conv_bias,
        grad_step_bias,
        grad_decay,
        grad_skip,
        grad_scan,
        grad_step_weight,
        grads["ssm"],
        grads["gate"],
        grads["down"],
    )


def solution(mesh):
    return jax.shard_map(
        functools.partial(per_device, mesh.shape["dp"], mesh.shape["tensor"]),
        mesh=mesh,
        in_specs=(
            P(None, "dp", None, None),
            P(None, "dp", None, None),
            P(None, "dp"),
            P(),
            P(None, "dp", None),
            P(None, "dp", None, None),
            P(None, None, "dp"),
            P(None, "dp", None, "tensor"),
            P(None, None, "tensor"),
            P(None, "tensor"),
            P(None, "tensor"),
            P(None, "tensor", None),
            P(None, "tensor"),
            P(None, "tensor", None),
            P(None, None, "tensor"),
            P(None, "tensor", "dp"),
            P(None, "dp", None, "tensor"),
            P(None, "tensor", "dp"),
        ),
        out_specs=(
            P(None, "dp", None, None),
            P(None, "dp", None, None),
            P(),
            P(None, "dp", None),
            P(None, "dp", None, None),
            P(None, None, "dp"),
            P(None, "dp", None, "tensor"),
            P(None, None, "tensor"),
            P(None, "tensor"),
            P(None, "tensor"),
            P(None, "tensor", None),
            P(None, "tensor"),
            P(None, "tensor", None),
            P(None, None, "tensor"),
            P(None, "tensor", "dp"),
            P(None, "dp", None, "tensor"),
            P(None, "tensor", "dp"),
        ),
        check_vma=False,
    )
```

time: 5560 us -> 1500 us (0.27); the launches traced: 5470 us -> 1490 us
  local copies, waits for them, and re-layouts: 2310 us -> 196 us
  waiting for transfers between devices: 1950 us -> 537 us
  other arithmetic: 685 us -> 91.1 us
  matrix products: 377 us -> 0 us
  starting transfers between devices: 2.67 us -> 301 us
  Pallas kernels: 0 us -> 292 us
  blocking collectives: 116 us -> 53.6 us
    pad x312 -> x14, local copies, waits for them, and re-layouts: 1720 us -> 8.37 us  [the longest x2 1.28 us: per_device(): jnp.pad(scan_t, pad_chan)]
    psum x9 -> x0, waiting for transfers between devices: 724 us -> none  [the longest x1 440 us: per_device(): lax.psum(stacked(6).astype(jnp.bfloat16), 'dp').astype(jnp.float32)]
    unnamed x41 -> x2, waiting for transfers between devices: 651 us -> 0.03 us
    all_gather x12 -> x2, waiting for transfers between devices: 577 us -> 0.01 us  [by_unit(): every = lax.all_gather(mine, 'tensor', axis=1)]
    ppermute x0 -> x192, waiting for transfers between devices: none -> 537 us  [the longest x111 257 us: slow(): return lax.ppermute(values, 'dp', slow_perm(by)) if by % GROUP else values]
    dot_general x200 -> x0, matrix products: 377 us -> none  [the longest x4 35.7 us: per_device(): jnp.einsum('sd,skf->dkf', backward_ffn_b16, gate_b16, preferred_element_t...]
    ppermute x0 -> x192, starting transfers between devices: none -> 301 us  [the longest x111 232 us: slow(): return lax.ppermute(values, 'dp', slow_perm(by)) if by % GROUP else values]
    pallas_call x0 -> x18, Pallas kernels: none -> 292 us  [call(): pl.pallas_call(kernel, out_shape=outs, in_specs=[vmem] * len(args), out_s...]
  transfers between devices with their start and end apart: 31 -> 194, of which waited for: 24 -> 87; matrix products, arithmetic and copies ran while one was open for 40% -> 16% of each run, Pallas kernels for 0% -> 18%
where the time goes in v1:
time: 1500 us; the launch traced here: 1490 us
  waiting for transfers between devices  537 us (36%)
  starting transfers between devices  301 us (20%)
  Pallas kernels  292 us (19%)
  local copies, waits for them, and re-layouts  196 us (13%)
  other arithmetic  91.1 us (6%)
  blocking collectives  53.6 us (4%)
  between operations  18.9 us (1%)
    pallas_call x18, Pallas kernels, call(): pl.pallas_call(kernel, out_shape=outs, in_specs=[vmem] * len(args), out_s...  292 us
    ppermute x111, waiting for transfers between devices, slow(): return lax.ppermute(values, 'dp', slow_perm(by)) if by % GROUP else values  257 us
    ppermute x111, starting transfers between devices, slow(): return lax.ppermute(values, 'dp', slow_perm(by)) if by % GROUP else values  232 us
    ppermute x33, waiting for transfers between devices, other_fast(): return lax.ppermute(values, 'dp', fast_perm(by)) if by % fast else values  161 us
    ppermute x10, waiting for transfers between devices, scatter_tokens(): parts = add_low(mine, lax.ppermute(theirs, 'tensor', chip_perm))  55.2 us
    ppermute x10, waiting for transfers between devices, gather_tokens(): moved = lax.ppermute(parts, 'tensor', chip_perm)  45.7 us
    psum x1, blocking collectives, per_device(): lax.psum(jnp.stack(gain_grads).astype(BF16), ('dp', 'tensor')).astype(F32)  38.3 us
    ppermute x33, starting transfers between devices, other_fast(): return lax.ppermute(values, 'dp', fast_perm(by)) if by % fast else values  33.4 us
  transfers between devices with their start and end apart: 194, of which 87 were waited for; matrix products, arithmetic and copies ran while one was open for 16% of the time, Pallas kernels for 18%

profile of v1, /device:TPU:0, one launch (start us, length us, event | category | flops | bytes accessed | tf_op | source)
XLA Modules:
  0.0 1490.3 jit_solution(9634371134873248754)
XLA Ops:
  18.6 11.5 fusion.131
  127.3 16.2 %collective-permute-done.6 = bf16[200,984]{1,0:T(8,128)(2,1)S(1)} collective-permute-done((bf16[200,984]{1,0:T(8,128)(2,1)S(1)}, bf16[200,984]{1,0:T(8,128)(2,1)S(1)}, u32[]{:S(2)}, u32[]{:S(2)}) %collective-permute-start.6) | collective-permute-done | bytes 393632 | tf_op jit(solution)/shard_map/ppermute | solution.py:449
  143.6 15.2 %collective-permute-done.8 = bf16[200,984]{1,0:T(8,128)(2,1)S(1)} collective-permute-done((bf16[200,984]{1,0:T(8,128)(2,1)S(1)}, bf16[200,984]{1,0:T(8,128)(2,1)S(1)}, u32[]{:S(2)}, u32[]{:S(2)}) %collective-permute-start.8) | collective-permute-done | bytes 393632 | tf_op jit(solution)/shard_map/ppermute | solution.py:449
  161.2 10.0 collective-permute-done.7
  180.1 9.4 collective-permute-done.11
  226.9 25.4 %shard_map.306 = (bf16[512,256]{1,0:T(8,128)(2,1)}, bf16[512,1600]{1,0:T(8,128)(2,1)}) custom-call(bf16[144,512]{1,0:T(8,128)(2,1)} %pad_maximum_fusion.25.proj, bf16[512,256]{1,0:T(8,128)(2,1)} %get-tuple-element.65.conv, f32[512,256]{1,0:T(8,128)} %get-tuple-element.66.z, bf16[112,256]{1,0:T(8,128)(2,1)} %pad.387.step_w, f32[1,256]{1,0:T(1,128)} %pad.76.step_b, ...), custom_call_target="tpu_custom_call" | custom-call | flops 537395200 | bytes 6059008 | tf_op jit(solution)/shard_map/pallas_call | solution.py:49
  258.3 10.3 collective-permute-done.13
  361.8 14.6 collective-permute-done.45
  384.5 12.6 collective-permute-done.48
  397.1 13.4 collective-permute-start.57
  472.9 25.4 %shard_map.309 = (bf16[512,256]{1,0:T(8,128)(2,1)}, bf16[512,1600]{1,0:T(8,128)(2,1)}) custom-call(bf16[144,512]{1,0:T(8,128)(2,1)} %pad_maximum_fusion.26.proj, bf16[512,256]{1,0:T(8,128)(2,1)} %get-tuple-element.71.conv, f32[512,256]{1,0:T(8,128)} %get-tuple-element.72.z, bf16[112,256]{1,0:T(8,128)(2,1)} %pad.388.step_w, f32[1,256]{1,0:T(1,128)} %pad.86.step_b, ...), custom_call_target="tpu_custom_call" | custom-call | flops 537395200 | bytes 6059008 | tf_op jit(solution)/shard_map/pallas_call | solution.py:49
  505.4 10.3 collective-permute-done.60
  549.4 10.1 collective-permute-done.80
  594.5 10.2 collective-permute-done.90
  633.6 9.9 collective-permute-done.186
  643.4 9.9 collective-permute-done.188
  668.7 39.5 %collective-permute-done.105 = bf16[32,1600]{1,0:T(8,128)(2,1)S(1)} collective-permute-done((bf16[32,1600]{1,0:T(8,128)(2,1)S(1)}, bf16[32,1600]{1,0:T(8,128)(2,1)S(1)}, u32[]{:S(2)}, u32[]{:S(2)}) %collective-permute-start.105) | collective-permute-done | bytes 102432 | tf_op jit(solution)/shard_map/ppermute | solution.py:449
  709.4 10.6 collective-permute-done.107
  734.9 74.5 %shard_map.312 = (bf16[144,512]{1,0:T(8,128)(2,1)}, f32[512,256]{1,0:T(8,128)}, bf16[512,256]{1,0:T(8,128)(2,1)}, f32[24,256]{1,0:T(8,128)}, f32[112,256]{1,0:T(8,128)}) custom-call(bf16[512,1600]{1,0:T(8,128)(2,1)} %bitcast.1156, bf16[144,512]{1,0:T(8,128)(2,1)} %pad_maximum_fusion.26.proj, bf16[512,256]{1,0:T(8,128)(2,1)} %get-tuple-element.71.conv, ...), custom_call_target="tpu_custom_call" | custom-call | flops 1166540800 | bytes 6870016 | tf_op jit(solution)/shard_map/pallas_call | solution.py:49
  912.5 9.7 collective-permute-done.171
  966.0 13.1 collective-permute-done.130
  1012.4 9.9 collective-permute-done.179
  1022.3 9.9 collective-permute-done.181
  1032.1 9.1 collective-permute-done.183
  1057.2 18.3 %collective-permute-done.182 = bf16[200,1032]{1,0:T(8,128)(2,1)S(1)} collective-permute-done((bf16[200,1032]{1,0:T(8,128)(2,1)S(1)}, bf16[200,1032]{1,0:T(8,128)(2,1)S(1)}, u32[]{:S(2)}, u32[]{:S(2)}) %collective-permute-start.182) | collective-permute-done | bytes 412832 | tf_op jit(solution)/shard_map/ppermute | solution.py:449
  1084.8 12.5 collective-permute-start.134
  1141.3 74.5 %shard_map.316 = (bf16[144,512]{1,0:T(8,128)(2,1)}, f32[512,256]{1,0:T(8,128)}, bf16[512,256]{1,0:T(8,128)(2,1)}, f32[24,256]{1,0:T(8,128)}, f32[112,256]{1,0:T(8,128)}) custom-call(bf16[512,1600]{1,0:T(8,128)(2,1)} %bitcast.1154, bf16[144,512]{1,0:T(8,128)(2,1)} %pad_maximum_fusion.25.proj, bf16[512,256]{1,0:T(8,128)(2,1)} %get-tuple-element.65.conv, ...), custom_call_target="tpu_custom_call" | custom-call | flops 1166540800 | bytes 6870016 | tf_op jit(solution)/shard_map/pallas_call | solution.py:49
  1277.6 35.0 %collective-permute-done.174 = bf16[2,288,200]{2,1,0:T(8,128)(2,1)S(1)} collective-permute-done((bf16[2,288,200]{2,1,0:T(8,128)(2,1)S(1)}, bf16[2,288,200]{2,1,0:T(8,128)(2,1)S(1)}, u32[]{:S(2)}, u32[]{:S(2)}) %collective-permute-start.174) | collective-permute-done | bytes 230432 | tf_op jit(solution)/shard_map/ppermute | solution.py:452
  1324.6 12.5 collective-permute-start.164
  1351.7 17.7 %collective-permute-done.164 = bf16[200,984]{1,0:T(8,128)(2,1)S(1)} collective-permute-done((bf16[200,984]{1,0:T(8,128)(2,1)S(1)}, bf16[200,984]{1,0:T(8,128)(2,1)S(1)}, u32[]{:S(2)}, u32[]{:S(2)}) %collective-permute-start.164) | collective-permute-done | bytes 393632 | tf_op jit(solution)/shard_map/ppermute | solution.py:449
  1391.8 17.9 %collective-permute-start.157 = (bf16[32,1600]{1,0:T(8,128)(2,1)S(1)}, bf16[32,1600]{1,0:T(8,128)(2,1)S(1)}, u32[]{:S(2)}, u32[]{:S(2)}) collective-permute-start(bf16[32,1600]{1,0:T(8,128)(2,1)S(1)} %get-tuple-element.444), channel_id=1, source_target_pairs={{0,24},{4,28},{8,0},{12,4},{16,8},{20,12},{24,16},{28,20},{1,25},{... | collective-permute-start | bytes 307208 | tf_op jit(solution)/shard_map/ppermute | solution.py:449
  1419.4 38.3 %psum.7 = bf16[2,4,1600]{2,1,0:T(4,128)(2,1)S(1)} all-reduce(bf16[2,4,1600]{2,1,0:T(4,128)(2,1)S(1)} %pad_maximum_fusion.31), channel_id=1, replica_groups=mesh['dp'=8,'tensor'=4] {'dp','tensor'}, use_global_device_ids=true, to_apply=%region_24.25 | all-reduce | flops 12800 | bytes 51200 | tf_op jit(solution)/shard_map/psum | solution.py:768
  (1313 shorter events, 854.1 us)
Async XLA Ops:
  7.2 1127.1 %all-gather.7.cloned.1.call-start = ((), (), s32[]{:S(2)}) async-start(), calls=%async_computation.1 | async-start | bytes 3072000 | tf_op jit(solution)/shard_map/all_gather | solution.py:799
  11.7 107.5 %collective-permute-start = (bf16[32,1600]{1,0:T(8,128)(2,1)}, bf16[32,1600]{1,0:T(8,128)(2,1)}, u32[]{:S(2)}, u32[]{:S(2)}) collective-permute-start(bf16[32,1600]{1,0:T(8,128)(2,1)} %fusion.44), channel_id=1, source_target_pairs={{0,8},{4,12},{8,16},{12,20},{16,24},{20,28},{24,0},{28,4},{1,9},{5... | collective-permute-start | bytes 307208 | tf_op jit(solution)/shard_map/ppermute | solution.py:449
  14.7 105.2 %collective-permute-start.1 = (bf16[32,1600]{1,0:T(8,128)(2,1)}, bf16[32,1600]{1,0:T(8,128)(2,1)}, u32[]{:S(2)}, u32[]{:S(2)}) collective-permute-start(bf16[32,1600]{1,0:T(8,128)(2,1)} %fusion.44), channel_id=1, source_target_pairs={{0,16},{4,20},{8,24},{12,28},{16,0},{20,4},{24,8},{28,12},{1,17},{... | collective-permute-start | bytes 307208 | tf_op jit(solution)/shard_map/ppermute | solution.py:449
  17.3 102.9 %collective-permute-start.2 = (bf16[32,1600]{1,0:T(8,128)(2,1)}, bf16[32,1600]{1,0:T(8,128)(2,1)}, u32[]{:S(2)}, u32[]{:S(2)}) collective-permute-start(bf16[32,1600]{1,0:T(8,128)(2,1)} %fusion.44), channel_id=1, source_target_pairs={{0,24},{4,28},{8,0},{12,4},{16,8},{20,12},{24,16},{28,20},{1,25},{... | collective-permute-start | bytes 307208 | tf_op jit(solution)/shard_map/ppermute | solution.py:449
  38.1 170.7 %collective-permute-start.35 = (bf16[200,1032]{1,0:T(8,128)(2,1)}, bf16[200,1032]{1,0:T(8,128)(2,1)}, u32[]{:S(2)}, u32[]{:S(2)}) collective-permute-start(bf16[200,1032]{1,0:T(8,128)(2,1)} %get-tuple-element.328), channel_id=1, source_target_pairs={{0,4},{4,0},{8,12},{12,8},{16,20},{20,16},{24,28},{28,24},{1,5},{5... | collective-permute-start | bytes 1238408 | tf_op jit(solution)/shard_map/ppermute | solution.py:452
  67.1 57.6 %collective-permute-start.5 = (bf16[200,984]{1,0:T(8,128)(2,1)}, bf16[200,984]{1,0:T(8,128)(2,1)}, u32[]{:S(2)}, u32[]{:S(2)}) collective-permute-start(bf16[200,984]{1,0:T(8,128)(2,1)} %get-tuple-element.364), channel_id=1, source_target_pairs={{0,4},{4,0},{8,12},{12,8},{16,20},{20,16},{24,28},{28,24},{1,5},{5... | collective-permute-start | bytes 1180808 | tf_op jit(solution)/shard_map/ppermute | solution.py:452
  119.2 93.8 %collective-permute-start.36 = (bf16[200,1032]{1,0:T(8,128)(2,1)}, bf16[200,1032]{1,0:T(8,128)(2,1)}, u32[]{:S(2)}, u32[]{:S(2)}) collective-permute-start(bf16[200,1032]{1,0:T(8,128)(2,1)} %get-tuple-element.330), channel_id=1, source_target_pairs={{0,8},{4,12},{8,16},{12,20},{16,24},{20,28},{24,0},{28,4},{1,9},{5... | collective-permute-start | bytes 1238408 | tf_op jit(solution)/shard_map/ppermute | solution.py:449
  120.1 38.7 %collective-permute-start.8 = (bf16[200,984]{1,0:T(8,128)(2,1)S(1)}, bf16[200,984]{1,0:T(8,128)(2,1)S(1)}, u32[]{:S(2)}, u32[]{:S(2)}) collective-permute-start(bf16[200,984]{1,0:T(8,128)(2,1)S(1)} %copy-done.110), channel_id=1, source_target_pairs={{0,16},{4,20},{8,24},{12,28},{16,0},{20,4},{24,8},{28,12},{1,17},{... | collective-permute-start | bytes 1180808 | tf_op jit(solution)/shard_map/ppermute | solution.py:449
  171.3 100.4 %collective-permute-start.38 = (bf16[200,1032]{1,0:T(8,128)(2,1)}, bf16[200,1032]{1,0:T(8,128)(2,1)}, u32[]{:S(2)}, u32[]{:S(2)}) collective-permute-start(bf16[200,1032]{1,0:T(8,128)(2,1)} %get-tuple-element.329), channel_id=1, source_target_pairs={{0,16},{4,20},{8,24},{12,28},{16,0},{20,4},{24,8},{28,12},{1,17},{... | collective-permute-start | bytes 1238408 | tf_op jit(solution)/shard_map/ppermute | solution.py:449
  189.4 108.9 %collective-permute-start.40 = (bf16[200,1032]{1,0:T(8,128)(2,1)}, bf16[200,1032]{1,0:T(8,128)(2,1)}, u32[]{:S(2)}, u32[]{:S(2)}) collective-permute-start(bf16[200,1032]{1,0:T(8,128)(2,1)} %get-tuple-element.327), channel_id=1, source_target_pairs={{0,24},{4,28},{8,0},{12,4},{16,8},{20,12},{24,16},{28,20},{1,25},{... | collective-permute-start | bytes 1238408 | tf_op jit(solution)/shard_map/ppermute | solution.py:449
  338.1 42.6 %collective-permute-start.55 = (bf16[200,984]{1,0:T(8,128)(2,1)S(1)}, bf16[200,984]{1,0:T(8,128)(2,1)S(1)}, u32[]{:S(2)}, u32[]{:S(2)}) collective-permute-start(bf16[200,984]{1,0:T(8,128)(2,1)S(1)} %copy-done.113), channel_id=1, source_target_pairs={{0,16},{4,20},{8,24},{12,28},{16,0},{20,4},{24,8},{28,12},{1,17},{... | collective-permute-start | bytes 1180808 | tf_op jit(solution)/shard_map/ppermute | solution.py:449
  340.8 70.9 %collective-permute-start.54 = (bf16[200,984]{1,0:T(8,128)(2,1)}, bf16[200,984]{1,0:T(8,128)(2,1)S(1)}, u32[]{:S(2)}, u32[]{:S(2)}) collective-permute-start(bf16[200,984]{1,0:T(8,128)(2,1)} %collective-permute-done.53), channel_id=1, source_target_pairs={{0,4},{4,0},{8,12},{12,8},{16,20},{20,16},{24,28},{28,24},{1,5},{5... | collective-permute-start | bytes 1180808 | tf_op jit(solution)/shard_map/ppermute | solution.py:452
  380.7 137.6 %collective-permute-start.85 = (bf16[200,1032]{1,0:T(8,128)(2,1)}, bf16[200,1032]{1,0:T(8,128)(2,1)}, u32[]{:S(2)}, u32[]{:S(2)}) collective-permute-start(bf16[200,1032]{1,0:T(8,128)(2,1)} %get-tuple-element.325), channel_id=1, source_target_pairs={{0,16},{4,20},{8,24},{12,28},{16,0},{20,4},{24,8},{28,12},{1,17},{... | collective-permute-start | bytes 1238408 | tf_op jit(solution)/shard_map/ppermute | solution.py:449
  384.5 136.0 %collective-permute-start.87 = (bf16[200,1032]{1,0:T(8,128)(2,1)}, bf16[200,1032]{1,0:T(8,128)(2,1)}, u32[]{:S(2)}, u32[]{:S(2)}) collective-permute-start(bf16[200,1032]{1,0:T(8,128)(2,1)} %get-tuple-element.323), channel_id=1, source_target_pairs={{0,24},{4,28},{8,0},{12,4},{16,8},{20,12},{24,16},{28,20},{1,25},{... | collective-permute-start | bytes 1238408 | tf_op jit(solution)/shard_map/ppermute | solution.py:449
  521.5 39.3 %collective-permute-start.88 = (bf16[200,1032]{1,0:T(8,128)(2,1)}, bf16[200,1032]{1,0:T(8,128)(2,1)S(1)}, u32[]{:S(2)}, u32[]{:S(2)}) collective-permute-start(bf16[200,1032]{1,0:T(8,128)(2,1)} %collective-permute-done.87), channel_id=1, source_target_pairs={{0,4},{4,0},{8,12},{12,8},{16,20},{20,16},{24,28},{28,24},{1,5},{5... | collective-permute-start | bytes 1238408 | tf_op jit(solution)/shard_map/ppermute | solution.py:452
  661.5 47.4 %collective-permute-start.187 = (bf16[200,1032]{1,0:T(8,128)(2,1)S(1)}, bf16[200,1032]{1,0:T(8,128)(2,1)S(1)}, u32[]{:S(2)}, u32[]{:S(2)}) collective-permute-start(bf16[200,1032]{1,0:T(8,128)(2,1)S(1)} %get-tuple-element.200), channel_id=1, source_target_pairs={{0,8},{4,12},{8,16},{12,20},{16,24},{20,28},{24,0},{28,4},{1,9},{5... | collective-permute-start | bytes 1238408 | tf_op jit(solution)/shard_map/ppermute | solution.py:449
  663.1 45.8 %collective-permute-start.189 = (bf16[200,1032]{1,0:T(8,128)(2,1)S(1)}, bf16[200,1032]{1,0:T(8,128)(2,1)S(1)}, u32[]{:S(2)}, u32[]{:S(2)}) collective-permute-start(bf16[200,1032]{1,0:T(8,128)(2,1)S(1)} %get-tuple-element.199), channel_id=1, source_target_pairs={{0,16},{4,20},{8,24},{12,28},{16,0},{20,4},{24,8},{28,12},{1,17},{... | collective-permute-start | bytes 1238408 | tf_op jit(solution)/shard_map/ppermute | solution.py:449
  664.3 44.6 %collective-permute-start.191 = (bf16[200,1032]{1,0:T(8,128)(2,1)S(1)}, bf16[200,1032]{1,0:T(8,128)(2,1)S(1)}, u32[]{:S(2)}, u32[]{:S(2)}) collective-permute-start(bf16[200,1032]{1,0:T(8,128)(2,1)S(1)} %get-tuple-element.198), channel_id=1, source_target_pairs={{0,24},{4,28},{8,0},{12,4},{16,8},{20,12},{24,16},{28,20},{1,25},{... | collective-permute-start | bytes 1238408 | tf_op jit(solution)/shard_map/ppermute | solution.py:449
  665.8 42.4 %collective-permute-start.105 = (bf16[32,1600]{1,0:T(8,128)(2,1)S(1)}, bf16[32,1600]{1,0:T(8,128)(2,1)S(1)}, u32[]{:S(2)}, u32[]{:S(2)}) collective-permute-start(bf16[32,1600]{1,0:T(8,128)(2,1)S(1)} %get-tuple-element.549), channel_id=1, source_target_pairs={{0,16},{4,20},{8,24},{12,28},{16,0},{20,4},{24,8},{28,12},{1,17},{... | collective-permute-start | bytes 307208 | tf_op jit(solution)/shard_map/ppermute | solution.py:449
  667.4 40.7 %collective-permute-start.106 = (bf16[32,1600]{1,0:T(8,128)(2,1)S(1)}, bf16[32,1600]{1,0:T(8,128)(2,1)S(1)}, u32[]{:S(2)}, u32[]{:S(2)}) collective-permute-start(bf16[32,1600]{1,0:T(8,128)(2,1)S(1)} %get-tuple-element.549), channel_id=1, source_target_pairs={{0,24},{4,28},{8,0},{12,4},{16,8},{20,12},{24,16},{28,20},{1,25},{... | collective-permute-start | bytes 307208 | tf_op jit(solution)/shard_map/ppermute | solution.py:449
  732.4 81.1 %collective-permute-start.120 = (bf16[4,32,1600]{2,1,0:T(8,128)(2,1)S(1)}, bf16[4,32,1600]{2,1,0:T(8,128)(2,1)S(1)}, u32[]{:S(2)}, u32[]{:S(2)}) collective-permute-start(bf16[4,32,1600]{2,1,0:T(8,128)(2,1)S(1)} %get-tuple-element.464), channel_id=1, source_target_pairs={{0,2},{1,3},{2,0},{3,1},{4,6},{5,7},{6,4},{7,5},{8,10},{9,11},{10,... | collective-permute-start | bytes 1228808 | tf_op jit(solution)/shard_map/ppermute | solution.py:462
  866.5 57.3 %collective-permute-start.122 = (bf16[4,2,32,1600]{3,2,0,1:T(8,128)(2,1)}, bf16[4,2,32,1600]{3,2,0,1:T(8,128)(2,1)}, u32[]{:S(2)}, u32[]{:S(2)}) collective-permute-start(bf16[4,2,32,1600]{3,2,0,1:T(8,128)(2,1)} %bitcast.1117), channel_id=1, source_target_pairs={{0,1},{1,0},{2,3},{3,2},{4,5},{5,4},{6,7},{7,6},{8,9},{9,8},{10,11... | collective-permute-start | bytes 2457608 | tf_op jit(solution)/shard_map/ppermute | solution.py:472
  960.4 507.3 %all-gather.5.cloned.1.call-start = ((), (), s32[]{:S(2)}) async-start(), calls=%async_computation | async-start | bytes 3072000 | tf_op jit(solution)/shard_map/all_gather | solution.py:799
  1001.1 40.1 %collective-permute-start.183 = (bf16[200,1032]{1,0:T(8,128)(2,1)S(1)}, bf16[200,1032]{1,0:T(8,128)(2,1)S(1)}, u32[]{:S(2)}, u32[]{:S(2)}) collective-permute-start(bf16[200,1032]{1,0:T(8,128)(2,1)S(1)} %get-tuple-element.194), channel_id=1, source_target_pairs={{0,4},{4,0},{8,12},{12,8},{16,20},{20,16},{24,28},{28,24},{1,5},{5... | collective-permute-start | bytes 1238408 | tf_op jit(solution)/shard_map/ppermute | solution.py:452
  1003.4 45.0 %collective-permute-start.132 = (bf16[4,2,32,1600]{3,2,0,1:T(8,128)(2,1)S(1)}, bf16[4,2,32,1600]{3,2,0,1:T(8,128)(2,1)S(1)}, u32[]{:S(2)}, u32[]{:S(2)}) collective-permute-start(bf16[4,2,32,1600]{3,2,0,1:T(8,128)(2,1)S(1)} %bitcast.1256), channel_id=1, source_target_pairs={{0,1},{1,0},{2,3},{3,2},{4,5},{5,4},{6,7},{7,6},{8,9},{9,8},{10,11... | collective-permute-start | bytes 2457608 | tf_op jit(solution)/shard_map/ppermute | solution.py:472
  1131.7 95.6 %collective-permute-start.153 = (bf16[4,32,1600]{2,1,0:T(8,128)(2,1)}, bf16[4,32,1600]{2,1,0:T(8,128)(2,1)S(1)}, u32[]{:S(2)}, u32[]{:S(2)}) collective-permute-start(bf16[4,32,1600]{2,1,0:T(8,128)(2,1)} %get-tuple-element.449), channel_id=1, source_target_pairs={{0,2},{1,3},{2,0},{3,1},{4,6},{5,7},{6,4},{7,5},{8,10},{9,11},{10,... | collective-permute-start | bytes 1228808 | tf_op jit(solution)/shard_map/ppermute | solution.py:462
  1271.3 41.5 %collective-permute-start.160 = (bf16[200,984]{1,0:T(8,128)(2,1)S(1)}, bf16[200,984]{1,0:T(8,128)(2,1)S(1)}, u32[]{:S(2)}, u32[]{:S(2)}) collective-permute-start(bf16[200,984]{1,0:T(8,128)(2,1)S(1)} %get-tuple-element.209), channel_id=1, source_target_pairs={{0,4},{4,0},{8,12},{12,8},{16,20},{20,16},{24,28},{28,24},{1,5},{5... | collective-permute-start | bytes 1180808 | tf_op jit(solution)/shard_map/ppermute | solution.py:452
  1272.1 41.3 %collective-permute-start.161 = (bf16[200,984]{1,0:T(8,128)(2,1)S(1)}, bf16[200,984]{1,0:T(8,128)(2,1)S(1)}, u32[]{:S(2)}, u32[]{:S(2)}) collective-permute-start(bf16[200,984]{1,0:T(8,128)(2,1)S(1)} %get-tuple-element.212), channel_id=1, source_target_pairs={{0,4},{4,0},{8,12},{12,8},{16,20},{20,16},{24,28},{28,24},{1,5},{5... | collective-permute-start | bytes 1180808 | tf_op jit(solution)/shard_map/ppermute | solution.py:452
  1273.4 41.3 %collective-permute-start.163 = (bf16[200,984]{1,0:T(8,128)(2,1)S(1)}, bf16[200,984]{1,0:T(8,128)(2,1)S(1)}, u32[]{:S(2)}, u32[]{:S(2)}) collective-permute-start(bf16[200,984]{1,0:T(8,128)(2,1)S(1)} %get-tuple-element.211), channel_id=1, source_target_pairs={{0,4},{4,0},{8,12},{12,8},{16,20},{20,16},{24,28},{28,24},{1,5},{5... | collective-permute-start | bytes 1180808 | tf_op jit(solution)/shard_map/ppermute | solution.py:452
  1274.2 43.4 %collective-permute-start.165 = (bf16[200,984]{1,0:T(8,128)(2,1)S(1)}, bf16[200,984]{1,0:T(8,128)(2,1)S(1)}, u32[]{:S(2)}, u32[]{:S(2)}) collective-permute-start(bf16[200,984]{1,0:T(8,128)(2,1)S(1)} %get-tuple-element.210), channel_id=1, source_target_pairs={{0,4},{4,0},{8,12},{12,8},{16,20},{20,16},{24,28},{28,24},{1,5},{5... | collective-permute-start | bytes 1180808 | tf_op jit(solution)/shard_map/ppermute | solution.py:452
  1312.6 65.8 %collective-permute-start.155 = (bf16[4,2,32,1600]{3,2,0,1:T(8,128)(2,1)}, bf16[4,2,32,1600]{3,2,0,1:T(8,128)(2,1)}, u32[]{:S(2)}, u32[]{:S(2)}) collective-permute-start(bf16[4,2,32,1600]{3,2,0,1:T(8,128)(2,1)} %bitcast.1115), channel_id=1, source_target_pairs={{0,1},{1,0},{2,3},{3,2},{4,5},{5,4},{6,7},{7,6},{8,9},{9,8},{10,11... | collective-permute-start | bytes 2457608 | tf_op jit(solution)/shard_map/ppermute | solution.py:472
  1324.6 44.9 %collective-permute-start.164 = (bf16[200,984]{1,0:T(8,128)(2,1)S(1)}, bf16[200,984]{1,0:T(8,128)(2,1)S(1)}, u32[]{:S(2)}, u32[]{:S(2)}) collective-permute-start(bf16[200,984]{1,0:T(8,128)(2,1)S(1)} %get-tuple-element.207), channel_id=1, source_target_pairs={{0,16},{4,20},{8,24},{12,28},{16,0},{20,4},{24,8},{28,12},{1,17},{... | collective-permute-start | bytes 1180808 | tf_op jit(solution)/shard_map/ppermute | solution.py:449
  (400 other events, 4798.5 us)
Sparse Core Ops, SparseCore 0:
  960.5 26.5 all-gather.6
  1373.9 31.1 all-gather.4

commit v2 on v1

v2 whole, which is shorter than its diff:
```python
import functools

import jax
import jax.numpy as jnp
from jax import lax
from jax.experimental import pallas as pl
from jax.experimental.pallas import tpu as pltpu
from jax.sharding import PartitionSpec as P

KVH = 5
HEAD = 64
GQ = 5
CONV = 4
WINDOW = 1024
EPSILON = 1e-06
GROUP = 4
LANES = 128
F32 = jnp.float32
BF16 = jnp.bfloat16
NN = (((1,), (0,)), ((), ()))
NT = (((1,), (1,)), ((), ()))
TN = (((0,), (0,)), ((), ()))


def mm(left, right, dims=NN):
    return lax.dot_general(left, right, dims, preferred_element_type=F32)


def sigmoid(v):
    return 1.0 / (1.0 + jnp.exp(-v))


def softplus(v):
    return jnp.maximum(v, 0.0) + jnp.log(1.0 + jnp.exp(-jnp.abs(v)))


def params(megabytes=56):
    return pltpu.CompilerParams(vmem_limit_bytes=megabytes * 2**20)


def cost(micros):
    return pl.CostEstimate(flops=int(micros * 10**9), bytes_accessed=1, transcendentals=0)


def call(kernel, outs, args, micros, scratch=(), place=None, layers=()):
    vmem = pl.BlockSpec(memory_space=pltpu.VMEM)
    specs = []
    for k, a in enumerate(args):
        layer = layers[k] if k < len(layers) else None
        if layer is None:
            specs.append(vmem)
        else:
            at = (layer,) + (0,) * (a.ndim - 1)
            specs.append(pl.BlockSpec((None,) + a.shape[1:], lambda step, at=at: at))
    if place is not None:
        specs.insert(0, pl.BlockSpec(memory_space=pltpu.SMEM))
        args = [place] + list(args)
    return pl.pallas_call(
        kernel,
        out_shape=outs,
        grid=(1,) if layers else (),
        in_specs=specs,
        out_specs=[vmem] * len(outs),
        scratch_shapes=list(scratch),
        compiler_params=params(),
        cost_estimate=cost(micros),
    )(*args)


def call_into(kernel, layer, outs, before, args, place):
    vmem = pl.BlockSpec(memory_space=pltpu.VMEM)
    specs = [pl.BlockSpec(memory_space=pltpu.SMEM)] + [vmem] * len(args)
    out_specs = []
    for o in outs:
        at = (layer,) + (0,) * (len(o.shape) - 1)
        out_specs.append(pl.BlockSpec((None,) + o.shape[1:], lambda step, at=at: at))
    operands = [place] + list(args)
    aliases = {}
    if before is not None:
        aliases = {len(operands) + k: k for k in range(len(outs))}
        specs += [pl.BlockSpec(memory_space=pl.ANY)] * len(outs)
        operands += list(before)
    skip = len(aliases)

    def body(*refs):
        count = 1 + len(args)
        kernel(*refs[:count], *refs[count + skip :])

    return pl.pallas_call(
        body,
        out_shape=outs,
        grid=(1,),
        in_specs=specs,
        out_specs=out_specs,
        input_output_aliases=aliases,
        compiler_params=params(),
        cost_estimate=cost(4),
    )(*operands)


def out(shape, dtype):
    return jax.ShapeDtypeStruct(shape, dtype)


def widen(values, width):
    rows, have = values.shape
    if have == width:
        return values
    return jnp.concatenate([values, jnp.zeros((rows, width - have), values.dtype)], axis=1)


def shift_rows(values, amount, length):
    if amount == 0:
        return values
    rows = values.shape[0]
    place = lax.broadcasted_iota(jnp.int32, values.shape, 0) % length
    moved = pltpu.roll(values, amount % rows, 0)
    inside = place >= amount if amount > 0 else place < length + amount
    return jnp.where(inside, moved, 0.0)


def conv_pre(inner_x, taps, bias, length):
    running = bias
    for k in range(CONV):
        running = running + shift_rows(inner_x, CONV - 1 - k, length) * taps[k : k + 1]
    return running


def scores_of(queries, keys, length):
    scores = lax.dot_general(
        queries, keys, (((2,), (2,)), ((0,), (0,))), preferred_element_type=F32
    ) * HEAD ** (-0.5)
    shape = scores.shape
    query_pos = lax.broadcasted_iota(jnp.int32, shape, 1)
    key_pos = lax.broadcasted_iota(jnp.int32, shape, 2)
    allowed = (key_pos <= query_pos) & (key_pos > query_pos - WINDOW)
    scores = jnp.where(allowed, scores, -1e30)
    weights = jnp.exp(scores - jnp.max(scores, axis=-1, keepdims=True))
    return weights / jnp.sum(weights, axis=-1, keepdims=True)


class Mix:
    def __init__(self, chan):
        self.q = 0
        self.kv = 2 * HEAD
        self.o = 4 * HEAD
        self.s = 6 * HEAD
        self.x = self.s + chan
        self.z = self.x + chan
        self.end = self.z + chan


def swap(flag, first, second):
    return jnp.where(flag, second, first), jnp.where(flag, first, second)


def to_sequences(place, values):
    rows, columns = values.shape
    blocks = values.reshape(4, GROUP, rows // (4 * GROUP), columns)
    chip, core = place[2] == 1, place[3] == 1
    low, high = [], []
    for own in (0, 1):
        first, second = swap(chip, blocks[2 * own], blocks[2 * own + 1])
        low.append(first)
        high.append(second)
    parts = []
    for pair in (low, high):
        parts.append(jnp.stack(swap(core, pair[0], pair[1]), axis=1))
    return jnp.stack(parts, axis=1).reshape(rows, columns)


def to_blocks(place, values):
    rows, columns = values.shape
    parts = values.reshape(GROUP, 2, 2, rows // (4 * GROUP), columns)
    chip, core = place[2] == 1, place[3] == 1
    own, other = swap(core, parts[:, :, 0], parts[:, :, 1])
    blocks = []
    for half in (own, other):
        blocks.extend(swap(chip, half[:, 0], half[:, 1]))
    return jnp.concatenate([b.reshape(rows // 4, columns) for b in blocks], axis=0)


def rows_of(blocks):
    return jnp.concatenate([b[...] for b in blocks], axis=0)


def to_parts(parts, values):
    count = values.shape[0] // 4
    for k in range(4):
        parts[k][...] = values[k * count : (k + 1) * count].astype(BF16)


def mix_forward_kernel(cols, chan, wide, length, place, n0, n1, n2, n3, w, vec, scan_w, xi, z, conv, qkv, heads, proj, p0, p1, p2, p3):
    normed = rows_of((n0, n1, n2, n3))
    both = to_sequences(place, mm(normed, w[:, : cols.o]).astype(BF16))
    qkv[...] = both
    inner = to_sequences(place, mm(normed, w[:, cols.x :]))
    inner_x = widen(inner[:, :chan], wide)
    xi[...] = inner_x
    z[...] = widen(inner[:, chan:], wide)
    running = conv_pre(inner_x, vec[:CONV], vec[CONV : CONV + 1], length)
    conv_low = (running * sigmoid(running)).astype(BF16)
    conv[...] = conv_low
    proj[...] = mm(scan_w[...], conv_low, NT).astype(BF16)
    seqs = normed.shape[0] // length
    keys = both[:, cols.kv : cols.kv + HEAD].reshape(seqs, length, HEAD)
    values = both[:, cols.kv + HEAD : cols.o].reshape(seqs, length, HEAD)
    outs = []
    for h in range(2):
        queries = both[:, h * HEAD : (h + 1) * HEAD].reshape(seqs, length, HEAD)
        probs = scores_of(queries, keys, length).astype(BF16)
        mixed = lax.dot_general(
            probs, values, (((2,), (1,)), ((0,), (0,))), preferred_element_type=F32
        )
        outs.append(mixed.reshape(seqs * length, HEAD))
    heads_out = to_blocks(place, jnp.concatenate(outs, axis=1).astype(BF16))
    heads[...] = heads_out
    to_parts((p0, p1, p2, p3), mm(heads_out, w[:, cols.o : cols.s], NT))


def spread(state, wide):
    row = lax.broadcasted_iota(jnp.int32, (state, wide), 0)
    col = lax.broadcasted_iota(jnp.int32, (state, wide), 1) // LANES
    return (row == col).astype(BF16)


def lane(n):
    return slice(n * LANES, (n + 1) * LANES)


def tiles_in(ref, values):
    for n in range(ref.shape[0]):
        ref[n] = values[:, lane(n)]


def tiles_out(ref):
    return jnp.concatenate([ref[n] for n in range(ref.shape[0])], axis=1)


LOG2E = 1.4426950408889634
STATES_AT_ONCE = 8


def time_major(rows, length):
    seqs = rows // length
    came = lax.broadcasted_iota(jnp.int32, (rows, rows), 0)
    goes = lax.broadcasted_iota(jnp.int32, (rows, rows), 1)
    return (came == (goes % seqs) * length + goes // seqs).astype(BF16)


def scan_setup(rank, state, seqs, length, proj, conv, step_w, step_b, dlog, dt_s, dtx_s, drive_s, read_s, rate_s):
    pre = mm(proj[:rank], step_w[...], TN) + step_b
    dt = softplus(pre)
    tiles_in(dt_s, dt)
    tiles_in(dtx_s, dt * conv)
    table = spread(state, state * LANES)
    order = time_major(seqs * length, length)
    maps = mm(proj[rank:], order).astype(BF16)
    drive = mm(maps[:state], table, TN)
    read = mm(maps[state:], table, TN)
    for n in range(state):
        drive_s[:, n] = drive[:, lane(n)].reshape(length, seqs, LANES)
        read_s[:, n] = read[:, lane(n)].reshape(length, seqs, LANES)
    rates = -LOG2E * jnp.exp(dlog[...])
    for n in range(state):
        rate_s[n] = jnp.broadcast_to(rates[n : n + 1], (seqs, rates.shape[1]))
    return pre


def scan_forward_loop(first, tiles, seqs, length, dt_s, dtx_s, drive_s, read_s, rate_s, y_s, keep_s):
    def step(t, held):
        rows = pl.ds(t, seqs, stride=length)
        dt = [dt_s[i, rows] for i in range(tiles)]
        dtx = [dtx_s[i, rows] for i in range(tiles)]
        total = [y_s[i, rows] if first else jnp.zeros_like(dt[i]) for i in range(tiles)]
        fresh = []
        for j in range(STATES_AT_ONCE):
            n = first + j
            drive = drive_s[t, n]
            read = read_s[t, n]
            for i in range(tiles):
                decay = jnp.exp2(dt[i] * rate_s[n, :, lane(i)])
                now = decay * held[j * tiles + i] + dtx[i] * drive
                total[i] = total[i] + now * read
                if keep_s is not None:
                    keep_s[t, j * tiles + i] = now
                fresh.append(now)
        for i in range(tiles):
            y_s[i, rows] = total[i]
        return tuple(fresh)

    zero = jnp.zeros((seqs, LANES), F32)
    lax.fori_loop(0, length, step, (zero,) * (STATES_AT_ONCE * tiles))


def scan_forward_kernel(cols, chan, wide, rank, state, seqs, length, place, proj, conv, z, step_w, vec, dlog, w, gated, p0, p1, p2, p3, dt_s, dtx_s, drive_s, read_s, rate_s, y_s):
    conv32 = conv[...].astype(F32)
    step_b, skip = vec[CONV + 1 : CONV + 2], vec[CONV + 2 : CONV + 3]
    scan_setup(rank, state, seqs, length, proj, conv32, step_w, step_b, dlog, dt_s, dtx_s, drive_s, read_s, rate_s)
    for first in range(0, state, STATES_AT_ONCE):
        scan_forward_loop(first, wide // LANES, seqs, length, dt_s, dtx_s, drive_s, read_s, rate_s, y_s, None)
    gate = z[...]
    low = ((tiles_out(y_s) + skip * conv32) * (gate * sigmoid(gate))).astype(BF16)
    low = to_blocks(place, low)
    gated[...] = low
    to_parts((p0, p1, p2, p3), mm(low[:, :chan], w[:, cols.s : cols.x], NT))


def split_sum(table, values):
    high = values.astype(BF16)
    rest = (values - high.astype(F32)).astype(BF16)
    return mm(table, high, NT) + mm(table, rest, NT)


def scan_backward_loop(first, tiles, seqs, length, dt_s, dtx_s, drive_s, read_s, rate_s, keep_s, ds_s, ddt_s, dsrc_s, pd_s, pr_s):
    count = STATES_AT_ONCE * tiles

    def step(back, carry):
        t = length - 1 - back
        rows = pl.ds(t, seqs, stride=length)
        dt = [dt_s[i, rows] for i in range(tiles)]
        dtx = [dtx_s[i, rows] for i in range(tiles)]
        ds = [ds_s[i, rows] for i in range(tiles)]
        zero = jnp.zeros_like(dt[0])
        d_src = [dsrc_s[i, rows] if first else zero for i in range(tiles)]
        d_dt = [ddt_s[i, rows] if first else zero for i in range(tiles)]
        lams = []
        sums = []
        for j in range(STATES_AT_ONCE):
            n = first + j
            drive = drive_s[t, n]
            read = read_s[t, n]
            of_read = zero
            of_drive = zero
            for i in range(tiles):
                k = j * tiles + i
                rate = rate_s[n, :, lane(i)]
                kept = keep_s[t, k]
                lam = carry[k] + read * ds[i]
                of_read = of_read + kept * ds[i]
                of_drive = of_drive + lam * dtx[i]
                d_src[i] = d_src[i] + lam * drive
                d_log = lam * (kept - dtx[i] * drive)
                d_dt[i] = d_dt[i] + d_log * rate
                sums.append(carry[count + k] + d_log * dt[i])
                lams.append(jnp.exp2(dt[i] * rate) * lam)
            pr_s[t, n] = of_read
            pd_s[t, n] = of_drive
        for i in range(tiles):
            dsrc_s[i, rows] = d_src[i]
            ddt_s[i, rows] = d_dt[i]
        return tuple(lams) + tuple(sums)

    zero = jnp.zeros((seqs, LANES), F32)
    return lax.fori_loop(0, length, step, (zero,) * (2 * count))[count:]


def scan_backward_kernel(cols, chan, wide, rank, state, seqs, length, place, g0, g1, g2, g3, proj, conv, z, step_w, vec, dlog, w, d_proj, d_conv, d_z, small, d_step_w, dt_s, dtx_s, drive_s, read_s, rate_s, y_s, keep_s, ds_s, ddt_s, dsrc_s, pd_s, pr_s):
    tiles = wide // LANES
    conv32 = conv[...].astype(F32)
    step_b, skip = vec[CONV + 1 : CONV + 2], vec[CONV + 2 : CONV + 3]
    pre = scan_setup(rank, state, seqs, length, proj, conv32, step_w, step_b, dlog, dt_s, dtx_s, drive_s, read_s, rate_s)
    d_gated = to_sequences(place, mm(rows_of((g0, g1, g2, g3)), w[:, cols.s : cols.x]))
    d_gated = widen(d_gated, wide)
    gate = z[...]
    sig = sigmoid(gate)
    d_scanned = d_gated * (gate * sig)
    tiles_in(ds_s, d_scanned)
    d_rates = []
    for first in range(0, state, STATES_AT_ONCE):
        scan_forward_loop(first, tiles, seqs, length, dt_s, dtx_s, drive_s, read_s, rate_s, y_s, keep_s)
        sums = scan_backward_loop(first, tiles, seqs, length, dt_s, dtx_s, drive_s, read_s, rate_s, keep_s, ds_s, ddt_s, dsrc_s, pd_s, pr_s)
        for j in range(STATES_AT_ONCE):
            d_rates.append(
                jnp.concatenate(
                    [jnp.sum(sums[j * tiles + i], axis=0, keepdims=True) for i in range(tiles)],
                    axis=1,
                )
            )
    d_src = tiles_out(dsrc_s)
    dt = tiles_out(dt_s)
    d_dt = tiles_out(ddt_s) * (1.0 / LOG2E) + d_src * conv32
    d_conv[...] = skip * d_scanned + d_src * dt
    scanned = tiles_out(y_s) + skip * conv32
    d_z[...] = (d_gated * scanned * (sig * (1.0 + gate * (1.0 - sig)))).astype(BF16)
    d_pre = d_dt * sigmoid(pre)
    rates = -jnp.exp(dlog[...])
    small[0:1] = jnp.sum(d_pre, axis=0, keepdims=True)
    small[1:2] = jnp.sum(d_scanned * conv32, axis=0, keepdims=True)
    small[2:8] = jnp.zeros((6, wide), F32)
    small[8:] = jnp.concatenate(d_rates, axis=0) * rates
    low = d_pre.astype(BF16)
    d_step_w[...] = mm(proj[:rank], low)
    table = spread(state, state * LANES)
    tokens = seqs * length
    by_time = [
        jnp.concatenate([ref[:, n].reshape(tokens, LANES) for n in range(state)], axis=1)
        for ref in (pd_s, pr_s)
    ]
    d_maps = jnp.concatenate([split_sum(table, values) for values in by_time], axis=0)
    order = time_major(tokens, length)
    d_proj[:rank] = mm(step_w[...], low, NT).astype(BF16)
    d_proj[rank:] = mm(d_maps.astype(BF16), order, NT).astype(BF16)


def attend_backward_kernel(cols, length, place, g0, g1, g2, g3, w, qkv, d_qkv):
    d_heads = mm(rows_of((g0, g1, g2, g3)), w[:, cols.o : cols.s]).astype(BF16)
    d_heads = to_sequences(place, d_heads)
    both = qkv[...]
    seqs = both.shape[0] // length
    keys = both[:, cols.kv : cols.kv + HEAD].reshape(seqs, length, HEAD)
    values = both[:, cols.kv + HEAD : cols.o].reshape(seqs, length, HEAD)
    parts = []
    d_keys = 0.0
    d_values = 0.0
    for h in range(2):
        queries = both[:, h * HEAD : (h + 1) * HEAD].reshape(seqs, length, HEAD)
        d_out = d_heads[:, h * HEAD : (h + 1) * HEAD].reshape(seqs, length, HEAD)
        probs = scores_of(queries, keys, length)
        d_probs = lax.dot_general(
            d_out, values, (((2,), (2,)), ((0,), (0,))), preferred_element_type=F32
        )
        d_scores = (
            probs
            * (d_probs - jnp.sum(d_probs * probs, axis=-1, keepdims=True))
            * HEAD ** (-0.5)
        ).astype(BF16)
        d_query = lax.dot_general(
            d_scores, keys, (((2,), (1,)), ((0,), (0,))), preferred_element_type=F32
        )
        parts.append(d_query.reshape(seqs * length, HEAD))
        d_keys = d_keys + lax.dot_general(
            d_scores, queries, (((1,), (1,)), ((0,), (0,))), preferred_element_type=F32
        )
        d_values = d_values + lax.dot_general(
            probs.astype(BF16), d_out, (((1,), (1,)), ((0,), (0,))), preferred_element_type=F32
        )
    parts.append(d_keys.reshape(seqs * length, HEAD))
    parts.append(d_values.reshape(seqs * length, HEAD))
    d_qkv[...] = jnp.concatenate(parts, axis=1).astype(BF16)


def mix_backward_kernel(cols, chan, length, place, proj, conv, xi, d_conv, d_z, d_qkv, w, vec, scan_w, d_x, p0, p1, p2, p3, d_scan_w, small):
    taps, bias = vec[:CONV], vec[CONV : CONV + 1]
    d_out = d_conv[...] + mm(proj[...], scan_w[...], TN)
    inner_x = xi[...]
    running = conv_pre(inner_x, taps, bias, length)
    sig = sigmoid(running)
    d_run = d_out * (sig * (1.0 + running * (1.0 - sig)))
    d_in = 0.0
    for k in range(CONV):
        back = CONV - 1 - k
        d_in = d_in + shift_rows(d_run, -back, length) * taps[k : k + 1]
        small[k : k + 1] = jnp.sum(d_run * shift_rows(inner_x, back, length), axis=0, keepdims=True)
    small[CONV : CONV + 1] = jnp.sum(d_run, axis=0, keepdims=True)
    small[CONV + 1 :] = jnp.zeros((8 - CONV - 1, inner_x.shape[1]), F32)
    low = d_in.astype(BF16)
    d_x[...] = low
    inner = to_blocks(place, jnp.concatenate([low[:, :chan], d_z[:, :chan]], axis=1))
    heads = to_blocks(place, d_qkv[...])
    to_parts((p0, p1, p2, p3), mm(inner, w[:, cols.x :], NT) + mm(heads, w[:, : cols.o], NT))
    d_scan_w[...] = mm(proj[...], conv[...])


def mix_weights_kernel(cols, chan, place, n0, n1, n2, n3, a0, a1, a2, a3, s0, s1, s2, s3, d_qkv, heads, gated, d_x, d_z, keep, rest):
    normed = rows_of((n0, n1, n2, n3))
    inner = jnp.concatenate([d_x[:, :chan], d_z[:, :chan]], axis=1)
    to_shares(place, keep, rest, 0, mm(normed, to_blocks(place, d_qkv[...]), TN))
    to_shares(place, keep, rest, cols.o, mm(rows_of((a0, a1, a2, a3)), heads[...], TN))
    to_shares(place, keep, rest, cols.s, mm(rows_of((s0, s1, s2, s3)), gated[:, :chan], TN))
    to_shares(place, keep, rest, cols.x, mm(normed, to_blocks(place, inner), TN))


def picker(rows, columns, start, valid):
    row = lax.broadcasted_iota(jnp.int32, (rows, columns), 0)
    col = lax.broadcasted_iota(jnp.int32, (rows, columns), 1)
    return ((row == start + col) & (col < valid)).astype(BF16)


def pack_mix_kernel(cols, chan, tensor_size, place, q, key, value, o, x, z, ssm, *packed):
    tensor_idx = place[1]
    for slow_idx in range(GROUP):

        @pl.when(place[0] == slow_idx)
        def _():
            for by in range(GROUP):
                s = (slow_idx + by) % GROUP
                unit = s * tensor_size + tensor_idx
                group = lax.div(unit, 3)
                sub = lax.rem(unit, 3)
                valid = jnp.where(group >= KVH, 0, jnp.where(sub == 2, HEAD, 2 * HEAD))
                heads = picker(q.shape[1], 2 * HEAD, group * GQ * HEAD + sub * 2 * HEAD, valid)
                both = picker(key.shape[1], HEAD, jnp.minimum(group, KVH - 1) * HEAD, HEAD)
                mine = slice(s * chan, (s + 1) * chan)
                packed[by][:, : cols.kv] = mm(q[...], heads).astype(BF16)
                packed[by][:, cols.kv : cols.o] = jnp.concatenate(
                    [mm(key[...], both), mm(value[...], both)], axis=1
                ).astype(BF16)
                packed[by][:, cols.o : cols.s] = mm(o[...], heads).astype(BF16)
                packed[by][:, cols.s : cols.x] = ssm[:, mine]
                packed[by][:, cols.x : cols.z] = x[:, mine]
                packed[by][:, cols.z :] = z[:, mine]


def pack_ffn_kernel(units, place, gate, up, down, *packed):
    for slow_idx in range(GROUP):

        @pl.when(place[0] == slow_idx)
        def _():
            for by in range(GROUP):
                s = (slow_idx + by) % GROUP
                mine = slice(s * units, (s + 1) * units)
                packed[by][:, :units] = gate[:, mine]
                packed[by][:, units : 2 * units] = up[:, mine]
                packed[by][:, 2 * units :] = down[:, mine]


def to_shares(place, keep, rest, start, values):
    share = keep.shape[1]
    fast = rest.shape[0] + 1
    values = values.astype(BF16)
    columns = slice(start, start + values.shape[1])
    for s in range(GROUP):
        by = lax.rem(s - place[0] + GROUP, GROUP)
        for f in range(fast):
            at = (s * fast + f) * share
            rows = values[at : at + share]
            turn = lax.rem(f - place[4] + fast, fast)

            @pl.when(turn == 0)
            def _():
                keep[by, :, columns] = rows

            @pl.when(turn > 0)
            def _():
                rest[turn - 1, by, :, columns] = rows


def unpack_mix_kernel(cols, chan, tensor_size, place, pieces, every, d_q, d_kv, d_o, d_ssm, d_in):
    slow_idx = place[0]

    def came(s):
        return lax.rem(slow_idx - s + GROUP, GROUP)

    for s in range(GROUP):
        mine = slice(s * chan, (s + 1) * chan)
        d_ssm[:, mine] = pieces[came(s), :, cols.s : cols.x].astype(F32)
        d_in[:, 0, mine] = pieces[came(s), :, cols.x : cols.z].astype(F32)
        d_in[:, 1, mine] = pieces[came(s), :, cols.z :].astype(F32)
    for group in range(KVH):
        total = 0.0
        for sub in range(3):
            unit = 3 * group + sub
            s, t = unit // tensor_size, unit % tensor_size
            piece = every[t, came(s)].astype(F32)
            start = group * GQ * HEAD + sub * 2 * HEAD
            width = HEAD if sub == 2 else 2 * HEAD
            d_q[:, start : start + width] = piece[:, :width]
            d_o[:, start : start + width] = piece[:, cols.o : cols.o + width]
            total = total + piece[:, cols.kv : cols.o]
        d_kv[:, 0, group * HEAD : (group + 1) * HEAD] = total[:, :HEAD]
        d_kv[:, 1, group * HEAD : (group + 1) * HEAD] = total[:, HEAD:]


def unpack_columns_kernel(width, place, pieces, pair, *single):
    slow_idx = place[0]
    for s in range(GROUP):
        came = lax.rem(slow_idx - s + GROUP, GROUP)
        mine = slice(s * width, (s + 1) * width)
        for k in range(2):
            pair[:, k, mine] = pieces[came, :, k * width : (k + 1) * width].astype(F32)
        for ref in single:
            ref[:, mine] = pieces[came, :, 2 * width :].astype(F32)


def small_weights_kernel(chan, wide, rank, place, conv_w, conv_b, step_b, dlog, skip, scan_w, step_w, vec, dlog_out, scan_out, step_out):
    layers = vec.shape[0]
    low = scan_w.shape[0] - 2 * dlog.shape[1]
    vec[...] = jnp.zeros(vec.shape, F32)
    dlog_out[...] = jnp.zeros(dlog_out.shape, F32)
    scan_out[...] = jnp.zeros(scan_out.shape, BF16)
    step_out[...] = jnp.zeros(step_out.shape, BF16)
    for s in range(GROUP):

        @pl.when(place[0] == s)
        def _():
            mine = slice(s * chan, (s + 1) * chan)
            for layer in range(layers):
                vec[layer, :CONV, :chan] = conv_w[layer, :, mine]
                vec[layer, CONV : CONV + 1, :chan] = conv_b[layer : layer + 1, mine]
                vec[layer, CONV + 1 : CONV + 2, :chan] = step_b[layer : layer + 1, mine]
                vec[layer, CONV + 2 : CONV + 3, :chan] = skip[layer : layer + 1, mine]
                dlog_out[layer, :, :chan] = dlog[layer, :, mine]
                scan_out[layer, :low, :chan] = scan_w[:low, layer, mine]
                scan_out[layer, rank:, :chan] = scan_w[low:, layer, mine]
                step_out[layer, :low, :chan] = step_w[:, layer, mine]


def ffn_forward_kernel(units, f0, f1, f2, f3, w, hidden, p0, p1, p2, p3):
    both = mm(rows_of((f0, f1, f2, f3)), w[:, : 2 * units])
    hidden[...] = both
    gate = both[:, :units]
    activ = (gate * sigmoid(gate) * both[:, units:]).astype(BF16)
    to_parts((p0, p1, p2, p3), mm(activ, w[:, 2 * units :], NT))


def ffn_backward_kernel(units, d0, d1, d2, d3, hidden, w, d_hidden, activ, p0, p1, p2, p3):
    d_activ = mm(rows_of((d0, d1, d2, d3)), w[:, 2 * units :])
    gate = hidden[:, :units]
    up = hidden[:, units:]
    sig = sigmoid(gate)
    swish = gate * sig
    activ[...] = (swish * up).astype(BF16)
    low = jnp.concatenate(
        [d_activ * up * (sig * (1.0 + gate * (1.0 - sig))), d_activ * swish], axis=1
    ).astype(BF16)
    d_hidden[...] = low
    to_parts((p0, p1, p2, p3), mm(low, w[:, : 2 * units], NT))


def ffn_weights_kernel(units, place, f0, f1, f2, f3, d0, d1, d2, d3, d_hidden, activ, keep, rest):
    to_shares(place, keep, rest, 0, mm(rows_of((f0, f1, f2, f3)), d_hidden[...], TN))
    to_shares(place, keep, rest, 2 * units, mm(rows_of((d0, d1, d2, d3)), activ[...], TN))


def rms_scale(values, gain_vec):
    return (
        values * lax.rsqrt(jnp.mean(values * values, axis=-1, keepdims=True) + EPSILON) * gain_vec
    )


def mix_branches(resid_in, attn_out, ssm_out, gain_attn, gain_ssm, gain_ffn):
    residual = resid_in + 0.5 * (rms_scale(attn_out, gain_attn) + rms_scale(ssm_out, gain_ssm))
    return (residual, rms_scale(residual, gain_ffn))


def per_device(
    dp_size,
    tensor_size,
    hidden_in,
    out_grad,
    lengths,
    norm_gains,
    q_weight,
    kv_weight,
    o_weight,
    in_weight,
    conv_weight,
    conv_bias,
    step_bias,
    decay_log,
    skip_gain,
    scan_weight,
    step_weight,
    ssm_weight,
    gate_weight,
    down_weight,
):
    layers = q_weight.shape[0]
    batches, _, length, width = hidden_in.shape
    fast = dp_size // GROUP
    share = width // dp_size
    chan = in_weight.shape[3] // GROUP
    wide = -(-chan // LANES) * LANES
    units = gate_weight.shape[3] // GROUP
    rank_true = step_weight.shape[1]
    state = decay_log.shape[2]
    rank = -(-rank_true // 16) * 16
    proj_rows = rank + 2 * state
    cols = Mix(chan)
    ffn_cols = 3 * units
    dp_idx = lax.axis_index("dp")
    slow_idx = dp_idx // fast
    fast_idx = dp_idx % fast
    tensor_idx = lax.axis_index("tensor")
    rows_here = batches * length // tensor_size
    seqs = GROUP * batches
    tokens = seqs * length
    half = tensor_size // 2

    def slow_perm(by):
        return [
            (s * fast + f, ((s + by) % GROUP) * fast + f) for s in range(GROUP) for f in range(fast)
        ]

    def fast_perm(by):
        return [
            (s * fast + f, s * fast + (f + by) % fast) for s in range(GROUP) for f in range(fast)
        ]

    core_perm = [(t, t ^ 1) for t in range(tensor_size)]
    chip_perm = [(t, t ^ 2) for t in range(tensor_size)]
    core_idx = tensor_idx % 2
    chip_idx = tensor_idx // 2

    def slow(values, by):
        return lax.ppermute(values, "dp", slow_perm(by)) if by % GROUP else values

    def other_fast(values, by):
        return lax.ppermute(values, "dp", fast_perm(by)) if by % fast else values

    def add_low(*terms):
        total = terms[0].astype(F32)
        for term in terms[1:]:
            total = total + term.astype(F32)
        return total.astype(BF16)

    def after(values, *earlier):
        return lax.optimization_barrier((values,) + earlier)[0] if earlier else values

    def gather_tokens(own):
        mine = jnp.concatenate([slow(own, by) for by in range(GROUP)], axis=0)
        chip = lax.ppermute(mine, "tensor", chip_perm)
        core = lax.ppermute(mine, "tensor", core_perm)
        return [mine, chip, core, lax.ppermute(chip, "tensor", core_perm)]

    def joined(values, done):
        values, done = tuple(values), tuple(done)
        return list(lax.optimization_barrier(values + done)[: len(values)]) if done else list(values)

    def scatter_near(parts):
        far = add_low(parts[1], lax.ppermute(parts[3], "tensor", core_perm))
        near = add_low(parts[0], lax.ppermute(parts[2], "tensor", core_perm))
        return add_low(near, lax.ppermute(far, "tensor", chip_perm))

    def scatter_far(total):
        total = total.reshape(GROUP, rows_here, width)
        result = total[0].astype(F32)
        for by in range(1, GROUP):
            result = result + slow(total[by], GROUP - by).astype(F32)
        return result

    def sum_group(values):
        values = add_low(values, lax.ppermute(values, "tensor", core_perm))
        values = add_low(values, lax.ppermute(values, "tensor", chip_perm))
        chunk = tokens // GROUP
        parts = [values[:, k * chunk : (k + 1) * chunk] for k in range(GROUP)]
        total = add_low(parts[0], *[slow(parts[by], GROUP - by) for by in range(1, GROUP)])
        return jnp.concatenate([slow(total, by) for by in range(GROUP)], axis=1)

    place = jnp.stack([slow_idx, tensor_idx, chip_idx, core_idx, fast_idx]).astype(jnp.int32)

    middle = share // 16 * 8
    one, three, two = (1, 0, share), (3, 0, share), (2, 0, share)
    two_a, two_b = (2, 0, middle), (2, middle, share)

    def send(pieces, unit, *ties):
        by, low, high = unit
        return slow(after(pieces[by][low:high], *ties), by)

    class Fetched:
        def __init__(self, own):
            self.full = jnp.zeros((GROUP, fast, share, own.shape[1]), BF16)
            self.add((0, 0, share), own)

        def add(self, unit, piece):
            by, low, _ = unit
            for turn in range(fast):
                self.full = lax.dynamic_update_slice(
                    self.full,
                    other_fast(piece, turn)[None, None],
                    ((slow_idx - by) % GROUP, (fast_idx - turn) % fast, low, 0),
                )

        def whole(self):
            return self.full.reshape(width, self.full.shape[3])

    def rows_round(own, units_in, tie):
        columns = own.shape[1]
        half = jnp.zeros((GROUP, share, columns), BF16)
        for (by, low, _), piece in [((0, 0, share), own)] + list(units_in.items()):
            half = lax.dynamic_update_slice(half, piece[None], ((slow_idx - by) % GROUP, low, 0))
        moved = [half] + [other_fast(half, turn) for turn in range(1, fast)]
        moved = joined(moved, [tie])
        if fast == 2:
            first, second = moved
            full = jnp.where(
                fast_idx == 0, jnp.stack([first, second], 1), jnp.stack([second, first], 1)
            )
        else:
            full = jnp.zeros((GROUP, fast, share, columns), BF16)
            for turn, rows in enumerate(moved):
                full = lax.dynamic_update_slice(
                    full, rows[:, None], (0, (fast_idx - turn) % fast, 0, 0)
                )
        return full.reshape(width, columns)

    def shares_out(columns):
        return [
            out((GROUP, share, columns), BF16),
            out((fast - 1, GROUP, share, columns), BF16),
        ]

    def settle_fast(keep, rest):
        return add_low(keep, *[other_fast(rest[turn - 1], turn) for turn in range(1, fast)])

    def stacked(rows, units_in, tie):
        two_rows = units_in[two] if two in units_in else None
        if two_rows is None:
            two_rows = jnp.concatenate([units_in[two_a], units_in[two_b]], axis=0)
        pieces = [rows[0], units_in[one], two_rows, units_in[three]]
        return jnp.stack(joined(pieces, [] if tie is None else [tie]))

    o_turned = o_weight.swapaxes(1, 2)
    ssm_turned = ssm_weight.swapaxes(1, 2)
    down_turned = down_weight.swapaxes(1, 2)

    def pack_mix(layer, place):
        inner = in_weight[layer]
        both = kv_weight[layer]
        packed = call(
            functools.partial(pack_mix_kernel, cols, chan, tensor_size),
            [out((share, cols.end), BF16)] * GROUP,
            [q_weight, both[:, 0], both[:, 1], o_turned, inner[:, 0], inner[:, 1], ssm_turned],
            5,
            place=place,
            layers=(layer, None, None, layer, None, None, layer),
        )
        return packed

    def pack_ffn(layer, place):
        gate = gate_weight[layer]
        packed = call(
            functools.partial(pack_ffn_kernel, units),
            [out((share, ffn_cols), BF16)] * GROUP,
            [gate[:, 0], gate[:, 1], down_turned],
            3,
            place=place,
            layers=(None, None, layer),
        )
        return packed

    vecs, dlogs, scan_mats, step_mats = call(
        functools.partial(small_weights_kernel, chan, wide, rank),
        [
            out((layers, 8, wide), F32),
            out((layers, state, wide), F32),
            out((layers, proj_rows, wide), BF16),
            out((layers, rank, wide), BF16),
        ],
        [
            conv_weight,
            conv_bias,
            step_bias,
            decay_log.swapaxes(1, 2),
            skip_gain,
            scan_weight.transpose(2, 0, 1),
            step_weight.swapaxes(0, 1),
        ],
        2,
        place=place,
    )

    bf_rows = lambda columns: out((tokens, columns), BF16)
    f_rows = lambda columns: out((tokens, columns), F32)
    tiled = pltpu.VMEM((wide // LANES, tokens, LANES), F32)
    state_tiled = pltpu.VMEM((length, state, seqs, LANES), F32)
    scan_scratch = [
        tiled,
        tiled,
        state_tiled,
        state_tiled,
        pltpu.VMEM((state, seqs, wide), F32),
        tiled,
    ]

    def own_rows(values):
        flat = values.reshape(batches * length, width)
        return lax.dynamic_slice_in_dim(flat, tensor_idx * rows_here, rows_here, 0)

    part_outs = [out((tokens // 4, width), BF16)] * 4
    token = tensor_idx * rows_here + jnp.arange(rows_here)
    mask = (token % length < lengths[token // length, 0]).astype(F32)[:, None]
    grad_run = own_rows(out_grad).astype(F32) * mask
    part_outs = [out((tokens // 4, width), BF16)] * 4
    running = own_rows(hidden_in).astype(F32)
    kept = []
    fetched = []
    own = pack_mix(0, place)
    first = {unit: send(own, unit) for unit in (one, three)}
    first[two] = send(own, two, first[one])
    mix_packed = [own]
    ffn_packed = [pack_ffn(0, after(place, first[one]))]
    for layer in range(layers):
        final = layer + 1 == layers
        gains = norm_gains[layer]
        normed, pull_input = jax.vjp(rms_scale, running, gains[0])
        normed = normed.astype(BF16)
        ffn_own, ffn_in_units = ffn_packed[layer], {}
        if layer == 0:
            mix_got = Fetched(own[0])
            for unit, piece in first.items():
                mix_got.add(unit, piece)
            n = gather_tokens(after(normed, own[0]))
            mix_w = after(mix_got.whole(), ffn_own[0])
            with_first, with_scan = (one, three), (two,)
        else:
            n = gather_tokens(normed)
            ffn_in_units[one] = send(ffn_own, one, n[0])
            mix_w = after(mix_got.whole(), ffn_in_units[one])
            with_first, with_scan = (three,), (two,)
        ready = joined(n, [mix_w])
        for unit in with_first:
            ffn_in_units[unit] = send(ffn_own, unit, first[two] if layer == 0 else ready[0])
        xi, z, conv, qkv, heads, proj_part, *attn_parts = call(
            functools.partial(mix_forward_kernel, cols, chan, wide, length),
            [
                f_rows(wide),
                f_rows(wide),
                bf_rows(wide),
                bf_rows(cols.o),
                bf_rows(2 * HEAD),
                out((proj_rows, tokens), BF16),
            ]
            + part_outs,
            ready + [mix_w, vecs, scan_mats],
            7,
            place=place,
            layers=(None,) * 5 + (layer, layer),
        )
        proj_part = after(proj_part, *[ffn_in_units[unit] for unit in with_first])
        proj = sum_group(proj_part)
        if not final:
            mix_packed.append(pack_mix(layer + 1, after(place, proj_part)))
            ffn_packed.append(pack_ffn(layer + 1, after(place, proj_part)))
            proj = after(proj, mix_packed[-1][0], ffn_packed[-1][0])
        for unit in with_scan:
            ffn_in_units[unit] = send(ffn_own, unit, proj)
        attn_total = scatter_near(joined(attn_parts, [proj]))
        gated, *ssm_parts = call(
            functools.partial(
                scan_forward_kernel, cols, chan, wide, rank, state, seqs, length
            ),
            [bf_rows(wide)] + part_outs,
            [proj, conv, z, step_mats, vecs, dlogs, mix_w],
            11,
            scan_scratch,
            place=place,
            layers=(None,) * 3 + (layer,) * 3,
        )
        done = [ffn_in_units[unit] for unit in with_scan]
        ssm_parts = joined(ssm_parts, [attn_total] + done)
        attn_out = scatter_far(after(attn_total, ssm_parts[0]))
        ssm_out = scatter_far(scatter_near(ssm_parts))
        (residual, ffn_in), pull_mix = jax.vjp(
            mix_branches, running, attn_out, ssm_out, gains[1], gains[2], gains[3]
        )
        ffn_in = ffn_in.astype(BF16)
        f = gather_tokens(ffn_in)
        ffn_w = rows_round(ffn_own[0], ffn_in_units, ffn_in)
        fetched.append((mix_w, ffn_w))
        if final:
            d_out = gather_tokens(after(grad_run.astype(BF16), f[0]))
            ffn_w = after(ffn_w, d_out[0])
        else:
            own = mix_packed[layer + 1]
            mix_got = Fetched(own[0])
            unit_two = send(own, two, f[0])
            ffn_w = after(ffn_w, unit_two)
            mix_got.add(two, unit_two)
        ready = joined(f, [ffn_w])
        if not final:
            unit_one = send(own, one, ready[0])
        hidden, *ffn_parts = call(
            functools.partial(ffn_forward_kernel, units),
            [f_rows(2 * units)] + part_outs,
            ready + [ffn_w],
            7,
        )
        if not final:
            ffn_parts = joined(ffn_parts, [unit_one])
            mix_got.add(one, unit_one)
            unit_three = send(own, three, ffn_parts[0])
            total = after(scatter_near(ffn_parts), unit_three)
            mix_got.add(three, unit_three)
            running = residual + scatter_far(total)
        kept.append((n, pull_input, xi, z, conv, qkv, heads, proj, gated, pull_mix, f, hidden))

    def every_tensor(values):
        moved = lax.ppermute(values, "tensor", chip_perm)
        values = jnp.where(chip_idx == 0, jnp.stack([values, moved]), jnp.stack([moved, values]))
        moved = lax.ppermute(values, "tensor", core_perm)
        values = jnp.where(
            core_idx == 0, jnp.stack([values, moved], 1), jnp.stack([moved, values], 1)
        )
        return values.reshape((tensor_size,) + values.shape[2:])

    def every_fast(values):
        turned = jnp.stack([other_fast(values, turn) for turn in range(fast)])
        return [
            lax.dynamic_index_in_dim(turned, (fast_idx - source) % fast, 0, False)
            for source in range(fast)
        ]

    def every_slow(values):
        turned = jnp.stack([slow(values, by) for by in range(GROUP)])
        return [
            lax.dynamic_index_in_dim(turned, (slow_idx - source) % GROUP, 0, False)
            for source in range(GROUP)
        ]

    def rounded(values):
        return lax.optimization_barrier(values.astype(BF16))

    def all_rows(own, *ties):
        return every_tensor(after(rounded(own), *ties)).reshape(batches, 1, length, width)

    big = {"mix": None, "ffn": None}
    small_rows = []
    gain_grads = [None] * layers
    early_rows = late_rows = None

    def finish_mix(layer, rows, units_in, tie):
        pieces = stacked(rows, units_in, tie)
        every = every_tensor(pieces[:, :, : cols.s])
        big["mix"] = call_into(
            functools.partial(unpack_mix_kernel, cols, chan, tensor_size),
            layer,
            [
                out((layers, share, KVH * GQ * HEAD), F32),
                out((layers, share, 2, KVH * HEAD), F32),
                out((layers, share, KVH * GQ * HEAD), F32),
                out((layers, share, GROUP * chan), F32),
                out((layers, share, 2, GROUP * chan), F32),
            ],
            big["mix"],
            [pieces, every],
            place,
        )

    def finish_ffn(layer, rows, units_in, tie):
        big["ffn"] = call_into(
            functools.partial(unpack_columns_kernel, units),
            layer,
            [
                out((layers, share, 2, GROUP * units), F32),
                out((layers, share, GROUP * units), F32),
            ],
            big["ffn"],
            [stacked(rows, units_in, tie)],
            place,
        )

    def finish_small(rows):
        small = rounded(sum(p.astype(F32) for p in every_fast(rounded(rows))))
        return jnp.concatenate(every_slow(small), axis=2).astype(F32)

    above = None
    for layer in reversed(range(layers)):
        mix_w, ffn_w = fetched[layer]
        n, pull_input, xi, z, conv, qkv, heads, proj, gated, pull_mix, f, hidden = kept[layer]
        if above is not None:
            d_out = gather_tokens(grad_run.astype(BF16))
            mix_rows, ffn_above, ffn_above_units = above
            mix_units = {one: send(mix_rows, one, d_out[0])}
            ffn_w = after(ffn_w, mix_units[one])
        ready = joined(d_out, [ffn_w])
        if above is not None:
            mix_units[three] = send(mix_rows, three, ready[0])
        d_hidden, activ, *parts = call(
            functools.partial(ffn_backward_kernel, units),
            [bf_rows(2 * units), bf_rows(units)] + part_outs,
            ready + [hidden, ffn_w],
            7,
        )
        done = []
        if above is not None:
            parts = joined(parts, [mix_units[three]])
            mix_units[two] = send(mix_rows, two, parts[0])
            done = [mix_units[two]]
        d_ffn_w = call(
            functools.partial(ffn_weights_kernel, units),
            shares_out(ffn_cols),
            f + joined(d_out, [parts[0]]) + [d_hidden, activ],
            6,
            place=place,
        )
        total = after(scatter_near(parts), d_ffn_w[0], *done)
        d_ffn_in = scatter_far(total)
        ffn_rows = settle_fast(*d_ffn_w)
        if above is None:
            out_total = scatter_near(joined(ffn_parts, [total]))
            d_ffn_in = after(d_ffn_in, out_total)
        grad_resid, d_attn, d_ssm, d_gain_attn, d_gain_ssm, d_gain_ffn = pull_mix(
            (grad_run, d_ffn_in)
        )
        d_ssm = gather_tokens(d_ssm.astype(BF16))
        d_attn = gather_tokens(after(d_attn.astype(BF16), d_ssm[0]))
        if above is not None:
            finish_ffn(layer + 1, ffn_above, ffn_above_units, d_ssm[0])
        ready = joined(d_ssm, [d_attn[0], ffn_rows])
        ffn_units = {unit: send(ffn_rows, unit, ready[0]) for unit in (one, three, two_a)}
        d_proj, d_conv, d_z, small_scan, d_step_w = call(
            functools.partial(
                scan_backward_kernel, cols, chan, wide, rank, state, seqs, length
            ),
            [
                out((proj_rows, tokens), BF16),
                f_rows(wide),
                bf_rows(wide),
                out((8 + state, wide), F32),
                out((rank, wide), F32),
            ],
            ready + [proj, conv, z, step_mats, vecs, dlogs, mix_w],
            26,
            scan_scratch
            + [
                pltpu.VMEM((length, STATES_AT_ONCE * (wide // LANES), seqs, LANES), F32),
                tiled,
                tiled,
                tiled,
                state_tiled,
                state_tiled,
            ],
            place=place,
            layers=(None,) * 7 + (layer,) * 3,
        )
        d_proj = after(d_proj, *ffn_units.values(), *d_attn[1:3])
        (d_qkv,) = call(
            functools.partial(attend_backward_kernel, cols, length),
            [bf_rows(cols.o)],
            joined(d_attn, [d_proj]) + [mix_w, qkv],
            5,
            place=place,
        )
        d_proj = after(sum_group(d_proj), d_qkv)
        ffn_units[two_b] = send(ffn_rows, two_b, d_proj)
        d_x, *parts, d_scan_w, small_conv = call(
            functools.partial(mix_backward_kernel, cols, chan, length),
            [bf_rows(wide)] + part_outs + [out((proj_rows, wide), F32), out((8, wide), F32)],
            [d_proj, conv, xi, d_conv, d_z, d_qkv, mix_w, vecs, scan_mats],
            6,
            place=place,
            layers=(None,) * 7 + (layer, layer),
        )
        parts = joined(parts, [ffn_units[two_b]])
        d_mix_w = call(
            functools.partial(mix_weights_kernel, cols, chan),
            shares_out(cols.end),
            n + d_attn + d_ssm + [d_qkv, heads, gated, after(d_x, parts[0]), d_z],
            7,
            place=place,
        )
        done = [d_mix_w[0]]
        if above is None:
            running = residual + scatter_far(after(out_total, parts[0]))
            output = (running * mask).astype(BF16)
            done.append(output)
        total = after(scatter_near(parts), *done)
        d_normed = scatter_far(total)
        mix_rows = settle_fast(*d_mix_w)
        if above is not None:
            finish_mix(layer + 1, above[0], mix_units, total)
        grad_lower, d_gain_input = pull_input(d_normed)
        grad_run = grad_resid + grad_lower
        gain_grads[layer] = jnp.stack([d_gain_input, d_gain_attn, d_gain_ssm, d_gain_ffn])
        small = jnp.concatenate([small_scan, small_conv, d_step_w, d_scan_w], axis=0)[:, :chan]
        small_rows.append(small)
        above = (mix_rows, ffn_rows, ffn_units)

    output = all_rows(output, d_normed)
    mix_units = {unit: send(mix_rows, unit, d_normed) for unit in (one, two, three)}
    finish_ffn(0, ffn_rows, ffn_units, d_normed)
    small = finish_small(after(jnp.stack(small_rows[::-1]), grad_run))
    input_grad = all_rows(grad_run).astype(F32)
    finish_mix(0, mix_rows, mix_units, None)

    gains = jnp.sum(every_tensor(rounded(jnp.stack(gain_grads))).astype(F32), axis=0)
    gains = sum(p.astype(F32) for p in every_fast(rounded(gains)))
    grad_gains = sum(p.astype(F32) for p in every_slow(rounded(gains)))

    base = 8 + state
    grad_step_bias = small[:, 0]
    grad_skip = small[:, 1]
    grad_decay = small[:, 8:base].transpose(0, 2, 1)
    grad_conv_weight = small[:, base : base + CONV]
    grad_conv_bias = small[:, base + CONV]
    base = base + 8
    grad_step_weight = small[:, base : base + rank_true]
    base = base + rank
    scan_rows = jnp.concatenate(
        [small[:, base : base + rank_true], small[:, base + rank :]], axis=1
    )
    grad_scan = scan_rows.transpose(0, 2, 1)
    d_q, d_kv, d_o, d_ssm_w, d_in = big["mix"]
    d_gate, d_down = big["ffn"]
    return (
        output,
        input_grad,
        grad_gains,
        d_q,
        d_kv,
        d_o.swapaxes(1, 2),
        d_in,
        grad_conv_weight,
        grad_conv_bias,
        grad_step_bias,
        grad_decay,
        grad_skip,
        grad_scan,
        grad_step_weight,
        d_ssm_w.swapaxes(1, 2),
        d_gate,
        d_down.swapaxes(1, 2),
    )


def solution(mesh):
    return jax.shard_map(
        functools.partial(per_device, mesh.shape["dp"], mesh.shape["tensor"]),
        mesh=mesh,
        in_specs=(
            P(None, "dp", None, None),
            P(None, "dp", None, None),
            P(None, "dp"),
            P(),
            P(None, "dp", None),
            P(None, "dp", None, None),
            P(None, None, "dp"),
            P(None, "dp", None, "tensor"),
            P(None, None, "tensor"),
            P(None, "tensor"),
            P(None, "tensor"),
            P(None, "tensor", None),
            P(None, "tensor"),
            P(None, "tensor", None),
            P(None, None, "tensor"),
            P(None, "tensor", "dp"),
            P(None, "dp", None, "tensor"),
            P(None, "tensor", "dp"),
        ),
        out_specs=(
            P(None, "dp", None, None),
            P(None, "dp", None, None),
            P(),
            P(None, "dp", None),
            P(None, "dp", None, None),
            P(None, None, "dp"),
            P(None, "dp", None, "tensor"),
            P(None, None, "tensor"),
            P(None, "tensor"),
            P(None, "tensor"),
            P(None, "tensor", None),
            P(None, "tensor"),
            P(None, "tensor", None),
            P(None, None, "tensor"),
            P(None, "tensor", "dp"),
            P(None, "dp", None, "tensor"),
            P(None, "tensor", "dp"),
        ),
        check_vma=False,
    )
```

time: 1500 us -> 984 us (0.66)
  local copies, waits for them, and re-layouts: 196 us -> 45.2 us
  starting transfers between devices: 301 us -> 212 us
  waiting for transfers between devices: 537 us -> 452 us
  Pallas kernels: 292 us -> 220 us
  other arithmetic: 91.1 us -> 36.7 us
  blocking collectives: 53.6 us -> 0 us
  between operations: 18.9 us -> 3.49 us
    ppermute x33 -> x16, waiting for transfers between devices: 161 us -> 54.6 us  [other_fast(): return lax.ppermute(values, 'dp', fast_perm(by)) if by % fast else values]
    pallas_call x18 -> x27, Pallas kernels: 292 us -> 220 us  [the longest x23 197 us: call(): pl.pallas_call(kernel, out_shape=outs, grid=(1,) if layers else (), in_sp...]
    ppermute x111 -> x116, starting transfers between devices: 232 us -> 161 us  [slow(): return lax.ppermute(values, 'dp', slow_perm(by)) if by % GROUP else values]
    psum x1 -> x0, blocking collectives: 38.3 us -> none  [per_device(): lax.psum(jnp.stack(gain_grads).astype(BF16), ('dp', 'tensor')).astype(F32)]
    another operation x61 -> x12, other arithmetic: 39.8 us -> 4.14 us  [the longest x4 3.54 us: stacked(): return jnp.stack(joined(pieces, [] if tie is None else [tie]))]
    concatenate x31 -> x4, local copies, waits for them, and re-layouts: 34 us -> 0.71 us  [gather_tokens(): mine = jnp.concatenate([slow(own, by) for by in range(GROUP)], axis=0)]
    slice x34 -> x18, local copies, waits for them, and re-layouts: 33.8 us -> 4.51 us  [the longest x1 1.57 us: pack_ffn(): gate = gate_weight[layer]]
    ppermute x111 -> x116, waiting for transfers between devices: 257 us -> 285 us  [slow(): return lax.ppermute(values, 'dp', slow_perm(by)) if by % GROUP else values]
  transfers between devices with their start and end apart: 194 -> 210, of which waited for: 87 -> 112; matrix products, arithmetic and copies ran while one was open for 16% -> 6% of each run, Pallas kernels for 18% -> 21%
where the time goes in v2:
time: 984 us; the launch traced here: 969 us
  waiting for transfers between devices  452 us (46%)
  Pallas kernels  220 us (22%)
  starting transfers between devices  212 us (22%)
  local copies, waits for them, and re-layouts  45.2 us (5%)
  other arithmetic  36.7 us (4%)
    ppermute x116, waiting for transfers between devices, slow(): return lax.ppermute(values, 'dp', slow_perm(by)) if by % GROUP else values  285 us
    pallas_call x23, Pallas kernels, call(): pl.pallas_call(kernel, out_shape=outs, grid=(1,) if layers else (), in_sp...  197 us
    ppermute x116, starting transfers between devices, slow(): return lax.ppermute(values, 'dp', slow_perm(by)) if by % GROUP else values  161 us
    ppermute x16, waiting for transfers between devices, other_fast(): return lax.ppermute(values, 'dp', fast_perm(by)) if by % fast else values  54.6 us
    ppermute x10, waiting for transfers between devices, gather_tokens(): chip = lax.ppermute(mine, 'tensor', chip_perm)  48.2 us
    ppermute x10, waiting for transfers between devices, scatter_near(): return add_low(near, lax.ppermute(far, 'tensor', chip_perm))  26.5 us
    pallas_call x4, Pallas kernels, call_into(): pl.pallas_call(body, out_shape=outs, grid=(1,), in_specs=specs, out_specs...  23.3 us
  transfers between devices with their start and end apart: 210, of which 112 were waited for; matrix products, arithmetic and copies ran while one was open for 6% of the time, Pallas kernels for 21%

profile of v2, /device:TPU:0, one launch (start us, length us, event | category | flops | bytes accessed | tf_op | source)
XLA Modules:
  0.0 969.3 jit_solution(5731477028738393668)
XLA Ops:
  41.7 8.2 collective-permute-start.11
  57.3 9.9 %collective-permute-done.11 = bf16[200,984]{1,0:T(8,128)(2,1)S(1)} collective-permute-done((bf16[200,984]{1,0:T(8,128)(2,1)S(1)}, bf16[200,984]{1,0:T(8,128)(2,1)S(1)}, u32[]{:S(2)}, u32[]{:S(2)}) %collective-permute-start.11) | collective-permute-done | bytes 393632 | tf_op jit(solution)/shard_map/ppermute | solution.py:697
  71.3 9.2 collective-permute-done.12
  82.6 7.6 shard_map.308
  121.5 11.5 %shard_map.311 = (bf16[512,256]{1,0:T(8,128)(2,1)}, bf16[128,1600]{1,0:T(8,128)(2,1)}, bf16[128,1600]{1,0:T(8,128)(2,1)}, bf16[128,1600]{1,0:T(8,128)(2,1)}, bf16[128,1600]{1,0:T(8,128)(2,1)}) custom-call(s32[5]{0:T(128)} %stack.371.place.refs_0_, bf16[144,512]{1,0:T(8,128)(2,1)} %pad_maximum_fusion.20.proj, bf16[512,256]{1,0:T(8,128)(2,1)} %get-tuple-element.323.conv, ...), custom_call_target="tpu_custom_call" | custom-call | flops 11000000512 | bytes 1 | tf_op jit(solution)/shard_map/pallas_call | solution.py:58
  133.3 7.6 collective-permute-done.26
  188.2 7.7 collective-permute-done.39.f1
  208.3 7.1 shard_map.312
  225.3 7.7 collective-permute-done.58
  236.4 9.1 collective-permute-done.48
  279.6 7.3 collective-permute-done.62
  289.4 7.3 shard_map.313
  329.4 11.5 %shard_map.314 = (bf16[512,256]{1,0:T(8,128)(2,1)}, bf16[128,1600]{1,0:T(8,128)(2,1)}, bf16[128,1600]{1,0:T(8,128)(2,1)}, bf16[128,1600]{1,0:T(8,128)(2,1)}, bf16[128,1600]{1,0:T(8,128)(2,1)}) custom-call(s32[5]{0:T(128)} %stack.371.place.refs_0_, bf16[144,512]{1,0:T(8,128)(2,1)} %pad_maximum_fusion.21.proj, bf16[512,256]{1,0:T(8,128)(2,1)} %get-tuple-element.379.conv, ...), custom_call_target="tpu_custom_call" | custom-call | flops 11000000512 | bytes 1 | tf_op jit(solution)/shard_map/pallas_call | solution.py:58
  341.2 8.8 collective-permute-done.75
  403.6 10.5 %collective-permute-done.88.f1 = bf16[128,1600]{1,0:T(8,128)(2,1)S(1)} collective-permute-done((bf16[128,1600]{1,0:T(8,128)(2,1)S(1)}, bf16[128,1600]{1,0:T(8,128)(2,1)S(1)}, u32[]{:S(2)}, u32[]{:S(2)}) %collective-permute-start.88) | collective-permute-done | bytes 409632 | tf_op jit(solution)/shard_map/ppermute | solution.py:713
  421.0 7.1 shard_map.315
  429.0 7.0 shard_map.316
  439.7 8.1 shard_map.317
  475.9 14.4 %collective-permute-done.116 = bf16[4,200,1032]{2,1,0:T(8,128)(2,1)S(1)} collective-permute-done((bf16[4,200,1032]{2,1,0:T(8,128)(2,1)}, bf16[4,200,1032]{2,1,0:T(8,128)(2,1)S(1)}, u32[]{:S(2)}, u32[]{:S(2)}) %collective-permute-start.116) | collective-permute-done | bytes 1651232 | tf_op jit(solution)/shard_map/ppermute | solution.py:700
  514.6 25.9 %shard_map.318 = (bf16[144,512]{1,0:T(8,128)(2,1)}, f32[512,256]{1,0:T(8,128)}, bf16[512,256]{1,0:T(8,128)(2,1)}, f32[24,256]{1,0:T(8,128)}, f32[112,256]{1,0:T(8,128)}) custom-call(s32[5]{0:T(128)} %stack.371.place.refs_0_, bf16[128,1600]{1,0:T(8,128)(2,1)} %copy-done.31, bf16[128,1600]{1,0:T(8,128)(2,1)} %copy-done.101, bf16[128,1600]{1,0:T(8,128)(2,1)} %copy-done.102, ...), custom_call_target="tpu_custom_call" | custom-call | flops 25999998976 | bytes 1 | tf_op jit(solution)/shard_map/pallas_call | solution.py:58
  581.1 9.8 %shard_map.321 = (bf16[4,200,984]{2,1,0:T(8,128)(2,1)}, bf16[1,4,200,984]{3,2,1,0:T(8,128)(2,1)}) custom-call(s32[5]{0:T(128)} %stack.371.place.refs_0_, bf16[128,1600]{1,0:T(8,128)(2,1)} %copy-done.29, bf16[128,1600]{1,0:T(8,128)(2,1)} %copy-done.95, bf16[128,1600]{1,0:T(8,128)(2,1)} %copy-done.96, bf16[128,1600]{1,0:T(8,128)(2,1)} %copy-done.97, ...), custom_call_target="tpu_custom_call" | custom-call | flops 7000000000 | bytes 1 | tf_op jit(solution)/shard_map/pallas_call | solution.py:58
  592.4 10.4 %collective-permute-done.137 = bf16[128,1600]{1,0:T(8,128)(2,1)S(1)} collective-permute-done((bf16[128,1600]{1,0:T(8,128)(2,1)S(1)}, bf16[128,1600]{1,0:T(8,128)(2,1)S(1)}, u32[]{:S(2)}, u32[]{:S(2)}) %collective-permute-start.137) | collective-permute-done | bytes 409632 | tf_op jit(solution)/shard_map/ppermute | solution.py:724
  629.4 9.9 %collective-permute-done.144.d1 = bf16[128,1600]{1,0:T(8,128)(2,1)S(1)} collective-permute-done((bf16[128,1600]{1,0:T(8,128)(2,1)S(1)}, bf16[128,1600]{1,0:T(8,128)(2,1)S(1)}, u32[]{:S(2)}, u32[]{:S(2)}) %collective-permute-start.144) | collective-permute-done | bytes 409632 | tf_op jit(solution)/shard_map/ppermute | solution.py:713
  647.6 10.1 %collective-permute-done.148 = bf16[200,984]{1,0:T(8,128)(2,1)S(1)} collective-permute-done((bf16[200,984]{1,0:T(8,128)(2,1)S(1)}, bf16[200,984]{1,0:T(8,128)(2,1)S(1)}, u32[]{:S(2)}, u32[]{:S(2)}) %collective-permute-start.148) | collective-permute-done | bytes 393632 | tf_op jit(solution)/shard_map/ppermute | solution.py:697
  658.7 7.1 shard_map.322
  671.0 8.1 shard_map.323
  726.2 8.6 collective-permute-done.160.g1.s1
  743.2 25.9 %shard_map.324 = (bf16[144,512]{1,0:T(8,128)(2,1)}, f32[512,256]{1,0:T(8,128)}, bf16[512,256]{1,0:T(8,128)(2,1)}, f32[24,256]{1,0:T(8,128)}, f32[112,256]{1,0:T(8,128)}) custom-call(s32[5]{0:T(128)} %stack.371.place.refs_0_, bf16[128,1600]{1,0:T(8,128)(2,1)} %copy-done.30, bf16[128,1600]{1,0:T(8,128)(2,1)} %copy-done.99, bf16[128,1600]{1,0:T(8,128)(2,1)} %copy-done.98, ...), custom_call_target="tpu_custom_call" | custom-call | flops 25999998976 | bytes 1 | tf_op jit(solution)/shard_map/pallas_call | solution.py:58
  812.0 9.8 %shard_map.327 = (bf16[4,200,984]{2,1,0:T(8,128)(2,1)}, bf16[1,4,200,984]{3,2,1,0:T(8,128)(2,1)}) custom-call(s32[5]{0:T(128)} %stack.371.place.refs_0_, bf16[128,1600]{1,0:T(8,128)(2,1)} %copy-done.65, bf16[128,1600]{1,0:T(8,128)(2,1)} %copy-done.91, bf16[128,1600]{1,0:T(8,128)(2,1)} %copy-done.90, bf16[128,1600]{1,0:T(8,128)(2,1)} %copy-done.92, ...), custom_call_target="tpu_custom_call" | custom-call | flops 7000000000 | bytes 1 | tf_op jit(solution)/shard_map/pallas_call | solution.py:58
  849.4 17.1 %collective-permute-done.194 = bf16[2,4,1600]{2,1,0:T(4,128)(2,1)S(1)} collective-permute-done((bf16[2,4,1600]{2,1,0:T(4,128)(2,1)S(1)}, bf16[2,4,1600]{2,1,0:T(4,128)(2,1)S(1)}, u32[]{:S(2)}, u32[]{:S(2)}) %collective-permute-start.194) | collective-permute-done | bytes 25632 | tf_op jit(solution)/shard_map/ppermute | solution.py:700
  890.8 31.5 %collective-permute-done.208 = bf16[2,288,200]{2,1,0:T(8,128)(2,1)S(1)} collective-permute-done((bf16[2,288,200]{2,1,0:T(8,128)(2,1)S(1)}, bf16[2,288,200]{2,1,0:T(8,128)(2,1)S(1)}, u32[]{:S(2)}, u32[]{:S(2)}) %collective-permute-start.208) | collective-permute-done | bytes 230432 | tf_op jit(solution)/shard_map/ppermute | solution.py:697
  923.5 7.5 collective-permute-done.200
  (902 shorter events, 616.6 us)
Async XLA Ops:
  15.1 24.9 %collective-permute-start.2 = (bf16[32,1600]{1,0:T(8,128)(2,1)S(1)}, bf16[32,1600]{1,0:T(8,128)(2,1)S(1)}, u32[]{:S(2)}, u32[]{:S(2)}) collective-permute-start(bf16[32,1600]{1,0:T(8,128)(2,1)S(1)} %fusion.9), channel_id=1, source_target_pairs={{0,24},{4,28},{8,0},{12,4},{16,8},{20,12},{24,16},{28,20},{1,25},{... | collective-permute-start | bytes 307208 | tf_op jit(solution)/shard_map/ppermute | solution.py:697
  21.1 30.2 %collective-permute-start.6 = (bf16[200,984]{1,0:T(8,128)(2,1)}, bf16[200,984]{1,0:T(8,128)(2,1)}, u32[]{:S(2)}, u32[]{:S(2)}) collective-permute-start(bf16[200,984]{1,0:T(8,128)(2,1)} %get-tuple-element.290), channel_id=1, source_target_pairs={{0,4},{4,0},{8,12},{12,8},{16,20},{20,16},{24,28},{28,24},{1,5},{5... | collective-permute-start | bytes 1180808 | tf_op jit(solution)/shard_map/ppermute | solution.py:700
  40.0 40.6 %collective-permute-start.4 = (bf16[128,1600]{1,0:T(8,128)(2,1)S(1)}, bf16[128,1600]{1,0:T(8,128)(2,1)S(1)}, u32[]{:S(2)}, u32[]{:S(2)}) collective-permute-start(bf16[128,1600]{1,0:T(8,128)(2,1)S(1)} %constant_dynamic-update-slice_fusion.n0), channel_id=1, source_target_pairs={{0,1},{1,0},{2,3},{3,2},{4,5},{5,4},{6,7},{7,6},{8,9},{9,8},{10,11... | collective-permute-start | bytes 1228808 | tf_op jit(solution)/shard_map/ppermute | solution.py:714
  41.7 25.5 %collective-permute-start.11 = (bf16[200,984]{1,0:T(8,128)(2,1)S(1)}, bf16[200,984]{1,0:T(8,128)(2,1)S(1)}, u32[]{:S(2)}, u32[]{:S(2)}) collective-permute-start(bf16[200,984]{1,0:T(8,128)(2,1)S(1)} %copy-done.123), channel_id=1, source_target_pairs={{0,16},{4,20},{8,24},{12,28},{16,0},{20,4},{24,8},{28,12},{1,17},{... | collective-permute-start | bytes 1180808 | tf_op jit(solution)/shard_map/ppermute | solution.py:697
  57.2 23.4 %collective-permute-start.5 = (bf16[128,1600]{1,0:T(8,128)(2,1)S(1)}, bf16[128,1600]{1,0:T(8,128)(2,1)S(1)}, u32[]{:S(2)}, u32[]{:S(2)}) collective-permute-start(bf16[128,1600]{1,0:T(8,128)(2,1)S(1)} %collective-permute-done.3.n1), channel_id=1, source_target_pairs={{0,1},{1,0},{2,3},{3,2},{4,5},{5,4},{6,7},{7,6},{8,9},{9,8},{10,11... | collective-permute-start | bytes 1228808 | tf_op jit(solution)/shard_map/ppermute | solution.py:715
  67.2 23.1 %collective-permute-start.14 = (bf16[200,1032]{1,0:T(8,128)(2,1)}, bf16[200,1032]{1,0:T(8,128)(2,1)S(1)}, u32[]{:S(2)}, u32[]{:S(2)}) collective-permute-start(bf16[200,1032]{1,0:T(8,128)(2,1)} %get-tuple-element.313), channel_id=1, source_target_pairs={{0,24},{4,28},{8,0},{12,4},{16,8},{20,12},{24,16},{28,20},{1,25},{... | collective-permute-start | bytes 1238408 | tf_op jit(solution)/shard_map/ppermute | solution.py:697
  146.7 41.5 %collective-permute-start.42 = (bf16[4,200,1032]{2,1,0:T(8,128)(2,1)S(1)}, bf16[4,200,1032]{2,1,0:T(8,128)(2,1)}, u32[]{:S(2)}, u32[]{:S(2)}) collective-permute-start(bf16[4,200,1032]{2,1,0:T(8,128)(2,1)S(1)} %bitcast_dynamic-update-slice_fusion.4), channel_id=1, source_target_pairs={{0,4},{4,0},{8,12},{12,8},{16,20},{20,16},{24,28},{28,24},{1,5},{5... | collective-permute-start | bytes 4953608 | tf_op jit(solution)/shard_map/ppermute | solution.py:700
  233.1 26.8 %collective-permute-start.59 = (bf16[200,984]{1,0:T(8,128)(2,1)S(1)}, bf16[200,984]{1,0:T(8,128)(2,1)S(1)}, u32[]{:S(2)}, u32[]{:S(2)}) collective-permute-start(bf16[200,984]{1,0:T(8,128)(2,1)S(1)} %collective-permute-done.43), channel_id=1, source_target_pairs={{0,4},{4,0},{8,12},{12,8},{16,20},{20,16},{24,28},{28,24},{1,5},{5... | collective-permute-start | bytes 1180808 | tf_op jit(solution)/shard_map/ppermute | solution.py:700
  355.4 48.2 %collective-permute-start.91 = (bf16[4,200,1032]{2,1,0:T(8,128)(2,1)S(1)}, bf16[4,200,1032]{2,1,0:T(8,128)(2,1)S(1)}, u32[]{:S(2)}, u32[]{:S(2)}) collective-permute-start(bf16[4,200,1032]{2,1,0:T(8,128)(2,1)S(1)} %bitcast_dynamic-update-slice_fusion), channel_id=1, source_target_pairs={{0,4},{4,0},{8,12},{12,8},{16,20},{20,16},{24,28},{28,24},{1,5},{5... | collective-permute-start | bytes 4953608 | tf_op jit(solution)/shard_map/ppermute | solution.py:700
  395.6 24.7 %collective-permute-start.89 = (bf16[128,1600]{1,0:T(8,128)(2,1)S(1)}, bf16[128,1600]{1,0:T(8,128)(2,1)S(1)}, u32[]{:S(2)}, u32[]{:S(2)}) collective-permute-start(bf16[128,1600]{1,0:T(8,128)(2,1)S(1)} %pad_maximum_fusion.10.f0), channel_id=1, source_target_pairs={{0,1},{1,0},{2,3},{3,2},{4,5},{5,4},{6,7},{7,6},{8,9},{9,8},{10,11... | collective-permute-start | bytes 1228808 | tf_op jit(solution)/shard_map/ppermute | solution.py:714
  402.5 25.6 %collective-permute-start.96 = (bf16[128,1600]{1,0:T(8,128)(2,1)S(1)}, bf16[128,1600]{1,0:T(8,128)(2,1)S(1)}, u32[]{:S(2)}, u32[]{:S(2)}) collective-permute-start(bf16[128,1600]{1,0:T(8,128)(2,1)S(1)} %constant_dynamic-update-slice_fusion.4.d0), channel_id=1, source_target_pairs={{0,1},{1,0},{2,3},{3,2},{4,5},{5,4},{6,7},{7,6},{8,9},{9,8},{10,11... | collective-permute-start | bytes 1228808 | tf_op jit(solution)/shard_map/ppermute | solution.py:714
  447.8 42.5 %collective-permute-start.116 = (bf16[4,200,1032]{2,1,0:T(8,128)(2,1)}, bf16[4,200,1032]{2,1,0:T(8,128)(2,1)S(1)}, u32[]{:S(2)}, u32[]{:S(2)}) collective-permute-start(bf16[4,200,1032]{2,1,0:T(8,128)(2,1)} %bitcast.345), channel_id=1, source_target_pairs={{0,4},{4,0},{8,12},{12,8},{16,20},{20,16},{24,28},{28,24},{1,5},{5... | collective-permute-start | bytes 4953608 | tf_op jit(solution)/shard_map/ppermute | solution.py:700
  507.6 32.9 %collective-permute-start.121 = (bf16[128,1600]{1,0:T(8,128)(2,1)S(1)}, bf16[128,1600]{1,0:T(8,128)(2,1)}, u32[]{:S(2)}, u32[]{:S(2)}) collective-permute-start(bf16[128,1600]{1,0:T(8,128)(2,1)S(1)} %constant_dynamic-update-slice_fusion.8.g0.a0), channel_id=1, source_target_pairs={{0,1},{1,0},{2,3},{3,2},{4,5},{5,4},{6,7},{7,6},{8,9},{9,8},{10,11... | collective-permute-start | bytes 1228808 | tf_op jit(solution)/shard_map/ppermute | solution.py:714
  508.2 32.3 %collective-permute-start.120 = (bf16[128,1600]{1,0:T(8,128)(2,1)S(1)}, bf16[128,1600]{1,0:T(8,128)(2,1)}, u32[]{:S(2)}, u32[]{:S(2)}) collective-permute-start(bf16[128,1600]{1,0:T(8,128)(2,1)S(1)} %constant_dynamic-update-slice_fusion.8.g0.a0), channel_id=1, source_target_pairs={{0,2},{1,3},{2,0},{3,1},{4,6},{5,7},{6,4},{7,5},{8,10},{9,11},{10,... | collective-permute-start | bytes 1228808 | tf_op jit(solution)/shard_map/ppermute | solution.py:713
  509.9 30.6 %collective-permute-start.119 = (bf16[96,1032]{1,0:T(8,128)(2,1)S(1)}, bf16[96,1032]{1,0:T(8,128)(2,1)S(1)}, u32[]{:S(2)}, u32[]{:S(2)}) collective-permute-start(bf16[96,1032]{1,0:T(8,128)(2,1)S(1)} %slice_bitcast_fusion.24), channel_id=1, source_target_pairs={{0,16},{4,20},{8,24},{12,28},{16,0},{20,4},{24,8},{28,12},{1,17},{... | collective-permute-start | bytes 594440 | tf_op jit(solution)/shard_map/ppermute | solution.py:697
  510.8 29.8 %collective-permute-start.117 = (bf16[200,1032]{1,0:T(8,128)(2,1)S(1)}, bf16[200,1032]{1,0:T(8,128)(2,1)S(1)}, u32[]{:S(2)}, u32[]{:S(2)}) collective-permute-start(bf16[200,1032]{1,0:T(8,128)(2,1)S(1)} %get-tuple-element.433), channel_id=1, source_target_pairs={{0,8},{4,12},{8,16},{12,20},{16,24},{20,28},{24,0},{28,4},{1,9},{5... | collective-permute-start | bytes 1238408 | tf_op jit(solution)/shard_map/ppermute | solution.py:697
  512.7 27.9 %collective-permute-start.118 = (bf16[200,1032]{1,0:T(8,128)(2,1)S(1)}, bf16[200,1032]{1,0:T(8,128)(2,1)S(1)}, u32[]{:S(2)}, u32[]{:S(2)}) collective-permute-start(bf16[200,1032]{1,0:T(8,128)(2,1)S(1)} %get-tuple-element.434), channel_id=1, source_target_pairs={{0,24},{4,28},{8,0},{12,4},{16,8},{20,12},{24,16},{28,20},{1,25},{... | collective-permute-start | bytes 1238408 | tf_op jit(solution)/shard_map/ppermute | solution.py:697
  608.3 36.3 %collective-permute-start.147 = (bf16[4,200,984]{2,1,0:T(8,128)(2,1)S(1)}, bf16[4,200,984]{2,1,0:T(8,128)(2,1)S(1)}, u32[]{:S(2)}, u32[]{:S(2)}) collective-permute-start(bf16[4,200,984]{2,1,0:T(8,128)(2,1)S(1)} %bitcast.347), channel_id=1, source_target_pairs={{0,4},{4,0},{8,12},{12,8},{16,20},{20,16},{24,28},{28,24},{1,5},{5... | collective-permute-start | bytes 4723208 | tf_op jit(solution)/shard_map/ppermute | solution.py:700
  629.4 28.3 %collective-permute-start.145 = (bf16[128,1600]{1,0:T(8,128)(2,1)S(1)}, bf16[128,1600]{1,0:T(8,128)(2,1)S(1)}, u32[]{:S(2)}, u32[]{:S(2)}) collective-permute-start(bf16[128,1600]{1,0:T(8,128)(2,1)S(1)} %pad_maximum_fusion.12.d0), channel_id=1, source_target_pairs={{0,1},{1,0},{2,3},{3,2},{4,5},{5,4},{6,7},{7,6},{8,9},{9,8},{10,11... | collective-permute-start | bytes 1228808 | tf_op jit(solution)/shard_map/ppermute | solution.py:714
  690.4 44.5 %collective-permute-start.166 = (bf16[4,200,1032]{2,1,0:T(8,128)(2,1)S(1)}, bf16[4,200,1032]{2,1,0:T(8,128)(2,1)S(1)}, u32[]{:S(2)}, u32[]{:S(2)}) collective-permute-start(bf16[4,200,1032]{2,1,0:T(8,128)(2,1)S(1)} %bitcast.344), channel_id=1, source_target_pairs={{0,4},{4,0},{8,12},{12,8},{16,20},{20,16},{24,28},{28,24},{1,5},{5... | collective-permute-start | bytes 4953608 | tf_op jit(solution)/shard_map/ppermute | solution.py:700
  725.4 43.7 %collective-permute-start.171 = (bf16[128,1600]{1,0:T(8,128)(2,1)}, bf16[128,1600]{1,0:T(8,128)(2,1)}, u32[]{:S(2)}, u32[]{:S(2)}) collective-permute-start(bf16[128,1600]{1,0:T(8,128)(2,1)} %constant_dynamic-update-slice_fusion.12.g0.a0), channel_id=1, source_target_pairs={{0,1},{1,0},{2,3},{3,2},{4,5},{5,4},{6,7},{7,6},{8,9},{9,8},{10,11... | collective-permute-start | bytes 1228808 | tf_op jit(solution)/shard_map/ppermute | solution.py:714
  725.4 43.7 %collective-permute-start.170 = (bf16[128,1600]{1,0:T(8,128)(2,1)}, bf16[128,1600]{1,0:T(8,128)(2,1)}, u32[]{:S(2)}, u32[]{:S(2)}) collective-permute-start(bf16[128,1600]{1,0:T(8,128)(2,1)} %constant_dynamic-update-slice_fusion.12.g0.a0), channel_id=1, source_target_pairs={{0,2},{1,3},{2,0},{3,1},{4,6},{5,7},{6,4},{7,5},{8,10},{9,11},{10,... | collective-permute-start | bytes 1228808 | tf_op jit(solution)/shard_map/ppermute | solution.py:713
  736.6 32.5 %collective-permute-start.169 = (bf16[96,1032]{1,0:T(8,128)(2,1)S(1)}, bf16[96,1032]{1,0:T(8,128)(2,1)S(1)}, u32[]{:S(2)}, u32[]{:S(2)}) collective-permute-start(bf16[96,1032]{1,0:T(8,128)(2,1)S(1)} %slice_bitcast_fusion.23), channel_id=1, source_target_pairs={{0,16},{4,20},{8,24},{12,28},{16,0},{20,4},{24,8},{28,12},{1,17},{... | collective-permute-start | bytes 594440 | tf_op jit(solution)/shard_map/ppermute | solution.py:697
  739.4 29.7 %collective-permute-start.167 = (bf16[200,1032]{1,0:T(8,128)(2,1)S(1)}, bf16[200,1032]{1,0:T(8,128)(2,1)S(1)}, u32[]{:S(2)}, u32[]{:S(2)}) collective-permute-start(bf16[200,1032]{1,0:T(8,128)(2,1)S(1)} %get-tuple-element.495), channel_id=1, source_target_pairs={{0,8},{4,12},{8,16},{12,20},{16,24},{20,28},{24,0},{28,4},{1,9},{5... | collective-permute-start | bytes 1238408 | tf_op jit(solution)/shard_map/ppermute | solution.py:697
  739.4 29.7 %collective-permute-start.168 = (bf16[200,1032]{1,0:T(8,128)(2,1)S(1)}, bf16[200,1032]{1,0:T(8,128)(2,1)S(1)}, u32[]{:S(2)}, u32[]{:S(2)}) collective-permute-start(bf16[200,1032]{1,0:T(8,128)(2,1)S(1)} %get-tuple-element.496), channel_id=1, source_target_pairs={{0,24},{4,28},{8,0},{12,4},{16,8},{20,12},{24,16},{28,20},{1,25},{... | collective-permute-start | bytes 1238408 | tf_op jit(solution)/shard_map/ppermute | solution.py:697
  821.8 58.0 %collective-permute-start.198 = (bf16[4,200,984]{2,1,0:T(8,128)(2,1)}, bf16[4,200,984]{2,1,0:T(8,128)(2,1)S(1)}, u32[]{:S(2)}, u32[]{:S(2)}) collective-permute-start(bf16[4,200,984]{2,1,0:T(8,128)(2,1)} %bitcast.346), channel_id=1, source_target_pairs={{0,4},{4,0},{8,12},{12,8},{16,20},{20,16},{24,28},{28,24},{1,5},{5... | collective-permute-start | bytes 4723208 | tf_op jit(solution)/shard_map/ppermute | solution.py:700
  839.5 36.8 %collective-permute-start.206 = (bf16[2,288,200]{2,1,0:T(8,128)(2,1)S(1)}, bf16[2,288,200]{2,1,0:T(8,128)(2,1)S(1)}, u32[]{:S(2)}, u32[]{:S(2)}) collective-permute-start(bf16[2,288,200]{2,1,0:T(8,128)(2,1)S(1)} %pad_maximum_fusion.5), channel_id=1, source_target_pairs={{0,4},{4,0},{8,12},{12,8},{16,20},{20,16},{24,28},{28,24},{1,5},{5... | collective-permute-start | bytes 691208 | tf_op jit(solution)/shard_map/ppermute | solution.py:700
  877.2 45.1 %collective-permute-start.208 = (bf16[2,288,200]{2,1,0:T(8,128)(2,1)S(1)}, bf16[2,288,200]{2,1,0:T(8,128)(2,1)S(1)}, u32[]{:S(2)}, u32[]{:S(2)}) collective-permute-start(bf16[2,288,200]{2,1,0:T(8,128)(2,1)S(1)} %fusion.2), channel_id=1, source_target_pairs={{0,16},{4,20},{8,24},{12,28},{16,0},{20,4},{24,8},{28,12},{1,17},{... | collective-permute-start | bytes 691208 | tf_op jit(solution)/shard_map/ppermute | solution.py:697
  877.8 45.3 %collective-permute-start.207 = (bf16[2,288,200]{2,1,0:T(8,128)(2,1)S(1)}, bf16[2,288,200]{2,1,0:T(8,128)(2,1)S(1)}, u32[]{:S(2)}, u32[]{:S(2)}) collective-permute-start(bf16[2,288,200]{2,1,0:T(8,128)(2,1)S(1)} %fusion.2), channel_id=1, source_target_pairs={{0,8},{4,12},{8,16},{12,20},{16,24},{20,28},{24,0},{28,4},{1,9},{5... | collective-permute-start | bytes 691208 | tf_op jit(solution)/shard_map/ppermute | solution.py:697
  880.7 42.8 %collective-permute-start.199 = (bf16[200,984]{1,0:T(8,128)(2,1)S(1)}, bf16[200,984]{1,0:T(8,128)(2,1)S(1)}, u32[]{:S(2)}, u32[]{:S(2)}) collective-permute-start(bf16[200,984]{1,0:T(8,128)(2,1)S(1)} %get-tuple-element.525), channel_id=1, source_target_pairs={{0,8},{4,12},{8,16},{12,20},{16,24},{20,28},{24,0},{28,4},{1,9},{5... | collective-permute-start | bytes 1180808 | tf_op jit(solution)/shard_map/ppermute | solution.py:697
  881.7 49.3 %collective-permute-start.200 = (bf16[200,984]{1,0:T(8,128)(2,1)S(1)}, bf16[200,984]{1,0:T(8,128)(2,1)S(1)}, u32[]{:S(2)}, u32[]{:S(2)}) collective-permute-start(bf16[200,984]{1,0:T(8,128)(2,1)S(1)} %get-tuple-element.526), channel_id=1, source_target_pairs={{0,16},{4,20},{8,24},{12,28},{16,0},{20,4},{24,8},{28,12},{1,17},{... | collective-permute-start | bytes 1180808 | tf_op jit(solution)/shard_map/ppermute | solution.py:697
  886.6 46.4 %collective-permute-start.201 = (bf16[200,984]{1,0:T(8,128)(2,1)S(1)}, bf16[200,984]{1,0:T(8,128)(2,1)S(1)}, u32[]{:S(2)}, u32[]{:S(2)}) collective-permute-start(bf16[200,984]{1,0:T(8,128)(2,1)S(1)} %get-tuple-element.527), channel_id=1, source_target_pairs={{0,24},{4,28},{8,0},{12,4},{16,8},{20,12},{24,16},{28,20},{1,25},{... | collective-permute-start | bytes 1180808 | tf_op jit(solution)/shard_map/ppermute | solution.py:697
  (304 other events, 3425.6 us)

commit v3 on v2

--- a/solution.py
+++ b/solution.py
@@ -290,7 +290,7 @@
         return tuple(fresh)
 
     zero = jnp.zeros((seqs, LANES), F32)
-    lax.fori_loop(0, length, step, (zero,) * (STATES_AT_ONCE * tiles))
+    lax.fori_loop(0, length, step, (zero,) * (STATES_AT_ONCE * tiles), unroll=4)
 
 
 def scan_forward_kernel(cols, chan, wide, rank, state, seqs, length, place, proj, conv, z, step_w, vec, dlog, w, gated, p0, p1, p2, p3, dt_s, dtx_s, drive_s, read_s, rate_s, y_s):
@@ -352,7 +352,7 @@
         return tuple(lams) + tuple(sums)
 
     zero = jnp.zeros((seqs, LANES), F32)
-    return lax.fori_loop(0, length, step, (zero,) * (2 * count))[count:]
+    return lax.fori_loop(0, length, step, (zero,) * (2 * count), unroll=4)[count:]
 
 
 def scan_backward_kernel(cols, chan, wide, rank, state, seqs, length, place, g0, g1, g2, g3, proj, conv, z, step_w, vec, dlog, w, d_proj, d_conv, d_z, small, d_step_w, dt_s, dtx_s, drive_s, read_s, rate_s, y_s, keep_s, ds_s, ddt_s, dsrc_s, pd_s, pr_s):
@@ -385,12 +385,15 @@
     d_z[...] = (d_gated * scanned * (sig * (1.0 + gate * (1.0 - sig)))).astype(BF16)
     d_pre = d_dt * sigmoid(pre)
     rates = -jnp.exp(dlog[...])
-    small[0:1] = jnp.sum(d_pre, axis=0, keepdims=True)
-    small[1:2] = jnp.sum(d_scanned * conv32, axis=0, keepdims=True)
-    small[2:8] = jnp.zeros((6, wide), F32)
-    small[8:] = jnp.concatenate(d_rates, axis=0) * rates
+    sums = [
+        jnp.sum(d_pre, axis=0, keepdims=True),
+        jnp.sum(d_scanned * conv32, axis=0, keepdims=True),
+        jnp.zeros((14, wide), F32),
+        jnp.concatenate(d_rates, axis=0) * rates,
+    ]
+    small[...] = jnp.concatenate(sums, axis=0).astype(BF16)
     low = d_pre.astype(BF16)
-    d_step_w[...] = mm(proj[:rank], low)
+    d_step_w[...] = mm(proj[:rank], low).astype(BF16)
     table = spread(state, state * LANES)
     tokens = seqs * length
     by_time = [
@@ -448,27 +451,29 @@
     sig = sigmoid(running)
     d_run = d_out * (sig * (1.0 + running * (1.0 - sig)))
     d_in = 0.0
+    sums = []
     for k in range(CONV):
         back = CONV - 1 - k
         d_in = d_in + shift_rows(d_run, -back, length) * taps[k : k + 1]
-        small[k : k + 1] = jnp.sum(d_run * shift_rows(inner_x, back, length), axis=0, keepdims=True)
-    small[CONV : CONV + 1] = jnp.sum(d_run, axis=0, keepdims=True)
-    small[CONV + 1 :] = jnp.zeros((8 - CONV - 1, inner_x.shape[1]), F32)
+        sums.append(jnp.sum(d_run * shift_rows(inner_x, back, length), axis=0, keepdims=True))
+    sums.append(jnp.sum(d_run, axis=0, keepdims=True))
+    sums.append(jnp.zeros((16 - CONV - 1, inner_x.shape[1]), F32))
+    small[...] = jnp.concatenate(sums, axis=0).astype(BF16)
     low = d_in.astype(BF16)
     d_x[...] = low
     inner = to_blocks(place, jnp.concatenate([low[:, :chan], d_z[:, :chan]], axis=1))
     heads = to_blocks(place, d_qkv[...])
     to_parts((p0, p1, p2, p3), mm(inner, w[:, cols.x :], NT) + mm(heads, w[:, : cols.o], NT))
-    d_scan_w[...] = mm(proj[...], conv[...])
-
-
-def mix_weights_kernel(cols, chan, place, n0, n1, n2, n3, a0, a1, a2, a3, s0, s1, s2, s3, d_qkv, heads, gated, d_x, d_z, keep, rest):
+    d_scan_w[...] = mm(proj[...], conv[...]).astype(BF16)
+
+
+def mix_weights_kernel(cols, chan, place, n0, n1, n2, n3, a0, a1, a2, a3, s0, s1, s2, s3, d_qkv, heads, gated, d_x, d_z, *outs):
     normed = rows_of((n0, n1, n2, n3))
     inner = jnp.concatenate([d_x[:, :chan], d_z[:, :chan]], axis=1)
-    to_shares(place, keep, rest, 0, mm(normed, to_blocks(place, d_qkv[...]), TN))
-    to_shares(place, keep, rest, cols.o, mm(rows_of((a0, a1, a2, a3)), heads[...], TN))
-    to_shares(place, keep, rest, cols.s, mm(rows_of((s0, s1, s2, s3)), gated[:, :chan], TN))
-    to_shares(place, keep, rest, cols.x, mm(normed, to_blocks(place, inner), TN))
+    to_shares(place, outs, 0, mm(normed, to_blocks(place, d_qkv[...]), TN))
+    to_shares(place, outs, cols.o, mm(rows_of((a0, a1, a2, a3)), heads[...], TN))
+    to_shares(place, outs, cols.s, mm(rows_of((s0, s1, s2, s3)), gated[:, :chan], TN))
+    to_shares(place, outs, cols.x, mm(normed, to_blocks(place, inner), TN))
 
 
 def picker(rows, columns, start, valid):
@@ -515,9 +520,10 @@
                 packed[by][:, 2 * units :] = down[:, mine]
 
 
-def to_shares(place, keep, rest, start, values):
+def to_shares(place, outs, start, values):
+    keep, odd, even = outs
     share = keep.shape[1]
-    fast = rest.shape[0] + 1
+    fast = odd.shape[0] + 1
     values = values.astype(BF16)
     columns = slice(start, start + values.shape[1])
     for s in range(GROUP):
@@ -531,35 +537,51 @@
             def _():
                 keep[by, :, columns] = rows
 
-            @pl.when(turn > 0)
+            @pl.when((turn > 0) & (lax.rem(by, 2) == 1))
             def _():
-                rest[turn - 1, by, :, columns] = rows
-
-
-def unpack_mix_kernel(cols, chan, tensor_size, place, pieces, every, d_q, d_kv, d_o, d_ssm, d_in):
+                odd[turn - 1, lax.div(by, 2), :, columns] = rows
+
+            @pl.when((turn > 0) & (lax.rem(by, 2) == 0))
+            def _():
+                even[turn - 1, 1 - lax.div(by, 2), :, columns] = rows
+
+
+def unpack_heads_kernel(cols, tensor_size, place, *refs):
+    blocks, (d_q, d_kv, d_o) = (refs[:4], refs[4:8]), refs[8:]
     slow_idx = place[0]
-
-    def came(s):
-        return lax.rem(slow_idx - s + GROUP, GROUP)
-
+    for tensor_idx in range(tensor_size):
+
+        @pl.when(place[1] == tensor_idx)
+        def _():
+            for group in range(KVH):
+                total = 0.0
+                for sub in range(3):
+                    unit = 3 * group + sub
+                    s, t = unit // tensor_size, unit % tensor_size
+                    by = lax.rem(slow_idx - s + GROUP, GROUP)
+                    at = lax.div(by, 2)
+                    apart = t ^ tensor_idx
+                    block = apart // 2 + 2 * (apart % 2)
+                    piece = jnp.where(
+                        lax.rem(by, 2) == 0, blocks[0][block][at], blocks[1][block][at]
+                    ).astype(F32)
+                    start = group * GQ * HEAD + sub * 2 * HEAD
+                    width = HEAD if sub == 2 else 2 * HEAD
+                    d_q[:, start : start + width] = piece[:, :width]
+                    d_o[:, start : start + width] = piece[:, cols.o : cols.o + width]
+                    total = total + piece[:, cols.kv : cols.o]
+                d_kv[:, 0, group * HEAD : (group + 1) * HEAD] = total[:, :HEAD]
+                d_kv[:, 1, group * HEAD : (group + 1) * HEAD] = total[:, HEAD:]
+
+
+def unpack_channels_kernel(cols, chan, place, pieces, d_ssm, d_in):
+    slow_idx = place[0]
     for s in range(GROUP):
+        came = lax.rem(slow_idx - s + GROUP, GROUP)
         mine = slice(s * chan, (s + 1) * chan)
-        d_ssm[:, mine] = pieces[came(s), :, cols.s : cols.x].astype(F32)
-        d_in[:, 0, mine] = pieces[came(s), :, cols.x : cols.z].astype(F32)
-        d_in[:, 1, mine] = pieces[came(s), :, cols.z :].astype(F32)
-    for group in range(KVH):
-        total = 0.0
-        for sub in range(3):
-            unit = 3 * group + sub
-            s, t = unit // tensor_size, unit % tensor_size
-            piece = every[t, came(s)].astype(F32)
-            start = group * GQ * HEAD + sub * 2 * HEAD
-            width = HEAD if sub == 2 else 2 * HEAD
-            d_q[:, start : start + width] = piece[:, :width]
-            d_o[:, start : start + width] = piece[:, cols.o : cols.o + width]
-            total = total + piece[:, cols.kv : cols.o]
-        d_kv[:, 0, group * HEAD : (group + 1) * HEAD] = total[:, :HEAD]
-        d_kv[:, 1, group * HEAD : (group + 1) * HEAD] = total[:, HEAD:]
+        d_ssm[:, mine] = pieces[came, :, cols.s : cols.x].astype(F32)
+        d_in[:, 0, mine] = pieces[came, :, cols.x : cols.z].astype(F32)
+        d_in[:, 1, mine] = pieces[came, :, cols.z :].astype(F32)
 
 
 def unpack_columns_kernel(width, place, pieces, pair, *single):
@@ -571,6 +593,31 @@
             pair[:, k, mine] = pieces[came, :, k * width : (k + 1) * width].astype(F32)
         for ref in single:
             ref[:, mine] = pieces[came, :, 2 * width :].astype(F32)
+
+
+def small_grads_kernel(chan, rank, state, place, shared, conv_w, conv_b, step_b, dlog, skip, scan_w, step_w):
+    low = step_w.shape[0]
+    layers = conv_w.shape[0]
+    per = 2 * 16 + state + 2 * rank + 2 * state
+    for layer in range(layers):
+        for s in range(GROUP):
+            mine = slice(s * chan, (s + 1) * chan)
+
+            def rows(start, count):
+                at = layer * per + start
+                return shared[s, at : at + count].astype(F32)
+
+            step_b[layer : layer + 1, mine] = rows(0, 1)
+            skip[layer : layer + 1, mine] = rows(1, 1)
+            dlog[layer, :, mine] = rows(16, state)
+            base = 16 + state
+            conv_w[layer, :, mine] = rows(base, CONV)
+            conv_b[layer : layer + 1, mine] = rows(base + CONV, 1)
+            base = base + 16
+            step_w[:, layer, mine] = rows(base, low)
+            base = base + rank
+            scan_w[:low, layer, mine] = rows(base, low)
+            scan_w[low:, layer, mine] = rows(base + rank, 2 * state)
 
 
 def small_weights_kernel(chan, wide, rank, place, conv_w, conv_b, step_b, dlog, skip, scan_w, step_w, vec, dlog_out, scan_out, step_out):
@@ -618,9 +665,9 @@
     to_parts((p0, p1, p2, p3), mm(low, w[:, : 2 * units], NT))
 
 
-def ffn_weights_kernel(units, place, f0, f1, f2, f3, d0, d1, d2, d3, d_hidden, activ, keep, rest):
-    to_shares(place, keep, rest, 0, mm(rows_of((f0, f1, f2, f3)), d_hidden[...], TN))
-    to_shares(place, keep, rest, 2 * units, mm(rows_of((d0, d1, d2, d3)), activ[...], TN))
+def ffn_weights_kernel(units, place, f0, f1, f2, f3, d0, d1, d2, d3, d_hidden, activ, *outs):
+    to_shares(place, outs, 0, mm(rows_of((f0, f1, f2, f3)), d_hidden[...], TN))
+    to_shares(place, outs, 2 * units, mm(rows_of((d0, d1, d2, d3)), activ[...], TN))
 
 
 def rms_scale(values, gain_vec):
@@ -708,18 +755,26 @@
     def after(values, *earlier):
         return lax.optimization_barrier((values,) + earlier)[0] if earlier else values
 
-    def gather_tokens(own):
-        mine = jnp.concatenate([slow(own, by) for by in range(GROUP)], axis=0)
-        chip = lax.ppermute(mine, "tensor", chip_perm)
-        core = lax.ppermute(mine, "tensor", core_perm)
-        return [mine, chip, core, lax.ppermute(chip, "tensor", core_perm)]
+    def gather_far(own):
+        return jnp.concatenate([slow(own, by) for by in range(GROUP)], axis=0)
 
     def joined(values, done):
         values, done = tuple(values), tuple(done)
         return list(lax.optimization_barrier(values + done)[: len(values)]) if done else list(values)
 
-    def scatter_near(parts):
-        far = add_low(parts[1], lax.ppermute(parts[3], "tensor", core_perm))
+    def gather_near(mine, work=()):
+        chip = after(lax.ppermute(mine, "tensor", chip_perm), *work)
+        core = lax.ppermute(mine, "tensor", core_perm)
+        return [mine, chip, core, lax.ppermute(chip, "tensor", core_perm)]
+
+    def gather_tokens(own):
+        return gather_near(gather_far(own))
+
+    def scatter_core(parts):
+        return add_low(parts[1], lax.ppermute(parts[3], "tensor", core_perm))
+
+    def scatter_near(parts, far=None):
+        far = scatter_core(parts) if far is None else far
         near = add_low(parts[0], lax.ppermute(parts[2], "tensor", core_perm))
         return add_low(near, lax.ppermute(far, "tensor", chip_perm))
 
@@ -730,13 +785,23 @@
             result = result + slow(total[by], GROUP - by).astype(F32)
         return result
 
-    def sum_group(values):
-        values = add_low(values, lax.ppermute(values, "tensor", core_perm))
-        values = add_low(values, lax.ppermute(values, "tensor", chip_perm))
+    def sum_near(values):
+        halves = values.reshape(2, values.shape[0] // 2, tokens)
+        mine = lax.dynamic_index_in_dim(halves, core_idx, 0, False)
+        theirs = lax.dynamic_index_in_dim(halves, 1 - core_idx, 0, False)
+        mine = add_low(mine, lax.ppermute(theirs, "tensor", core_perm))
+        return add_low(mine, lax.ppermute(mine, "tensor", chip_perm))
+
+    def sum_far(mine):
         chunk = tokens // GROUP
-        parts = [values[:, k * chunk : (k + 1) * chunk] for k in range(GROUP)]
-        total = add_low(parts[0], *[slow(parts[by], GROUP - by) for by in range(1, GROUP)])
-        return jnp.concatenate([slow(total, by) for by in range(GROUP)], axis=1)
+        terms = [mine] + [slow(mine, by) for by in range(1, GROUP)]
+        mine = add_low(*[jnp.roll(term, by * chunk, axis=1) for by, term in enumerate(terms)])
+        theirs = lax.ppermute(mine, "tensor", core_perm)
+        return jnp.where(
+            core_idx == 0,
+            jnp.concatenate([mine, theirs], axis=0),
+            jnp.concatenate([theirs, mine], axis=0),
+        )
 
     place = jnp.stack([slow_idx, tensor_idx, chip_idx, core_idx, fast_idx]).astype(jnp.int32)
 
@@ -786,20 +851,24 @@
         return full.reshape(width, columns)
 
     def shares_out(columns):
-        return [
-            out((GROUP, share, columns), BF16),
-            out((fast - 1, GROUP, share, columns), BF16),
-        ]
-
-    def settle_fast(keep, rest):
-        return add_low(keep, *[other_fast(rest[turn - 1], turn) for turn in range(1, fast)])
+        some = out((fast - 1, 2, share, columns), BF16)
+        return [out((GROUP, share, columns), BF16), some, some]
+
+    def go_round(some, *ties):
+        some = after(some, *ties)
+        return [other_fast(some[turn - 1], turn) for turn in range(1, fast)]
+
+    def add_round(keep, moved, pieces):
+        return {by: add_low(keep[by], *[m[k] for m in moved]) for k, by in enumerate(pieces)}
+
+    def all_pieces(rows, units_in, tie):
+        names = (one, three) + ((two,) if two in units_in else (two_a, two_b))
+        own, first, third, *second = joined([rows[0]] + [units_in[unit] for unit in names], [tie])
+        second = second[0] if len(second) == 1 else jnp.concatenate(second, axis=0)
+        return own, first, second, third
 
     def stacked(rows, units_in, tie):
-        two_rows = units_in[two] if two in units_in else None
-        if two_rows is None:
-            two_rows = jnp.concatenate([units_in[two_a], units_in[two_b]], axis=0)
-        pieces = [rows[0], units_in[one], two_rows, units_in[three]]
-        return jnp.stack(joined(pieces, [] if tie is None else [tie]))
+        return jnp.stack(all_pieces(rows, units_in, tie))
 
     o_turned = o_weight.swapaxes(1, 2)
     ssm_turned = ssm_weight.swapaxes(1, 2)
@@ -878,9 +947,13 @@
     fetched = []
     own = pack_mix(0, place)
     first = {unit: send(own, unit) for unit in (one, three)}
-    first[two] = send(own, two, first[one])
+    first[two] = send(own, two, first[one], first[three])
     mix_packed = [own]
     ffn_packed = [pack_ffn(0, after(place, first[one]))]
+    place_later = after(place, first[one], first[three])
+    for layer in range(1, layers):
+        mix_packed.append(pack_mix(layer, place_later))
+        ffn_packed.append(pack_ffn(layer, place_later))
     for layer in range(layers):
         final = layer + 1 == layers
         gains = norm_gains[layer]
@@ -891,17 +964,17 @@
             mix_got = Fetched(own[0])
             for unit, piece in first.items():
                 mix_got.add(unit, piece)
-            n = gather_tokens(after(normed, own[0]))
-            mix_w = after(mix_got.whole(), ffn_own[0])
-            with_first, with_scan = (one, three), (two,)
+            n = gather_tokens(normed)
+            mix_w = after(mix_got.whole(), *[p[0] for p in mix_packed[1:] + ffn_packed])
         else:
             n = gather_tokens(normed)
-            ffn_in_units[one] = send(ffn_own, one, n[0])
+            for unit in (one, three):
+                ffn_in_units[unit] = send(ffn_own, unit, n[0])
             mix_w = after(mix_got.whole(), ffn_in_units[one])
-            with_first, with_scan = (three,), (two,)
         ready = joined(n, [mix_w])
-        for unit in with_first:
-            ffn_in_units[unit] = send(ffn_own, unit, first[two] if layer == 0 else ready[0])
+        if layer == 0:
+            for unit in (one, three):
+                ffn_in_units[unit] = send(ffn_own, unit, first[two])
         xi, z, conv, qkv, heads, proj_part, *attn_parts = call(
             functools.partial(mix_forward_kernel, cols, chan, wide, length),
             [
@@ -918,14 +991,10 @@
             place=place,
             layers=(None,) * 5 + (layer, layer),
         )
-        proj_part = after(proj_part, *[ffn_in_units[unit] for unit in with_first])
-        proj = sum_group(proj_part)
-        if not final:
-            mix_packed.append(pack_mix(layer + 1, after(place, proj_part)))
-            ffn_packed.append(pack_ffn(layer + 1, after(place, proj_part)))
-            proj = after(proj, mix_packed[-1][0], ffn_packed[-1][0])
-        for unit in with_scan:
-            ffn_in_units[unit] = send(ffn_own, unit, proj)
+        proj_part = after(proj_part, ffn_in_units[one], ffn_in_units[three])
+        ffn_in_units[two_a] = send(ffn_own, two_a, proj_part)
+        proj = sum_far(after(sum_near(proj_part), ffn_in_units[two_a]))
+        ffn_in_units[two_b] = send(ffn_own, two_b, proj)
         attn_total = scatter_near(joined(attn_parts, [proj]))
         gated, *ssm_parts = call(
             functools.partial(
@@ -938,8 +1007,7 @@
             place=place,
             layers=(None,) * 3 + (layer,) * 3,
         )
-        done = [ffn_in_units[unit] for unit in with_scan]
-        ssm_parts = joined(ssm_parts, [attn_total] + done)
+        ssm_parts = joined(ssm_parts, [attn_total, ffn_in_units[two_b]])
         attn_out = scatter_far(after(attn_total, ssm_parts[0]))
         ssm_out = scatter_far(scatter_near(ssm_parts))
         (residual, ffn_in), pull_mix = jax.vjp(
@@ -950,7 +1018,7 @@
         ffn_w = rows_round(ffn_own[0], ffn_in_units, ffn_in)
         fetched.append((mix_w, ffn_w))
         if final:
-            d_out = gather_tokens(after(grad_run.astype(BF16), f[0]))
+            d_out = gather_tokens(after(grad_run.astype(BF16), f[2]))
             ffn_w = after(ffn_w, d_out[0])
         else:
             own = mix_packed[layer + 1]
@@ -985,6 +1053,11 @@
         )
         return values.reshape((tensor_size,) + values.shape[2:])
 
+    def tensor_blocks(mine):
+        chip = lax.ppermute(mine, "tensor", chip_perm)
+        core = lax.ppermute(mine, "tensor", core_perm)
+        return [mine, chip, core, lax.ppermute(chip, "tensor", core_perm)]
+
     def every_fast(values):
         turned = jnp.stack([other_fast(values, turn) for turn in range(fast)])
         return [
@@ -1005,26 +1078,37 @@
     def all_rows(own, *ties):
         return every_tensor(after(rounded(own), *ties)).reshape(batches, 1, length, width)
 
-    big = {"mix": None, "ffn": None}
+    big = {"heads": None, "mix": None, "ffn": None}
     small_rows = []
     gain_grads = [None] * layers
     early_rows = late_rows = None
 
     def finish_mix(layer, rows, units_in, tie):
-        pieces = stacked(rows, units_in, tie)
-        every = every_tensor(pieces[:, :, : cols.s])
-        big["mix"] = call_into(
-            functools.partial(unpack_mix_kernel, cols, chan, tensor_size),
+        own, first, second, third = all_pieces(rows, units_in, tie)
+        blocks = []
+        for pair in ((own, second), (first, third)):
+            blocks += tensor_blocks(jnp.stack([p[:, : cols.s] for p in pair]))
+        big["heads"] = call_into(
+            functools.partial(unpack_heads_kernel, cols, tensor_size),
             layer,
             [
                 out((layers, share, KVH * GQ * HEAD), F32),
                 out((layers, share, 2, KVH * HEAD), F32),
                 out((layers, share, KVH * GQ * HEAD), F32),
+            ],
+            big["heads"],
+            blocks,
+            place,
+        )
+        big["mix"] = call_into(
+            functools.partial(unpack_channels_kernel, cols, chan),
+            layer,
+            [
                 out((layers, share, GROUP * chan), F32),
                 out((layers, share, 2, GROUP * chan), F32),
             ],
             big["mix"],
-            [pieces, every],
+            [stacked(rows, units_in, tie)],
             place,
         )
 
@@ -1041,9 +1125,13 @@
             place,
         )
 
-    def finish_small(rows):
-        small = rounded(sum(p.astype(F32) for p in every_fast(rounded(rows))))
-        return jnp.concatenate(every_slow(small), axis=2).astype(F32)
+    def small_near(rows):
+        parts = rows.reshape(fast, rows.shape[0] // fast, chan)
+        terms = []
+        for turn in range(fast):
+            part = lax.dynamic_index_in_dim(parts, (fast_idx + turn) % fast, 0, False)
+            terms.append(other_fast(part, turn).astype(F32))
+        return rounded(sum(terms))
 
     above = None
     for layer in reversed(range(layers)):
@@ -1052,11 +1140,12 @@
         if above is not None:
             d_out = gather_tokens(grad_run.astype(BF16))
             mix_rows, ffn_above, ffn_above_units = above
-            mix_units = {one: send(mix_rows, one, d_out[0])}
-            ffn_w = after(ffn_w, mix_units[one])
+            running = residual + scatter_far(after(out_total, d_out[0]))
+            output = (running * mask).astype(BF16)
+            ffn_w = after(ffn_w, output)
         ready = joined(d_out, [ffn_w])
         if above is not None:
-            mix_units[three] = send(mix_rows, three, ready[0])
+            mix_units = {one: send(mix_rows, one, ready[0])}
         d_hidden, activ, *parts = call(
             functools.partial(ffn_backward_kernel, units),
             [bf_rows(2 * units), bf_rows(units)] + part_outs,
@@ -1065,31 +1154,45 @@
         )
         done = []
         if above is not None:
-            parts = joined(parts, [mix_units[three]])
-            mix_units[two] = send(mix_rows, two, parts[0])
-            done = [mix_units[two]]
+            parts = joined(parts, [mix_units[one]])
+            mix_units[three] = send(mix_rows, three, parts[0])
+            done = [mix_units[three]]
+        far = scatter_core(parts)
         d_ffn_w = call(
             functools.partial(ffn_weights_kernel, units),
             shares_out(ffn_cols),
-            f + joined(d_out, [parts[0]]) + [d_hidden, activ],
+            f + joined(d_out, [far]) + [d_hidden, activ],
             6,
             place=place,
         )
-        total = after(scatter_near(parts), d_ffn_w[0], *done)
+        total = after(scatter_near(parts, far), d_ffn_w[0], *done)
         d_ffn_in = scatter_far(total)
-        ffn_rows = settle_fast(*d_ffn_w)
         if above is None:
             out_total = scatter_near(joined(ffn_parts, [total]))
             d_ffn_in = after(d_ffn_in, out_total)
         grad_resid, d_attn, d_ssm, d_gain_attn, d_gain_ssm, d_gain_ffn = pull_mix(
             (grad_run, d_ffn_in)
         )
-        d_ssm = gather_tokens(d_ssm.astype(BF16))
-        d_attn = gather_tokens(after(d_attn.astype(BF16), d_ssm[0]))
+        moved = go_round(d_ffn_w[1])
+        d_ssm = gather_far(d_ssm.astype(BF16))
+        work = ()
         if above is not None:
-            finish_ffn(layer + 1, ffn_above, ffn_above_units, d_ssm[0])
-        ready = joined(d_ssm, [d_attn[0], ffn_rows])
-        ffn_units = {unit: send(ffn_rows, unit, ready[0]) for unit in (one, three, two_a)}
+            finish_ffn(layer + 1, ffn_above, ffn_above_units, d_ssm)
+            work = (big["ffn"][1],)
+        d_ssm = gather_near(d_ssm, work)
+        d_attn = gather_far(after(d_attn.astype(BF16), d_ssm[0]))
+        done = [d_attn]
+        ffn_rows = add_round(after(d_ffn_w[0], d_ssm[0]), moved, (1, 3))
+        ffn_even = go_round(d_ffn_w[2], ffn_rows[1])
+        ready = joined(d_ssm, done + list(ffn_rows.values()))
+        d_attn = gather_near(after(d_attn, ready[0]))
+        ffn_units = {one: send(ffn_rows, one, ready[0])}
+        done = []
+        if above is None:
+            ffn_units[three] = send(ffn_rows, three, ready[0])
+        else:
+            mix_units[two] = send(mix_rows, two, ready[0])
+            done = [mix_units[two]]
         d_proj, d_conv, d_z, small_scan, d_step_w = call(
             functools.partial(
                 scan_backward_kernel, cols, chan, wide, rank, state, seqs, length
@@ -1098,8 +1201,8 @@
                 out((proj_rows, tokens), BF16),
                 f_rows(wide),
                 bf_rows(wide),
-                out((8 + state, wide), F32),
-                out((rank, wide), F32),
+                out((16 + state, wide), BF16),
+                out((rank, wide), BF16),
             ],
             ready + [proj, conv, z, step_mats, vecs, dlogs, mix_w],
             26,
@@ -1115,7 +1218,8 @@
             place=place,
             layers=(None,) * 7 + (layer,) * 3,
         )
-        d_proj = after(d_proj, *ffn_units.values(), *d_attn[1:3])
+        d_proj = after(d_proj, *ffn_units.values(), *done, *ffn_even, *d_attn[1:3])
+        ffn_rows.update(add_round(after(d_ffn_w[0], d_proj), ffn_even, (2, 0)))
         (d_qkv,) = call(
             functools.partial(attend_backward_kernel, cols, length),
             [bf_rows(cols.o)],
@@ -1123,34 +1227,39 @@
             5,
             place=place,
         )
-        d_proj = after(sum_group(d_proj), d_qkv)
-        ffn_units[two_b] = send(ffn_rows, two_b, d_proj)
+        d_proj = sum_far(after(sum_near(d_proj), d_qkv))
+        beside = two_a if above is None else three
+        ffn_units[beside] = send(ffn_rows, beside, d_proj)
         d_x, *parts, d_scan_w, small_conv = call(
             functools.partial(mix_backward_kernel, cols, chan, length),
-            [bf_rows(wide)] + part_outs + [out((proj_rows, wide), F32), out((8, wide), F32)],
+            [bf_rows(wide)] + part_outs + [out((proj_rows, wide), BF16), out((16, wide), BF16)],
             [d_proj, conv, xi, d_conv, d_z, d_qkv, mix_w, vecs, scan_mats],
             6,
             place=place,
             layers=(None,) * 7 + (layer, layer),
         )
-        parts = joined(parts, [ffn_units[two_b]])
+        parts = joined(parts, [ffn_units[beside]])
+        beside = two_b if above is None else two_a
+        ffn_units[beside] = send(ffn_rows, beside, parts[0])
+        done = [ffn_units[beside]]
+        far = scatter_core(parts)
         d_mix_w = call(
             functools.partial(mix_weights_kernel, cols, chan),
             shares_out(cols.end),
-            n + d_attn + d_ssm + [d_qkv, heads, gated, after(d_x, parts[0]), d_z],
+            n + d_attn + d_ssm + [d_qkv, heads, gated, after(d_x, far), d_z],
             7,
             place=place,
         )
-        done = [d_mix_w[0]]
-        if above is None:
-            running = residual + scatter_far(after(out_total, parts[0]))
-            output = (running * mask).astype(BF16)
-            done.append(output)
-        total = after(scatter_near(parts), *done)
+        done.append(d_mix_w[0])
+        total = after(scatter_near(parts, far), *done)
         d_normed = scatter_far(total)
-        mix_rows = settle_fast(*d_mix_w)
+        keep, odd, even = d_mix_w
+        mix_rows = add_round(keep, go_round(odd), (1, 3))
+        d_normed = after(d_normed, mix_rows[1], mix_rows[3])
+        moved = go_round(even, mix_rows[1])
+        mix_rows.update(add_round(after(keep, d_normed), moved, (2, 0)))
         if above is not None:
-            finish_mix(layer + 1, above[0], mix_units, total)
+            above_mix = above[0], mix_units
         grad_lower, d_gain_input = pull_input(d_normed)
         grad_run = grad_resid + grad_lower
         gain_grads[layer] = jnp.stack([d_gain_input, d_gain_attn, d_gain_ssm, d_gain_ffn])
@@ -1158,31 +1267,57 @@
         small_rows.append(small)
         above = (mix_rows, ffn_rows, ffn_units)
 
-    output = all_rows(output, d_normed)
-    mix_units = {unit: send(mix_rows, unit, d_normed) for unit in (one, two, three)}
-    finish_ffn(0, ffn_rows, ffn_units, d_normed)
-    small = finish_small(after(jnp.stack(small_rows[::-1]), grad_run))
-    input_grad = all_rows(grad_run).astype(F32)
-    finish_mix(0, mix_rows, mix_units, None)
-
+    mix_units = {unit: send(mix_rows, unit) for unit in (one, three)}
     gains = jnp.sum(every_tensor(rounded(jnp.stack(gain_grads))).astype(F32), axis=0)
-    gains = sum(p.astype(F32) for p in every_fast(rounded(gains)))
-    grad_gains = sum(p.astype(F32) for p in every_slow(rounded(gains)))
-
-    base = 8 + state
-    grad_step_bias = small[:, 0]
-    grad_skip = small[:, 1]
-    grad_decay = small[:, 8:base].transpose(0, 2, 1)
-    grad_conv_weight = small[:, base : base + CONV]
-    grad_conv_bias = small[:, base + CONV]
-    base = base + 8
-    grad_step_weight = small[:, base : base + rank_true]
-    base = base + rank
-    scan_rows = jnp.concatenate(
-        [small[:, base : base + rank_true], small[:, base + rank :]], axis=1
+    gains = after(gains, *mix_units.values(), mix_rows[2], mix_rows[0])
+    small_count = layers * small_rows[0].shape[0]
+    small = jnp.concatenate(small_rows[::-1] + [rounded(gains).reshape(-1, chan)], axis=0)
+    extra = -small.shape[0] % (8 * fast)
+    mix_units[two] = send(mix_rows, two, gains)
+    small = small_near(jnp.pad(small, ((0, extra), (0, 0))))
+    small = after(small, mix_units[two])
+    for unit in (one, three, two_a, two_b):
+        if unit not in ffn_units:
+            ffn_units[unit] = send(ffn_rows, unit, small)
+    if layers > 1:
+        finish_mix(1, *above_mix, small)
+    output = all_rows(output, small)
+    input_grad = all_rows(grad_run, small).astype(F32)
+    finish_mix(0, mix_rows, mix_units, small)
+    small = jnp.stack(every_slow(small))
+    finish_ffn(0, ffn_rows, ffn_units, small)
+    shared = jnp.concatenate(every_fast(small), axis=1)
+    grad_gains = jnp.sum(
+        shared[:, small_count : shared.shape[1] - extra].astype(F32), axis=0
+    ).reshape(norm_gains.shape)
+    (
+        grad_conv_weight,
+        grad_conv_bias,
+        grad_step_bias,
+        grad_decay,
+        grad_skip,
+        grad_scan,
+        grad_step_weight,
+    ) = call(
+        functools.partial(small_grads_kernel, chan, rank, state),
+        [
+            out(conv_weight.shape, F32),
+            out(conv_bias.shape, F32),
+            out(step_bias.shape, F32),
+            out((layers, state, GROUP * chan), F32),
+            out(skip_gain.shape, F32),
+            out((rank_true + 2 * state, layers, GROUP * chan), F32),
+            out((rank_true, layers, GROUP * chan), F32),
+        ],
+        [shared],
+        4,
+        place=place,
     )
-    grad_scan = scan_rows.transpose(0, 2, 1)
-    d_q, d_kv, d_o, d_ssm_w, d_in = big["mix"]
+    grad_decay = grad_decay.swapaxes(1, 2)
+    grad_scan = grad_scan.transpose(1, 2, 0)
+    grad_step_weight = grad_step_weight.swapaxes(0, 1)
+    d_q, d_kv, d_o = big["heads"]
+    d_ssm_w, d_in = big["mix"]
     d_gate, d_down = big["ffn"]
     return (
         output,

time: 984 us -> 919 us (0.934)
  waiting for transfers between devices: 452 us -> 415 us
  starting transfers between devices: 212 us -> 181 us
  other arithmetic: 36.7 us -> 47.9 us
    ppermute x116 -> x103, starting transfers between devices: 161 us -> 121 us  [slow(): return lax.ppermute(values, 'dp', slow_perm(by)) if by % GROUP else values]
    ppermute x116 -> x103, waiting for transfers between devices: 285 us -> 254 us  [slow(): return lax.ppermute(values, 'dp', slow_perm(by)) if by % GROUP else values]
    unnamed x269 -> x278, local copies, waits for them, and re-layouts: 19.1 us -> 8.67 us
    ppermute x48 -> x64, starting transfers between devices: 18.2 us -> 26.5 us  [the longest x10 12 us: gather_near(): chip = after(lax.ppermute(mine, 'tensor', chip_perm), *work)]
    ppermute x16 -> x20, waiting for transfers between devices: 54.6 us -> 61.1 us  [other_fast(): return lax.ppermute(values, 'dp', fast_perm(by)) if by % fast else values]
    pallas_call x4 -> x6, Pallas kernels: 23.3 us -> 27.1 us  [call_into(): pl.pallas_call(body, out_shape=outs, grid=(1,), in_specs=specs, out_specs...]
    pallas_call x23 -> x24, Pallas kernels: 197 us -> 194 us  [call(): pl.pallas_call(kernel, out_shape=outs, grid=(1,) if layers else (), in_sp...]
    ppermute x48 -> x64, waiting for transfers between devices: 76 us -> 74.9 us  [the longest x10 41.5 us: gather_near(): chip = after(lax.ppermute(mine, 'tensor', chip_perm), *work)]
  transfers between devices with their start and end apart: 210 -> 213, of which waited for: 112 -> 116; matrix products, arithmetic and copies ran while one was open for 6% -> 7% of each run, Pallas kernels for 21% -> 22%
where the time goes in v3:
time: 919 us; the launch traced here: 911 us
  waiting for transfers between devices  415 us (45%)
  Pallas kernels  221 us (24%)
  starting transfers between devices  181 us (20%)
  other arithmetic  47.9 us (5%)
  local copies, waits for them, and re-layouts  42 us (5%)
    ppermute x103, waiting for transfers between devices, slow(): return lax.ppermute(values, 'dp', slow_perm(by)) if by % GROUP else values  254 us
    pallas_call x24, Pallas kernels, call(): pl.pallas_call(kernel, out_shape=outs, grid=(1,) if layers else (), in_sp...  194 us
    ppermute x103, starting transfers between devices, slow(): return lax.ppermute(values, 'dp', slow_perm(by)) if by % GROUP else values  121 us
    ppermute x20, waiting for transfers between devices, other_fast(): return lax.ppermute(values, 'dp', fast_perm(by)) if by % fast else values  61.1 us
    ppermute x10, waiting for transfers between devices, gather_near(): chip = after(lax.ppermute(mine, 'tensor', chip_perm), *work)  41.5 us
    pallas_call x6, Pallas kernels, call_into(): pl.pallas_call(body, out_shape=outs, grid=(1,), in_specs=specs, out_specs...  27.1 us
    ppermute x10, waiting for transfers between devices, scatter_near(): return add_low(near, lax.ppermute(far, 'tensor', chip_perm))  21.2 us
    ppermute x20, starting transfers between devices, other_fast(): return lax.ppermute(values, 'dp', fast_perm(by)) if by % fast else values  19.5 us
  transfers between devices with their start and end apart: 213, of which 116 were waited for; matrix products, arithmetic and copies ran while one was open for 7% of the time, Pallas kernels for 22%

profile of v3, /device:TPU:0, one launch (start us, length us, event | category | flops | bytes accessed | tf_op | source)
XLA Modules:
  0.0 911.0 jit_solution(4050262892809033281)
XLA Ops:
  15.8 6.0 shard_map.305
  69.3 9.2 %collective-permute-done.12 = bf16[200,984]{1,0:T(8,128)(2,1)S(1)} collective-permute-done((bf16[200,984]{1,0:T(8,128)(2,1)S(1)}, bf16[200,984]{1,0:T(8,128)(2,1)S(1)}, u32[]{:S(2)}, u32[]{:S(2)}) %collective-permute-start.12) | collective-permute-done | bytes 393632 | tf_op jit(solution)/shard_map/ppermute | solution.py:747
  80.3 7.6 shard_map.310
  96.0 11.6 %collective-permute-done.17 = bf16[96,1032]{1,0:T(8,128)(2,1)S(1)} collective-permute-done((bf16[96,1032]{1,0:T(8,128)(2,1)S(1)}, bf16[96,1032]{1,0:T(8,128)(2,1)S(1)}, u32[]{:S(2)}, u32[]{:S(2)}) %collective-permute-start.17) | collective-permute-done | bytes 198176 | tf_op jit(solution)/shard_map/ppermute | solution.py:744
  121.8 9.8 %shard_map.311 = (bf16[512,256]{1,0:T(8,128)(2,1)}, bf16[128,1600]{1,0:T(8,128)(2,1)}, bf16[128,1600]{1,0:T(8,128)(2,1)}, bf16[128,1600]{1,0:T(8,128)(2,1)}, bf16[128,1600]{1,0:T(8,128)(2,1)}) custom-call(s32[5]{0:T(128)} %stack.316.place.refs_0_, bf16[144,512]{1,0:T(8,128)(2,1)} %maximum_select_fusion.7.proj, bf16[512,256]{1,0:T(8,128)(2,1)} %get-tuple-element.358.conv, ...), custom_call_target="tpu_custom_call" | custom-call | flops 11000000512 | bytes 1 | tf_op jit(solution)/shard_map/pallas_call | solution.py:58
  181.1 6.0 collective-permute-done.38.f1
  191.7 6.1 collective-permute-done.42
  198.7 7.1 shard_map.312
  216.5 6.7 collective-permute-done.57
  226.5 9.1 collective-permute-done.47
  277.6 7.3 shard_map.313
  294.2 10.6 %collective-permute-done.65 = bf16[96,1032]{1,0:T(8,128)(2,1)S(1)} collective-permute-done((bf16[96,1032]{1,0:T(8,128)(2,1)S(1)}, bf16[96,1032]{1,0:T(8,128)(2,1)S(1)}, u32[]{:S(2)}, u32[]{:S(2)}) %collective-permute-start.65) | collective-permute-done | bytes 198176 | tf_op jit(solution)/shard_map/ppermute | solution.py:744
  318.3 9.9 %shard_map.314 = (bf16[512,256]{1,0:T(8,128)(2,1)}, bf16[128,1600]{1,0:T(8,128)(2,1)}, bf16[128,1600]{1,0:T(8,128)(2,1)}, bf16[128,1600]{1,0:T(8,128)(2,1)}, bf16[128,1600]{1,0:T(8,128)(2,1)}) custom-call(s32[5]{0:T(128)} %stack.316.place.refs_0_, bf16[144,512]{1,0:T(8,128)(2,1)} %maximum_select_fusion.8.proj, bf16[512,256]{1,0:T(8,128)(2,1)} %get-tuple-element.416.conv, ...), custom_call_target="tpu_custom_call" | custom-call | flops 11000000512 | bytes 1 | tf_op jit(solution)/shard_map/pallas_call | solution.py:58
  394.7 6.0 collective-permute-done.93.d1
  400.7 7.1 shard_map.315
  408.8 7.0 shard_map.316
  420.3 8.4 shard_map.317
  484.3 23.5 %shard_map.318 = (bf16[144,512]{1,0:T(8,128)(2,1)}, f32[512,256]{1,0:T(8,128)}, bf16[512,256]{1,0:T(8,128)(2,1)}, bf16[32,256]{1,0:T(8,128)(2,1)}, bf16[112,256]{1,0:T(8,128)(2,1)}) custom-call(s32[5]{0:T(128)} %stack.316.place.refs_0_, bf16[128,1600]{1,0:T(8,128)(2,1)} %copy-done.32, bf16[128,1600]{1,0:T(8,128)(2,1)} %copy-done.100, ...), custom_call_target="tpu_custom_call" | custom-call | flops 25999998976 | bytes 1 | tf_op jit(solution)/shard_map/pallas_call | solution.py:58
  532.7 6.1 shard_map.320
  547.5 10.0 %shard_map.321 = (bf16[4,200,984]{2,1,0:T(8,128)(2,1)}, bf16[1,2,200,984]{3,2,1,0:T(8,128)(2,1)}, bf16[1,2,200,984]{3,2,1,0:T(8,128)(2,1)}) custom-call(s32[5]{0:T(128)} %stack.316.place.refs_0_, bf16[128,1600]{1,0:T(8,128)(2,1)} %copy-done.30, bf16[128,1600]{1,0:T(8,128)(2,1)} %copy-done.93, bf16[128,1600]{1,0:T(8,128)(2,1)} %copy-done.94, ...), custom_call_target="tpu_custom_call" | custom-call | flops 7000000000 | bytes 1 | tf_op jit(solution)/shard_map/pallas_call | solution.py:58
  571.4 6.4 collective-permute-done.135
  584.5 5.9 collective-permute-done.137
  604.7 7.0 shard_map.322
  621.1 8.2 shard_map.323
  646.7 6.4 collective-permute-done.164
  667.2 11.0 %collective-permute-done.156.g1.s1 = bf16[128,1600]{1,0:T(8,128)(2,1)S(1)} collective-permute-done((bf16[128,1600]{1,0:T(8,128)(2,1)S(1)}, bf16[128,1600]{1,0:T(8,128)(2,1)S(1)}, u32[]{:S(2)}, u32[]{:S(2)}) %collective-permute-start.156) | collective-permute-done | bytes 409632 | tf_op jit(solution)/shard_map/ppermute | solution.py:766
  685.3 23.5 %shard_map.325 = (bf16[144,512]{1,0:T(8,128)(2,1)}, f32[512,256]{1,0:T(8,128)}, bf16[512,256]{1,0:T(8,128)(2,1)}, bf16[32,256]{1,0:T(8,128)(2,1)}, bf16[112,256]{1,0:T(8,128)(2,1)}) custom-call(s32[5]{0:T(128)} %stack.316.place.refs_0_, bf16[128,1600]{1,0:T(8,128)(2,1)} %copy-done.31, bf16[128,1600]{1,0:T(8,128)(2,1)} %copy-done.96, ...), custom_call_target="tpu_custom_call" | custom-call | flops 25999998976 | bytes 1 | tf_op jit(solution)/shard_map/pallas_call | solution.py:58
  737.6 6.1 shard_map.327
  753.1 10.0 %shard_map.328 = (bf16[4,200,984]{2,1,0:T(8,128)(2,1)}, bf16[1,2,200,984]{3,2,1,0:T(8,128)(2,1)}, bf16[1,2,200,984]{3,2,1,0:T(8,128)(2,1)}) custom-call(s32[5]{0:T(128)} %stack.316.place.refs_0_, bf16[128,1600]{1,0:T(8,128)(2,1)} %copy-done.28, bf16[128,1600]{1,0:T(8,128)(2,1)} %collective-permute-done.3.n1, bf16[128,1600]{1,0:T(8,128)(2,1)} %copy-done.89, ...), custom_call_target="tpu_custom_call" | custom-call | flops 7000000000 | bytes 1 | tf_op jit(solution)/shard_map/pallas_call | solution.py:58
  794.9 12.3 %collective-permute-done.189 = bf16[2,200,984]{2,1,0:T(8,128)(2,1)S(1)} collective-permute-done((bf16[2,200,984]{2,1,0:T(8,128)(2,1)S(1)}, bf16[2,200,984]{2,1,0:T(8,128)(2,1)S(1)}, u32[]{:S(2)}, u32[]{:S(2)}) %collective-permute-start.189) | collective-permute-done | bytes 787232 | tf_op jit(solution)/shard_map/ppermute | solution.py:747
  815.7 13.5 %collective-permute-done.191 = bf16[200,984]{1,0:T(8,128)(2,1)} collective-permute-done((bf16[200,984]{1,0:T(8,128)(2,1)}, bf16[200,984]{1,0:T(8,128)(2,1)}, u32[]{:S(2)}, u32[]{:S(2)}) %collective-permute-start.191) | collective-permute-done | bytes 393632 | tf_op jit(solution)/shard_map/ppermute | solution.py:744
  854.7 10.3 %collective-permute-done.212 = bf16[104,1032]{1,0:T(8,128)(2,1)S(1)} collective-permute-done((bf16[104,1032]{1,0:T(8,128)(2,1)S(1)}, bf16[104,1032]{1,0:T(8,128)(2,1)S(1)}, u32[]{:S(2)}, u32[]{:S(2)}) %collective-permute-start.212) | collective-permute-done | bytes 214688 | tf_op jit(solution)/shard_map/ppermute | solution.py:744
  (947 shorter events, 611.8 us)
Async XLA Ops:
  4.6 30.3 %collective-permute-start.2 = (bf16[32,1600]{1,0:T(8,128)(2,1)S(1)}, bf16[32,1600]{1,0:T(8,128)(2,1)S(1)}, u32[]{:S(2)}, u32[]{:S(2)}) collective-permute-start(bf16[32,1600]{1,0:T(8,128)(2,1)S(1)} %fusion.22), channel_id=1, source_target_pairs={{0,24},{4,28},{8,0},{12,4},{16,8},{20,12},{24,16},{28,20},{1,25},{... | collective-permute-start | bytes 307208 | tf_op jit(solution)/shard_map/ppermute | solution.py:744
  9.7 26.8 %collective-permute-start.1 = (bf16[32,1600]{1,0:T(8,128)(2,1)S(1)}, bf16[32,1600]{1,0:T(8,128)(2,1)}, u32[]{:S(2)}, u32[]{:S(2)}) collective-permute-start(bf16[32,1600]{1,0:T(8,128)(2,1)S(1)} %fusion.22), channel_id=1, source_target_pairs={{0,16},{4,20},{8,24},{12,28},{16,0},{20,4},{24,8},{28,12},{1,17},{... | collective-permute-start | bytes 307208 | tf_op jit(solution)/shard_map/ppermute | solution.py:744
  9.7 26.8 %collective-permute-start = (bf16[32,1600]{1,0:T(8,128)(2,1)S(1)}, bf16[32,1600]{1,0:T(8,128)(2,1)}, u32[]{:S(2)}, u32[]{:S(2)}) collective-permute-start(bf16[32,1600]{1,0:T(8,128)(2,1)S(1)} %fusion.22), channel_id=1, source_target_pairs={{0,8},{4,12},{8,16},{12,20},{16,24},{20,28},{24,0},{28,4},{1,9},{5... | collective-permute-start | bytes 307208 | tf_op jit(solution)/shard_map/ppermute | solution.py:744
  37.4 41.1 %collective-permute-start.4 = (bf16[128,1600]{1,0:T(8,128)(2,1)S(1)}, bf16[128,1600]{1,0:T(8,128)(2,1)S(1)}, u32[]{:S(2)}, u32[]{:S(2)}) collective-permute-start(bf16[128,1600]{1,0:T(8,128)(2,1)S(1)} %pad_maximum_fusion.7.n0), channel_id=1, source_target_pairs={{0,1},{1,0},{2,3},{3,2},{4,5},{5,4},{6,7},{7,6},{8,9},{9,8},{10,11... | collective-permute-start | bytes 1228808 | tf_op jit(solution)/shard_map/ppermute | solution.py:767
  37.5 21.3 %collective-permute-start.3 = (bf16[128,1600]{1,0:T(8,128)(2,1)S(1)}, bf16[128,1600]{1,0:T(8,128)(2,1)}, u32[]{:S(2)}, u32[]{:S(2)}) collective-permute-start(bf16[128,1600]{1,0:T(8,128)(2,1)S(1)} %pad_maximum_fusion.7.n0), channel_id=1, source_target_pairs={{0,2},{1,3},{2,0},{3,1},{4,6},{5,7},{6,4},{7,5},{8,10},{9,11},{10,... | collective-permute-start | bytes 1228808 | tf_op jit(solution)/shard_map/ppermute | solution.py:766
  64.1 23.9 %collective-permute-start.14 = (bf16[200,1032]{1,0:T(8,128)(2,1)S(1)}, bf16[200,1032]{1,0:T(8,128)(2,1)S(1)}, u32[]{:S(2)}, u32[]{:S(2)}) collective-permute-start(bf16[200,1032]{1,0:T(8,128)(2,1)S(1)} %copy-done.88), channel_id=1, source_target_pairs={{0,24},{4,28},{8,0},{12,4},{16,8},{20,12},{24,16},{28,20},{1,25},{... | collective-permute-start | bytes 1238408 | tf_op jit(solution)/shard_map/ppermute | solution.py:744
  64.6 23.3 %collective-permute-start.13 = (bf16[200,1032]{1,0:T(8,128)(2,1)S(1)}, bf16[200,1032]{1,0:T(8,128)(2,1)S(1)}, u32[]{:S(2)}, u32[]{:S(2)}) collective-permute-start(bf16[200,1032]{1,0:T(8,128)(2,1)S(1)} %copy-done.87), channel_id=1, source_target_pairs={{0,8},{4,12},{8,16},{12,20},{16,24},{20,28},{24,0},{28,4},{1,9},{5... | collective-permute-start | bytes 1238408 | tf_op jit(solution)/shard_map/ppermute | solution.py:744
  139.2 41.9 %collective-permute-start.41 = (bf16[4,200,1032]{2,1,0:T(8,128)(2,1)S(1)}, bf16[4,200,1032]{2,1,0:T(8,128)(2,1)}, u32[]{:S(2)}, u32[]{:S(2)}) collective-permute-start(bf16[4,200,1032]{2,1,0:T(8,128)(2,1)S(1)} %bitcast_dynamic-update-slice_fusion.23), channel_id=1, source_target_pairs={{0,4},{4,0},{8,12},{12,8},{16,20},{20,16},{24,28},{28,24},{1,5},{5... | collective-permute-start | bytes 4953608 | tf_op jit(solution)/shard_map/ppermute | solution.py:747
  176.4 21.4 %collective-permute-start.39 = (bf16[128,1600]{1,0:T(8,128)(2,1)S(1)}, bf16[128,1600]{1,0:T(8,128)(2,1)S(1)}, u32[]{:S(2)}, u32[]{:S(2)}) collective-permute-start(bf16[128,1600]{1,0:T(8,128)(2,1)S(1)} %pad_maximum_fusion.8.f0), channel_id=1, source_target_pairs={{0,1},{1,0},{2,3},{3,2},{4,5},{5,4},{6,7},{7,6},{8,9},{9,8},{10,11... | collective-permute-start | bytes 1228808 | tf_op jit(solution)/shard_map/ppermute | solution.py:767
  176.4 21.4 %collective-permute-start.42 = (bf16[200,984]{1,0:T(8,128)(2,1)}, bf16[200,984]{1,0:T(8,128)(2,1)S(1)}, u32[]{:S(2)}, u32[]{:S(2)}) collective-permute-start(bf16[200,984]{1,0:T(8,128)(2,1)} %get-tuple-element.375), channel_id=1, source_target_pairs={{0,16},{4,20},{8,24},{12,28},{16,0},{20,4},{24,8},{28,12},{1,17},{... | collective-permute-start | bytes 1180808 | tf_op jit(solution)/shard_map/ppermute | solution.py:744
  223.2 26.8 %collective-permute-start.58 = (bf16[200,984]{1,0:T(8,128)(2,1)S(1)}, bf16[200,984]{1,0:T(8,128)(2,1)S(1)}, u32[]{:S(2)}, u32[]{:S(2)}) collective-permute-start(bf16[200,984]{1,0:T(8,128)(2,1)S(1)} %collective-permute-done.42), channel_id=1, source_target_pairs={{0,4},{4,0},{8,12},{12,8},{16,20},{20,16},{24,28},{28,24},{1,5},{5... | collective-permute-start | bytes 1180808 | tf_op jit(solution)/shard_map/ppermute | solution.py:747
  335.9 41.8 %collective-permute-start.89 = (bf16[4,200,1032]{2,1,0:T(8,128)(2,1)S(1)}, bf16[4,200,1032]{2,1,0:T(8,128)(2,1)S(1)}, u32[]{:S(2)}, u32[]{:S(2)}) collective-permute-start(bf16[4,200,1032]{2,1,0:T(8,128)(2,1)S(1)} %bitcast_dynamic-update-slice_fusion.22), channel_id=1, source_target_pairs={{0,4},{4,0},{8,12},{12,8},{16,20},{20,16},{24,28},{28,24},{1,5},{5... | collective-permute-start | bytes 4953608 | tf_op jit(solution)/shard_map/ppermute | solution.py:747
  428.7 35.7 %collective-permute-start.114 = (bf16[2,200,1032]{2,1,0:T(8,128)(2,1)}, bf16[2,200,1032]{2,1,0:T(8,128)(2,1)S(1)}, u32[]{:S(2)}, u32[]{:S(2)}) collective-permute-start(bf16[2,200,1032]{2,1,0:T(8,128)(2,1)} %bitcast.340), channel_id=1, source_target_pairs={{0,4},{4,0},{8,12},{12,8},{16,20},{20,16},{24,28},{28,24},{1,5},{5... | collective-permute-start | bytes 2476808 | tf_op jit(solution)/shard_map/ppermute | solution.py:747
  470.4 37.4 %collective-permute-start.117 = (bf16[2,200,1032]{2,1,0:T(8,128)(2,1)}, bf16[2,200,1032]{2,1,0:T(8,128)(2,1)S(1)}, u32[]{:S(2)}, u32[]{:S(2)}) collective-permute-start(bf16[2,200,1032]{2,1,0:T(8,128)(2,1)} %bitcast.75), channel_id=1, source_target_pairs={{0,4},{4,0},{8,12},{12,8},{16,20},{20,16},{24,28},{28,24},{1,5},{5... | collective-permute-start | bytes 2476808 | tf_op jit(solution)/shard_map/ppermute | solution.py:747
  478.5 29.3 %collective-permute-start.119 = (bf16[128,1600]{1,0:T(8,128)(2,1)S(1)}, bf16[128,1600]{1,0:T(8,128)(2,1)}, u32[]{:S(2)}, u32[]{:S(2)}) collective-permute-start(bf16[128,1600]{1,0:T(8,128)(2,1)S(1)} %constant_dynamic-update-slice_fusion.4.g0.a0), channel_id=1, source_target_pairs={{0,1},{1,0},{2,3},{3,2},{4,5},{5,4},{6,7},{7,6},{8,9},{9,8},{10,11... | collective-permute-start | bytes 1228808 | tf_op jit(solution)/shard_map/ppermute | solution.py:767
  479.3 28.6 %collective-permute-start.118 = (bf16[128,1600]{1,0:T(8,128)(2,1)S(1)}, bf16[128,1600]{1,0:T(8,128)(2,1)}, u32[]{:S(2)}, u32[]{:S(2)}) collective-permute-start(bf16[128,1600]{1,0:T(8,128)(2,1)S(1)} %constant_dynamic-update-slice_fusion.4.g0.a0), channel_id=1, source_target_pairs={{0,2},{1,3},{2,0},{3,1},{4,6},{5,7},{6,4},{7,5},{8,10},{9,11},{10,... | collective-permute-start | bytes 1228808 | tf_op jit(solution)/shard_map/ppermute | solution.py:766
  480.5 27.4 %collective-permute-start.115 = (bf16[200,1032]{1,0:T(8,128)(2,1)S(1)}, bf16[200,1032]{1,0:T(8,128)(2,1)S(1)}, u32[]{:S(2)}, u32[]{:S(2)}) collective-permute-start(bf16[200,1032]{1,0:T(8,128)(2,1)S(1)} %get-tuple-element.470), channel_id=1, source_target_pairs={{0,8},{4,12},{8,16},{12,20},{16,24},{20,28},{24,0},{28,4},{1,9},{5... | collective-permute-start | bytes 1238408 | tf_op jit(solution)/shard_map/ppermute | solution.py:744
  481.5 26.3 %collective-permute-start.116 = (bf16[200,1032]{1,0:T(8,128)(2,1)S(1)}, bf16[200,1032]{1,0:T(8,128)(2,1)S(1)}, u32[]{:S(2)}, u32[]{:S(2)}) collective-permute-start(bf16[200,1032]{1,0:T(8,128)(2,1)S(1)} %get-tuple-element.471), channel_id=1, source_target_pairs={{0,24},{4,28},{8,0},{12,4},{16,8},{20,12},{24,16},{28,20},{1,25},{... | collective-permute-start | bytes 1238408 | tf_op jit(solution)/shard_map/ppermute | solution.py:744
  653.4 24.9 %collective-permute-start.162 = (bf16[2,200,1032]{2,1,0:T(8,128)(2,1)}, bf16[2,200,1032]{2,1,0:T(8,128)(2,1)S(1)}, u32[]{:S(2)}, u32[]{:S(2)}) collective-permute-start(bf16[2,200,1032]{2,1,0:T(8,128)(2,1)} %bitcast.89), channel_id=1, source_target_pairs={{0,4},{4,0},{8,12},{12,8},{16,20},{20,16},{24,28},{28,24},{1,5},{5... | collective-permute-start | bytes 2476808 | tf_op jit(solution)/shard_map/ppermute | solution.py:747
  679.3 29.6 %collective-permute-start.166 = (bf16[2,200,1032]{2,1,0:T(8,128)(2,1)S(1)}, bf16[2,200,1032]{2,1,0:T(8,128)(2,1)}, u32[]{:S(2)}, u32[]{:S(2)}) collective-permute-start(bf16[2,200,1032]{2,1,0:T(8,128)(2,1)S(1)} %bitcast.339), channel_id=1, source_target_pairs={{0,4},{4,0},{8,12},{12,8},{16,20},{20,16},{24,28},{28,24},{1,5},{5... | collective-permute-start | bytes 2476808 | tf_op jit(solution)/shard_map/ppermute | solution.py:747
  680.2 32.4 %collective-permute-start.168 = (bf16[128,1600]{1,0:T(8,128)(2,1)S(1)}, bf16[128,1600]{1,0:T(8,128)(2,1)S(1)}, u32[]{:S(2)}, u32[]{:S(2)}) collective-permute-start(bf16[128,1600]{1,0:T(8,128)(2,1)S(1)} %constant_dynamic-update-slice_fusion.8.g0.a0), channel_id=1, source_target_pairs={{0,1},{1,0},{2,3},{3,2},{4,5},{5,4},{6,7},{7,6},{8,9},{9,8},{10,11... | collective-permute-start | bytes 1228808 | tf_op jit(solution)/shard_map/ppermute | solution.py:767
  680.5 32.1 %collective-permute-start.167 = (bf16[128,1600]{1,0:T(8,128)(2,1)S(1)}, bf16[128,1600]{1,0:T(8,128)(2,1)}, u32[]{:S(2)}, u32[]{:S(2)}) collective-permute-start(bf16[128,1600]{1,0:T(8,128)(2,1)S(1)} %constant_dynamic-update-slice_fusion.8.g0.a0), channel_id=1, source_target_pairs={{0,2},{1,3},{2,0},{3,1},{4,6},{5,7},{6,4},{7,5},{8,10},{9,11},{10,... | collective-permute-start | bytes 1228808 | tf_op jit(solution)/shard_map/ppermute | solution.py:766
  681.7 30.9 %collective-permute-start.165 = (bf16[200,984]{1,0:T(8,128)(2,1)S(1)}, bf16[200,984]{1,0:T(8,128)(2,1)S(1)}, u32[]{:S(2)}, u32[]{:S(2)}) collective-permute-start(bf16[200,984]{1,0:T(8,128)(2,1)S(1)} %get-tuple-element.549), channel_id=1, source_target_pairs={{0,16},{4,20},{8,24},{12,28},{16,0},{20,4},{24,8},{28,12},{1,17},{... | collective-permute-start | bytes 1180808 | tf_op jit(solution)/shard_map/ppermute | solution.py:744
  682.9 29.7 %collective-permute-start.163 = (bf16[200,1032]{1,0:T(8,128)(2,1)S(1)}, bf16[200,1032]{1,0:T(8,128)(2,1)}, u32[]{:S(2)}, u32[]{:S(2)}) collective-permute-start(bf16[200,1032]{1,0:T(8,128)(2,1)S(1)} %get-tuple-element.545), channel_id=1, source_target_pairs={{0,8},{4,12},{8,16},{12,20},{16,24},{20,28},{24,0},{28,4},{1,9},{5... | collective-permute-start | bytes 1238408 | tf_op jit(solution)/shard_map/ppermute | solution.py:744
  783.9 24.3 %collective-permute-start.188 = (bf16[200,984]{1,0:T(8,128)(2,1)S(1)}, bf16[200,984]{1,0:T(8,128)(2,1)}, u32[]{:S(2)}, u32[]{:S(2)}) collective-permute-start(bf16[200,984]{1,0:T(8,128)(2,1)S(1)} %get-tuple-element.740), channel_id=1, source_target_pairs={{0,24},{4,28},{8,0},{12,4},{16,8},{20,12},{24,16},{28,20},{1,25},{... | collective-permute-start | bytes 1180808 | tf_op jit(solution)/shard_map/ppermute | solution.py:744
  787.0 21.1 %collective-permute-start.187 = (bf16[200,984]{1,0:T(8,128)(2,1)S(1)}, bf16[200,984]{1,0:T(8,128)(2,1)}, u32[]{:S(2)}, u32[]{:S(2)}) collective-permute-start(bf16[200,984]{1,0:T(8,128)(2,1)S(1)} %get-tuple-element.741), channel_id=1, source_target_pairs={{0,8},{4,12},{8,16},{12,20},{16,24},{20,28},{24,0},{28,4},{1,9},{5... | collective-permute-start | bytes 1180808 | tf_op jit(solution)/shard_map/ppermute | solution.py:744
  829.3 21.6 %collective-permute-start.198 = (bf16[336,200]{0,1:T(8,128)(2,1)S(1)}, bf16[336,200]{0,1:T(8,128)(2,1)S(1)}, u32[]{:S(2)}, u32[]{:S(2)}) collective-permute-start(bf16[336,200]{0,1:T(8,128)(2,1)S(1)} %fusion.19), channel_id=1, source_target_pairs={{0,24},{4,28},{8,0},{12,4},{16,8},{20,12},{24,16},{28,20},{1,25},{... | collective-permute-start | bytes 403208 | tf_op jit(solution)/shard_map/ppermute | solution.py:744
  831.5 22.1 %collective-permute-start.197 = (bf16[336,200]{0,1:T(8,128)(2,1)S(1)}, bf16[336,200]{0,1:T(8,128)(2,1)S(1)}, u32[]{:S(2)}, u32[]{:S(2)}) collective-permute-start(bf16[336,200]{0,1:T(8,128)(2,1)S(1)} %fusion.19), channel_id=1, source_target_pairs={{0,16},{4,20},{8,24},{12,28},{16,0},{20,4},{24,8},{28,12},{1,17},{... | collective-permute-start | bytes 403208 | tf_op jit(solution)/shard_map/ppermute | solution.py:744
  831.5 22.8 %collective-permute-start.196 = (bf16[336,200]{0,1:T(8,128)(2,1)S(1)}, bf16[336,200]{0,1:T(8,128)(2,1)S(1)}, u32[]{:S(2)}, u32[]{:S(2)}) collective-permute-start(bf16[336,200]{0,1:T(8,128)(2,1)S(1)} %fusion.19), channel_id=1, source_target_pairs={{0,8},{4,12},{8,16},{12,20},{16,24},{20,28},{24,0},{28,4},{1,9},{5... | collective-permute-start | bytes 403208 | tf_op jit(solution)/shard_map/ppermute | solution.py:744
  849.3 24.3 %collective-permute-start.210 = (bf16[2,200,384]{2,1,0:T(8,128)(2,1)S(1)}, bf16[2,200,384]{2,1,0:T(8,128)(2,1)S(1)}, u32[]{:S(2)}, u32[]{:S(2)}) collective-permute-start(bf16[2,200,384]{2,1,0:T(8,128)(2,1)S(1)} %pad_maximum_fusion.23.refs_5_), channel_id=1, source_target_pairs={{0,1},{1,0},{2,3},{3,2},{4,5},{5,4},{6,7},{7,6},{8,9},{9,8},{10,11... | collective-permute-start | bytes 921608 | tf_op jit(solution)/shard_map/ppermute | solution.py:1058
  849.5 25.4 %collective-permute-start.209 = (bf16[2,200,384]{2,1,0:T(8,128)(2,1)S(1)}, bf16[2,200,384]{2,1,0:T(8,128)(2,1)S(1)}, u32[]{:S(2)}, u32[]{:S(2)}) collective-permute-start(bf16[2,200,384]{2,1,0:T(8,128)(2,1)S(1)} %pad_maximum_fusion.23.refs_5_), channel_id=1, source_target_pairs={{0,2},{1,3},{2,0},{3,1},{4,6},{5,7},{6,4},{7,5},{8,10},{9,11},{10,... | collective-permute-start | bytes 921608 | tf_op jit(solution)/shard_map/ppermute | solution.py:1057
  853.6 21.3 %collective-permute-start.206 = (bf16[2,200,384]{2,1,0:T(8,128)(2,1)S(1)}, bf16[2,200,384]{2,1,0:T(8,128)(2,1)S(1)}, u32[]{:S(2)}, u32[]{:S(2)}) collective-permute-start(bf16[2,200,384]{2,1,0:T(8,128)(2,1)S(1)} %pad_maximum_fusion.22.refs_1_), channel_id=1, source_target_pairs={{0,2},{1,3},{2,0},{3,1},{4,6},{5,7},{6,4},{7,5},{8,10},{9,11},{10,... | collective-permute-start | bytes 921608 | tf_op jit(solution)/shard_map/ppermute | solution.py:1057
  (315 other events, 3755.1 us)

commit v4 on v3

--- a/solution.py
+++ b/solution.py
@@ -190,11 +190,13 @@
         parts[k][...] = values[k * count : (k + 1) * count].astype(BF16)
 
 
-def mix_forward_kernel(cols, chan, wide, length, place, n0, n1, n2, n3, w, vec, scan_w, xi, z, conv, qkv, heads, proj, p0, p1, p2, p3):
+def mix_forward_kernel(cols, chan, wide, length, place, n0, n1, n2, n3, w, vec, scan_w, xi, z, conv, qkv, heads, proj, p0, p1, p2, p3, *rest):
+    if rest:
+        rest[0][...] = w[:, cols.end :]
     normed = rows_of((n0, n1, n2, n3))
     both = to_sequences(place, mm(normed, w[:, : cols.o]).astype(BF16))
     qkv[...] = both
-    inner = to_sequences(place, mm(normed, w[:, cols.x :]))
+    inner = to_sequences(place, mm(normed, w[:, cols.x : cols.end]))
     inner_x = widen(inner[:, :chan], wide)
     xi[...] = inner_x
     z[...] = widen(inner[:, chan:], wide)
@@ -463,17 +465,20 @@
     d_x[...] = low
     inner = to_blocks(place, jnp.concatenate([low[:, :chan], d_z[:, :chan]], axis=1))
     heads = to_blocks(place, d_qkv[...])
-    to_parts((p0, p1, p2, p3), mm(inner, w[:, cols.x :], NT) + mm(heads, w[:, : cols.o], NT))
+    to_parts((p0, p1, p2, p3), mm(inner, w[:, cols.x : cols.end], NT) + mm(heads, w[:, : cols.o], NT))
     d_scan_w[...] = mm(proj[...], conv[...]).astype(BF16)
 
 
-def mix_weights_kernel(cols, chan, place, n0, n1, n2, n3, a0, a1, a2, a3, s0, s1, s2, s3, d_qkv, heads, gated, d_x, d_z, *outs):
+def mix_weights_kernel(cols, chan, extra, place, n0, n1, n2, n3, a0, a1, a2, a3, s0, s1, s2, s3, d_qkv, heads, gated, d_x, d_z, *refs):
+    outs = refs[-3:]
     normed = rows_of((n0, n1, n2, n3))
     inner = jnp.concatenate([d_x[:, :chan], d_z[:, :chan]], axis=1)
     to_shares(place, outs, 0, mm(normed, to_blocks(place, d_qkv[...]), TN))
     to_shares(place, outs, cols.o, mm(rows_of((a0, a1, a2, a3)), heads[...], TN))
     to_shares(place, outs, cols.s, mm(rows_of((s0, s1, s2, s3)), gated[:, :chan], TN))
     to_shares(place, outs, cols.x, mm(normed, to_blocks(place, inner), TN))
+    if extra:
+        to_shares(place, outs, cols.end, refs[0][...])
 
 
 def picker(rows, columns, start, valid):
@@ -482,7 +487,7 @@
     return ((row == start + col) & (col < valid)).astype(BF16)
 
 
-def pack_mix_kernel(cols, chan, tensor_size, place, q, key, value, o, x, z, ssm, *packed):
+def pack_mix_kernel(cols, chan, units, extra, tensor_size, place, q, key, value, o, x, z, ssm, down, *packed):
     tensor_idx = place[1]
     for slow_idx in range(GROUP):
 
@@ -504,10 +509,12 @@
                 packed[by][:, cols.o : cols.s] = mm(o[...], heads).astype(BF16)
                 packed[by][:, cols.s : cols.x] = ssm[:, mine]
                 packed[by][:, cols.x : cols.z] = x[:, mine]
-                packed[by][:, cols.z :] = z[:, mine]
-
-
-def pack_ffn_kernel(units, place, gate, up, down, *packed):
+                packed[by][:, cols.z : cols.end] = z[:, mine]
+                if extra:
+                    packed[by][:, cols.end :] = down[:, (s + 1) * units - extra : (s + 1) * units]
+
+
+def pack_ffn_kernel(units, extra, place, gate, up, down, *packed):
     for slow_idx in range(GROUP):
 
         @pl.when(place[0] == slow_idx)
@@ -517,7 +524,7 @@
                 mine = slice(s * units, (s + 1) * units)
                 packed[by][:, :units] = gate[:, mine]
                 packed[by][:, units : 2 * units] = up[:, mine]
-                packed[by][:, 2 * units :] = down[:, mine]
+                packed[by][:, 2 * units :] = down[:, s * units : (s + 1) * units - extra]
 
 
 def to_shares(place, outs, start, values):
@@ -581,18 +588,21 @@
         mine = slice(s * chan, (s + 1) * chan)
         d_ssm[:, mine] = pieces[came, :, cols.s : cols.x].astype(F32)
         d_in[:, 0, mine] = pieces[came, :, cols.x : cols.z].astype(F32)
-        d_in[:, 1, mine] = pieces[came, :, cols.z :].astype(F32)
-
-
-def unpack_columns_kernel(width, place, pieces, pair, *single):
+        d_in[:, 1, mine] = pieces[came, :, cols.z : cols.end].astype(F32)
+
+
+def unpack_ffn_kernel(units, extra, place, pieces, mix_pieces, gate_up, down):
     slow_idx = place[0]
     for s in range(GROUP):
         came = lax.rem(slow_idx - s + GROUP, GROUP)
-        mine = slice(s * width, (s + 1) * width)
+        mine = slice(s * units, (s + 1) * units)
+        last = (s + 1) * units - extra
         for k in range(2):
-            pair[:, k, mine] = pieces[came, :, k * width : (k + 1) * width].astype(F32)
-        for ref in single:
-            ref[:, mine] = pieces[came, :, 2 * width :].astype(F32)
+            gate_up[:, k, mine] = pieces[came, :, k * units : (k + 1) * units].astype(F32)
+        down[:, s * units : last] = pieces[came, :, 2 * units :].astype(F32)
+        if extra:
+            columns = mix_pieces.shape[2]
+            down[:, last : last + extra] = mix_pieces[came, :, columns - extra :].astype(F32)
 
 
 def small_grads_kernel(chan, rank, state, place, shared, conv_w, conv_b, step_b, dlog, skip, scan_w, step_w):
@@ -643,16 +653,23 @@
                 step_out[layer, :low, :chan] = step_w[:, layer, mine]
 
 
-def ffn_forward_kernel(units, f0, f1, f2, f3, w, hidden, p0, p1, p2, p3):
+def down_weights(units, w, rest):
+    main = w[:, 2 * units :]
+    return jnp.concatenate([main, rest[0][...]], axis=1) if rest else main
+
+
+def ffn_forward_kernel(units, f0, f1, f2, f3, w, *refs):
+    rest, (hidden, p0, p1, p2, p3) = refs[:-5], refs[-5:]
     both = mm(rows_of((f0, f1, f2, f3)), w[:, : 2 * units])
     hidden[...] = both
     gate = both[:, :units]
     activ = (gate * sigmoid(gate) * both[:, units:]).astype(BF16)
-    to_parts((p0, p1, p2, p3), mm(activ, w[:, 2 * units :], NT))
-
-
-def ffn_backward_kernel(units, d0, d1, d2, d3, hidden, w, d_hidden, activ, p0, p1, p2, p3):
-    d_activ = mm(rows_of((d0, d1, d2, d3)), w[:, 2 * units :])
+    to_parts((p0, p1, p2, p3), mm(activ, down_weights(units, w, rest), NT))
+
+
+def ffn_backward_kernel(units, d0, d1, d2, d3, hidden, w, *refs):
+    rest, (d_hidden, activ, p0, p1, p2, p3) = refs[:-6], refs[-6:]
+    d_activ = mm(rows_of((d0, d1, d2, d3)), down_weights(units, w, rest))
     gate = hidden[:, :units]
     up = hidden[:, units:]
     sig = sigmoid(gate)
@@ -665,9 +682,14 @@
     to_parts((p0, p1, p2, p3), mm(low, w[:, : 2 * units], NT))
 
 
-def ffn_weights_kernel(units, place, f0, f1, f2, f3, d0, d1, d2, d3, d_hidden, activ, *outs):
+def ffn_weights_kernel(units, place, f0, f1, f2, f3, d0, d1, d2, d3, d_hidden, activ, *refs):
+    outs, rest = refs[:3], refs[3:]
     to_shares(place, outs, 0, mm(rows_of((f0, f1, f2, f3)), d_hidden[...], TN))
-    to_shares(place, outs, 2 * units, mm(rows_of((d0, d1, d2, d3)), activ[...], TN))
+    d_down = mm(rows_of((d0, d1, d2, d3)), activ[...], TN)
+    main = outs[0].shape[2] - 2 * units
+    to_shares(place, outs, 2 * units, d_down[:, :main])
+    if rest:
+        rest[0][...] = d_down[:, main:].astype(BF16)
 
 
 def rms_scale(values, gain_vec):
@@ -715,7 +737,10 @@
     rank = -(-rank_true // 16) * 16
     proj_rows = rank + 2 * state
     cols = Mix(chan)
-    ffn_cols = 3 * units
+    over = 3 * units % LANES
+    extra = over if over <= -cols.end % LANES else 0
+    ffn_cols = 3 * units - extra
+    mix_cols = cols.end + extra
     dp_idx = lax.axis_index("dp")
     slow_idx = dp_idx // fast
     fast_idx = dp_idx % fast
@@ -762,8 +787,8 @@
         values, done = tuple(values), tuple(done)
         return list(lax.optimization_barrier(values + done)[: len(values)]) if done else list(values)
 
-    def gather_near(mine, work=()):
-        chip = after(lax.ppermute(mine, "tensor", chip_perm), *work)
+    def gather_near(mine, beside=()):
+        chip = after(lax.ppermute(mine, "tensor", chip_perm), *beside)
         core = lax.ppermute(mine, "tensor", core_perm)
         return [mine, chip, core, lax.ppermute(chip, "tensor", core_perm)]
 
@@ -792,10 +817,11 @@
         mine = add_low(mine, lax.ppermute(theirs, "tensor", core_perm))
         return add_low(mine, lax.ppermute(mine, "tensor", chip_perm))
 
-    def sum_far(mine):
+    def sum_far(mine, work=None):
         chunk = tokens // GROUP
         terms = [mine] + [slow(mine, by) for by in range(1, GROUP)]
         mine = add_low(*[jnp.roll(term, by * chunk, axis=1) for by, term in enumerate(terms)])
+        mine = mine if work is None else after(mine, work)
         theirs = lax.ppermute(mine, "tensor", core_perm)
         return jnp.where(
             core_idx == 0,
@@ -878,19 +904,28 @@
         inner = in_weight[layer]
         both = kv_weight[layer]
         packed = call(
-            functools.partial(pack_mix_kernel, cols, chan, tensor_size),
-            [out((share, cols.end), BF16)] * GROUP,
-            [q_weight, both[:, 0], both[:, 1], o_turned, inner[:, 0], inner[:, 1], ssm_turned],
+            functools.partial(pack_mix_kernel, cols, chan, units, extra, tensor_size),
+            [out((share, mix_cols), BF16)] * GROUP,
+            [
+                q_weight,
+                both[:, 0],
+                both[:, 1],
+                o_turned,
+                inner[:, 0],
+                inner[:, 1],
+                ssm_turned,
+                down_turned,
+            ],
             5,
             place=place,
-            layers=(layer, None, None, layer, None, None, layer),
+            layers=(layer, None, None, layer, None, None, layer, layer),
         )
         return packed
 
     def pack_ffn(layer, place):
         gate = gate_weight[layer]
         packed = call(
-            functools.partial(pack_ffn_kernel, units),
+            functools.partial(pack_ffn_kernel, units, extra),
             [out((share, ffn_cols), BF16)] * GROUP,
             [gate[:, 0], gate[:, 1], down_turned],
             3,
@@ -967,13 +1002,14 @@
             n = gather_tokens(normed)
             mix_w = after(mix_got.whole(), *[p[0] for p in mix_packed[1:] + ffn_packed])
         else:
-            n = gather_tokens(normed)
-            for unit in (one, three):
-                ffn_in_units[unit] = send(ffn_own, unit, n[0])
-            mix_w = after(mix_got.whole(), ffn_in_units[one])
+            n = gather_far(normed)
+            for unit in (one, three, two_a):
+                ffn_in_units[unit] = send(ffn_own, unit, n)
+            n = gather_near(n, [ffn_in_units[one]])
+            mix_w = mix_got.whole()
         ready = joined(n, [mix_w])
         if layer == 0:
-            for unit in (one, three):
+            for unit in (one, three, two_a):
                 ffn_in_units[unit] = send(ffn_own, unit, first[two])
         xi, z, conv, qkv, heads, proj_part, *attn_parts = call(
             functools.partial(mix_forward_kernel, cols, chan, wide, length),
@@ -985,15 +1021,15 @@
                 bf_rows(2 * HEAD),
                 out((proj_rows, tokens), BF16),
             ]
-            + part_outs,
+            + part_outs
+            + ([out((width, extra), BF16)] if extra else []),
             ready + [mix_w, vecs, scan_mats],
             7,
             place=place,
             layers=(None,) * 5 + (layer, layer),
         )
-        proj_part = after(proj_part, ffn_in_units[one], ffn_in_units[three])
-        ffn_in_units[two_a] = send(ffn_own, two_a, proj_part)
-        proj = sum_far(after(sum_near(proj_part), ffn_in_units[two_a]))
+        attn_parts, rest_w = attn_parts[:4], attn_parts[4:]
+        proj = sum_far(sum_near(after(proj_part, *ffn_in_units.values())))
         ffn_in_units[two_b] = send(ffn_own, two_b, proj)
         attn_total = scatter_near(joined(attn_parts, [proj]))
         gated, *ssm_parts = call(
@@ -1014,17 +1050,18 @@
             mix_branches, running, attn_out, ssm_out, gains[1], gains[2], gains[3]
         )
         ffn_in = ffn_in.astype(BF16)
-        f = gather_tokens(ffn_in)
+        f = gather_far(ffn_in)
         ffn_w = rows_round(ffn_own[0], ffn_in_units, ffn_in)
-        fetched.append((mix_w, ffn_w))
+        fetched.append((mix_w, ffn_w, rest_w))
         if final:
+            f = gather_near(f, [ffn_w])
             d_out = gather_tokens(after(grad_run.astype(BF16), f[2]))
             ffn_w = after(ffn_w, d_out[0])
         else:
             own = mix_packed[layer + 1]
             mix_got = Fetched(own[0])
-            unit_two = send(own, two, f[0])
-            ffn_w = after(ffn_w, unit_two)
+            unit_two = send(own, two, f)
+            f = gather_near(f, [unit_two, ffn_w])
             mix_got.add(two, unit_two)
         ready = joined(f, [ffn_w])
         if not final:
@@ -1032,7 +1069,7 @@
         hidden, *ffn_parts = call(
             functools.partial(ffn_forward_kernel, units),
             [f_rows(2 * units)] + part_outs,
-            ready + [ffn_w],
+            ready + [ffn_w] + rest_w,
             7,
         )
         if not final:
@@ -1083,11 +1120,10 @@
     gain_grads = [None] * layers
     early_rows = late_rows = None
 
-    def finish_mix(layer, rows, units_in, tie):
-        own, first, second, third = all_pieces(rows, units_in, tie)
-        blocks = []
-        for pair in ((own, second), (first, third)):
-            blocks += tensor_blocks(jnp.stack([p[:, : cols.s] for p in pair]))
+    def heads_blocks(pair, tie):
+        return tensor_blocks(jnp.stack([p[:, : cols.s] for p in joined(pair, [tie])]))
+
+    def finish_mix(layer, rows, units_in, blocks, tie, last):
         big["heads"] = call_into(
             functools.partial(unpack_heads_kernel, cols, tensor_size),
             layer,
@@ -1098,8 +1134,9 @@
             ],
             big["heads"],
             blocks,
-            place,
-        )
+            after(place, last),
+        )
+        pieces = stacked(rows, units_in, tie)
         big["mix"] = call_into(
             functools.partial(unpack_channels_kernel, cols, chan),
             layer,
@@ -1108,20 +1145,21 @@
                 out((layers, share, 2, GROUP * chan), F32),
             ],
             big["mix"],
-            [stacked(rows, units_in, tie)],
+            [pieces],
             place,
         )
-
-    def finish_ffn(layer, rows, units_in, tie):
+        return pieces
+
+    def finish_ffn(layer, rows, units_in, mix_pieces, tie):
         big["ffn"] = call_into(
-            functools.partial(unpack_columns_kernel, units),
+            functools.partial(unpack_ffn_kernel, units, extra),
             layer,
             [
                 out((layers, share, 2, GROUP * units), F32),
                 out((layers, share, GROUP * units), F32),
             ],
             big["ffn"],
-            [stacked(rows, units_in, tie)],
+            [stacked(rows, units_in, tie), mix_pieces],
             place,
         )
 
@@ -1135,11 +1173,12 @@
 
     above = None
     for layer in reversed(range(layers)):
-        mix_w, ffn_w = fetched[layer]
+        mix_w, ffn_w, rest_w = fetched[layer]
         n, pull_input, xi, z, conv, qkv, heads, proj, gated, pull_mix, f, hidden = kept[layer]
         if above is not None:
-            d_out = gather_tokens(grad_run.astype(BF16))
             mix_rows, ffn_above, ffn_above_units = above
+            d_out = gather_far(grad_run.astype(BF16))
+            d_out = gather_near(after(d_out, mix_rows[1], mix_rows[3]))
             running = residual + scatter_far(after(out_total, d_out[0]))
             output = (running * mask).astype(BF16)
             ffn_w = after(ffn_w, output)
@@ -1149,7 +1188,7 @@
         d_hidden, activ, *parts = call(
             functools.partial(ffn_backward_kernel, units),
             [bf_rows(2 * units), bf_rows(units)] + part_outs,
-            ready + [hidden, ffn_w],
+            ready + [hidden, ffn_w] + rest_w,
             7,
         )
         done = []
@@ -1160,7 +1199,7 @@
         far = scatter_core(parts)
         d_ffn_w = call(
             functools.partial(ffn_weights_kernel, units),
-            shares_out(ffn_cols),
+            shares_out(ffn_cols) + ([out((width, extra), BF16)] if extra else []),
             f + joined(d_out, [far]) + [d_hidden, activ],
             6,
             place=place,
@@ -1169,17 +1208,12 @@
         d_ffn_in = scatter_far(total)
         if above is None:
             out_total = scatter_near(joined(ffn_parts, [total]))
-            d_ffn_in = after(d_ffn_in, out_total)
         grad_resid, d_attn, d_ssm, d_gain_attn, d_gain_ssm, d_gain_ffn = pull_mix(
             (grad_run, d_ffn_in)
         )
         moved = go_round(d_ffn_w[1])
         d_ssm = gather_far(d_ssm.astype(BF16))
-        work = ()
-        if above is not None:
-            finish_ffn(layer + 1, ffn_above, ffn_above_units, d_ssm)
-            work = (big["ffn"][1],)
-        d_ssm = gather_near(d_ssm, work)
+        d_ssm = gather_near(d_ssm if above is not None else after(d_ssm, out_total))
         d_attn = gather_far(after(d_attn.astype(BF16), d_ssm[0]))
         done = [d_attn]
         ffn_rows = add_round(after(d_ffn_w[0], d_ssm[0]), moved, (1, 3))
@@ -1227,7 +1261,12 @@
             5,
             place=place,
         )
-        d_proj = sum_far(after(sum_near(d_proj), d_qkv))
+        d_near = sum_near(d_proj)
+        d_proj = sum_far(d_near, d_qkv)
+        if above is not None:
+            odd = heads_blocks((mix_units[one], mix_units[three]), d_near)
+            d_proj = after(d_proj, *odd[1:3])
+            even = heads_blocks((above[0][0], mix_units[two]), d_proj)
         beside = two_a if above is None else three
         ffn_units[beside] = send(ffn_rows, beside, d_proj)
         d_x, *parts, d_scan_w, small_conv = call(
@@ -1238,28 +1277,30 @@
             place=place,
             layers=(None,) * 7 + (layer, layer),
         )
-        parts = joined(parts, [ffn_units[beside]])
+        parts = joined(parts, [ffn_units[beside]] + ([] if above is None else even[1:3]))
         beside = two_b if above is None else two_a
         ffn_units[beside] = send(ffn_rows, beside, parts[0])
         done = [ffn_units[beside]]
         far = scatter_core(parts)
         d_mix_w = call(
-            functools.partial(mix_weights_kernel, cols, chan),
-            shares_out(cols.end),
-            n + d_attn + d_ssm + [d_qkv, heads, gated, after(d_x, far), d_z],
+            functools.partial(mix_weights_kernel, cols, chan, extra),
+            shares_out(mix_cols),
+            n + d_attn + d_ssm + [d_qkv, heads, gated, after(d_x, far), d_z] + list(d_ffn_w[3:]),
             7,
             place=place,
         )
         done.append(d_mix_w[0])
         total = after(scatter_near(parts, far), *done)
         d_normed = scatter_far(total)
+        if above is not None:
+            mix_above = finish_mix(layer + 1, above[0], mix_units, even + odd, total, total)
+            d_normed = after(d_normed, big["heads"][0], big["mix"][0])
         keep, odd, even = d_mix_w
         mix_rows = add_round(keep, go_round(odd), (1, 3))
-        d_normed = after(d_normed, mix_rows[1], mix_rows[3])
+        if layer == 0:
+            d_normed = after(d_normed, mix_rows[1], mix_rows[3])
         moved = go_round(even, mix_rows[1])
         mix_rows.update(add_round(after(keep, d_normed), moved, (2, 0)))
-        if above is not None:
-            above_mix = above[0], mix_units
         grad_lower, d_gain_input = pull_input(d_normed)
         grad_run = grad_resid + grad_lower
         gain_grads[layer] = jnp.stack([d_gain_input, d_gain_attn, d_gain_ssm, d_gain_ffn])
@@ -1269,26 +1310,31 @@
 
     mix_units = {unit: send(mix_rows, unit) for unit in (one, three)}
     gains = jnp.sum(every_tensor(rounded(jnp.stack(gain_grads))).astype(F32), axis=0)
-    gains = after(gains, *mix_units.values(), mix_rows[2], mix_rows[0])
+    done = [mix_rows[2], mix_rows[0]]
+    if layers > 1:
+        finish_ffn(1, ffn_above, ffn_above_units, mix_above, d_normed)
+        done.append(big["ffn"][1])
+    gains = after(gains, *mix_units.values(), *done)
     small_count = layers * small_rows[0].shape[0]
     small = jnp.concatenate(small_rows[::-1] + [rounded(gains).reshape(-1, chan)], axis=0)
-    extra = -small.shape[0] % (8 * fast)
+    padding = -small.shape[0] % (8 * fast)
     mix_units[two] = send(mix_rows, two, gains)
-    small = small_near(jnp.pad(small, ((0, extra), (0, 0))))
+    small = small_near(jnp.pad(small, ((0, padding), (0, 0))))
     small = after(small, mix_units[two])
     for unit in (one, three, two_a, two_b):
         if unit not in ffn_units:
             ffn_units[unit] = send(ffn_rows, unit, small)
-    if layers > 1:
-        finish_mix(1, *above_mix, small)
     output = all_rows(output, small)
     input_grad = all_rows(grad_run, small).astype(F32)
-    finish_mix(0, mix_rows, mix_units, small)
+    tie = small
+    odd = heads_blocks((mix_units[one], mix_units[three]), tie)
+    even = heads_blocks((mix_rows[0], mix_units[two]), tie)
     small = jnp.stack(every_slow(small))
-    finish_ffn(0, ffn_rows, ffn_units, small)
     shared = jnp.concatenate(every_fast(small), axis=1)
+    mix_pieces = finish_mix(0, mix_rows, mix_units, even + odd, tie, shared)
+    finish_ffn(0, ffn_rows, ffn_units, mix_pieces, shared)
     grad_gains = jnp.sum(
-        shared[:, small_count : shared.shape[1] - extra].astype(F32), axis=0
+        shared[:, small_count : shared.shape[1] - padding].astype(F32), axis=0
     ).reshape(norm_gains.shape)
     (
         grad_conv_weight,

time: 919 us -> 871 us (0.948)
  waiting for transfers between devices: 415 us -> 358 us
    ppermute x103, waiting for transfers between devices: 254 us -> 224 us  [slow(): return lax.ppermute(values, 'dp', slow_perm(by)) if by % GROUP else values]
    ppermute x20, waiting for transfers between devices: 61.1 us -> 49.5 us  [other_fast(): return lax.ppermute(values, 'dp', fast_perm(by)) if by % fast else values]
  transfers between devices with their start and end apart: 213 -> 213, of which waited for: 116 -> 110; matrix products, arithmetic and copies ran while one was open for 7% -> 7% of each run, Pallas kernels for 22% -> 24%
where the time goes in v4:
time: 871 us; the launch traced here: 863 us
  waiting for transfers between devices  358 us (41%)
  Pallas kernels  224 us (26%)
  starting transfers between devices  190 us (22%)
  local copies, waits for them, and re-layouts  44 us (5%)
  other arithmetic  41.7 us (5%)
    ppermute x103, waiting for transfers between devices, slow(): return lax.ppermute(values, 'dp', slow_perm(by)) if by % GROUP else values  224 us
    pallas_call x24, Pallas kernels, call(): pl.pallas_call(kernel, out_shape=outs, grid=(1,) if layers else (), in_sp...  197 us
    ppermute x103, starting transfers between devices, slow(): return lax.ppermute(values, 'dp', slow_perm(by)) if by % GROUP else values  130 us
    ppermute x20, waiting for transfers between devices, other_fast(): return lax.ppermute(values, 'dp', fast_perm(by)) if by % fast else values  49.5 us
    ppermute x10, waiting for transfers between devices, gather_near(): chip = after(lax.ppermute(mine, 'tensor', chip_perm), *beside)  34.2 us
    pallas_call x6, Pallas kernels, call_into(): pl.pallas_call(body, out_shape=outs, grid=(1,), in_specs=specs, out_specs...  27.8 us
    ppermute x20, starting transfers between devices, other_fast(): return lax.ppermute(values, 'dp', fast_perm(by)) if by % fast else values  19.7 us
  transfers between devices with their start and end apart: 213, of which 110 were waited for; matrix products, arithmetic and copies ran while one was open for 7% of the time, Pallas kernels for 24%

profile of v4, /device:TPU:0, one launch (start us, length us, event | category | flops | bytes accessed | tf_op | source)
XLA Modules:
  0.0 862.8 jit_solution(12047553579448018781)
XLA Ops:
  15.7 6.2 shard_map.305
  54.3 5.8 shard_map.306
  69.4 8.3 collective-permute-done.12
  80.8 7.7 shard_map.310
  113.6 9.8 %shard_map.311 = (bf16[512,256]{1,0:T(8,128)(2,1)}, bf16[128,1600]{1,0:T(8,128)(2,1)}, bf16[128,1600]{1,0:T(8,128)(2,1)}, bf16[128,1600]{1,0:T(8,128)(2,1)}, bf16[128,1600]{1,0:T(8,128)(2,1)}) custom-call(s32[5]{0:T(128)} %stack.316.place.refs_0_, bf16[144,512]{1,0:T(8,128)(2,1)} %maximum_select_fusion.7.proj, bf16[512,256]{1,0:T(8,128)(2,1)} %get-tuple-element.371.conv, ...), custom_call_target="tpu_custom_call" | custom-call | flops 11000000512 | bytes 1 | tf_op jit(solution)/shard_map/pallas_call | solution.py:58
  175.0 13.7 %collective-permute-done.39 = bf16[200,992]{1,0:T(8,128)(2,1)S(1)} collective-permute-done((bf16[200,992]{1,0:T(8,128)(2,1)}, bf16[200,992]{1,0:T(8,128)(2,1)S(1)}, u32[]{:S(2)}, u32[]{:S(2)}) %collective-permute-start.39) | collective-permute-done | bytes 396832 | tf_op jit(solution)/shard_map/ppermute | solution.py:769
  191.3 7.1 shard_map.312
  198.3 5.9 collective-permute-done.43
  208.5 7.5 collective-permute-done.58
  219.4 9.1 %collective-permute-done.47 = bf16[200,992]{1,0:T(8,128)(2,1)S(1)} collective-permute-done((bf16[200,992]{1,0:T(8,128)(2,1)S(1)}, bf16[200,992]{1,0:T(8,128)(2,1)S(1)}, u32[]{:S(2)}, u32[]{:S(2)}) %collective-permute-start.47) | collective-permute-done | bytes 396832 | tf_op jit(solution)/shard_map/ppermute | solution.py:769
  253.5 10.8 %collective-permute-done.55 = bf16[200,1024]{1,0:T(8,128)(2,1)S(1)} collective-permute-done((bf16[200,1024]{1,0:T(8,128)(2,1)S(1)}, bf16[200,1024]{1,0:T(8,128)(2,1)S(1)}, u32[]{:S(2)}, u32[]{:S(2)}) %collective-permute-start.55) | collective-permute-done | bytes 409632 | tf_op jit(solution)/shard_map/ppermute | solution.py:769
  268.5 7.7 shard_map.313
  305.4 9.8 %shard_map.314 = (bf16[512,256]{1,0:T(8,128)(2,1)}, bf16[128,1600]{1,0:T(8,128)(2,1)}, bf16[128,1600]{1,0:T(8,128)(2,1)}, bf16[128,1600]{1,0:T(8,128)(2,1)}, bf16[128,1600]{1,0:T(8,128)(2,1)}) custom-call(s32[5]{0:T(128)} %stack.316.place.refs_0_, bf16[144,512]{1,0:T(8,128)(2,1)} %maximum_select_fusion.8.proj, bf16[512,256]{1,0:T(8,128)(2,1)} %get-tuple-element.429.conv, ...), custom_call_target="tpu_custom_call" | custom-call | flops 11000000512 | bytes 1 | tf_op jit(solution)/shard_map/pallas_call | solution.py:58
  375.7 9.3 %collective-permute-done.93.d1 = bf16[128,1600]{1,0:T(8,128)(2,1)S(1)} collective-permute-done((bf16[128,1600]{1,0:T(8,128)(2,1)S(1)}, bf16[128,1600]{1,0:T(8,128)(2,1)S(1)}, u32[]{:S(2)}, u32[]{:S(2)}) %collective-permute-start.93) | collective-permute-done | bytes 409632 | tf_op jit(solution)/shard_map/ppermute | solution.py:791
  385.0 7.2 shard_map.315
  393.2 6.9 shard_map.316
  404.3 8.2 shard_map.317
  445.5 8.1 collective-permute-done.114
  455.1 6.9 collective-permute-done.108.g1.s1
  468.4 23.5 %shard_map.318 = (bf16[144,512]{1,0:T(8,128)(2,1)}, f32[512,256]{1,0:T(8,128)}, bf16[512,256]{1,0:T(8,128)(2,1)}, bf16[32,256]{1,0:T(8,128)(2,1)}, bf16[112,256]{1,0:T(8,128)(2,1)}) custom-call(s32[5]{0:T(128)} %stack.316.place.refs_0_, bf16[128,1600]{1,0:T(8,128)(2,1)} %copy-done.27, bf16[128,1600]{1,0:T(8,128)(2,1)} %copy-done.131, ...), custom_call_target="tpu_custom_call" | custom-call | flops 25999998976 | bytes 1 | tf_op jit(solution)/shard_map/pallas_call | solution.py:58
  518.9 6.1 shard_map.320
  533.7 11.3 %shard_map.321 = (bf16[4,200,992]{2,1,0:T(8,128)(2,1)}, bf16[1,2,200,992]{3,2,1,0:T(8,128)(2,1)}, bf16[1,2,200,992]{3,2,1,0:T(8,128)(2,1)}) custom-call(s32[5]{0:T(128)} %stack.316.place.refs_0_, bf16[128,1600]{1,0:T(8,128)(2,1)} %copy-done.25, bf16[128,1600]{1,0:T(8,128)(2,1)} %copy-done.123, bf16[128,1600]{1,0:T(8,128)(2,1)} %copy-done.124, ...), custom_call_target="tpu_custom_call" | custom-call | flops 7000000000 | bytes 1 | tf_op jit(solution)/shard_map/pallas_call | solution.py:58
  584.3 6.9 shard_map.322
  600.6 8.2 shard_map.323
  627.4 6.1 collective-permute-done.164
  640.3 6.2 collective-permute-done.159
  647.6 8.8 %collective-permute-done.156.g1.s1 = bf16[128,1600]{1,0:T(8,128)(2,1)S(1)} collective-permute-done((bf16[128,1600]{1,0:T(8,128)(2,1)S(1)}, bf16[128,1600]{1,0:T(8,128)(2,1)S(1)}, u32[]{:S(2)}, u32[]{:S(2)}) %collective-permute-start.156) | collective-permute-done | bytes 409632 | tf_op jit(solution)/shard_map/ppermute | solution.py:791
  663.4 23.5 %shard_map.324 = (bf16[144,512]{1,0:T(8,128)(2,1)}, f32[512,256]{1,0:T(8,128)}, bf16[512,256]{1,0:T(8,128)(2,1)}, bf16[32,256]{1,0:T(8,128)(2,1)}, bf16[112,256]{1,0:T(8,128)(2,1)}) custom-call(s32[5]{0:T(128)} %stack.316.place.refs_0_, bf16[128,1600]{1,0:T(8,128)(2,1)} %copy-done.26, bf16[128,1600]{1,0:T(8,128)(2,1)} %copy-done.127, ...), custom_call_target="tpu_custom_call" | custom-call | flops 25999998976 | bytes 1 | tf_op jit(solution)/shard_map/pallas_call | solution.py:58
  719.9 6.1 shard_map.326
  734.5 11.0 %shard_map.327 = (bf16[4,200,992]{2,1,0:T(8,128)(2,1)}, bf16[1,2,200,992]{3,2,1,0:T(8,128)(2,1)}, bf16[1,2,200,992]{3,2,1,0:T(8,128)(2,1)}) custom-call(s32[5]{0:T(128)} %stack.316.place.refs_0_, bf16[128,1600]{1,0:T(8,128)(2,1)} %copy-done.23, bf16[128,1600]{1,0:T(8,128)(2,1)} %copy-done.118, bf16[128,1600]{1,0:T(8,128)(2,1)} %copy-done.117, ...), custom_call_target="tpu_custom_call" | custom-call | flops 7000000000 | bytes 1 | tf_op jit(solution)/shard_map/pallas_call | solution.py:58
  781.8 7.6 collective-permute-done.195
  797.7 14.7 %collective-permute-done.197 = bf16[200,992]{1,0:T(8,128)(2,1)S(1)} collective-permute-done((bf16[200,992]{1,0:T(8,128)(2,1)}, bf16[200,992]{1,0:T(8,128)(2,1)S(1)}, u32[]{:S(2)}, u32[]{:S(2)}) %collective-permute-start.197) | collective-permute-done | bytes 396832 | tf_op jit(solution)/shard_map/ppermute | solution.py:769
  (1001 shorter events, 563.0 us)
Async XLA Ops:
  4.6 30.6 %collective-permute-start.2 = (bf16[32,1600]{1,0:T(8,128)(2,1)S(1)}, bf16[32,1600]{1,0:T(8,128)(2,1)S(1)}, u32[]{:S(2)}, u32[]{:S(2)}) collective-permute-start(bf16[32,1600]{1,0:T(8,128)(2,1)S(1)} %fusion.22), channel_id=1, source_target_pairs={{0,24},{4,28},{8,0},{12,4},{16,8},{20,12},{24,16},{28,20},{1,25},{... | collective-permute-start | bytes 307208 | tf_op jit(solution)/shard_map/ppermute | solution.py:769
  9.7 27.0 %collective-permute-start.1 = (bf16[32,1600]{1,0:T(8,128)(2,1)S(1)}, bf16[32,1600]{1,0:T(8,128)(2,1)}, u32[]{:S(2)}, u32[]{:S(2)}) collective-permute-start(bf16[32,1600]{1,0:T(8,128)(2,1)S(1)} %fusion.22), channel_id=1, source_target_pairs={{0,16},{4,20},{8,24},{12,28},{16,0},{20,4},{24,8},{28,12},{1,17},{... | collective-permute-start | bytes 307208 | tf_op jit(solution)/shard_map/ppermute | solution.py:769
  9.7 27.0 %collective-permute-start = (bf16[32,1600]{1,0:T(8,128)(2,1)S(1)}, bf16[32,1600]{1,0:T(8,128)(2,1)}, u32[]{:S(2)}, u32[]{:S(2)}) collective-permute-start(bf16[32,1600]{1,0:T(8,128)(2,1)S(1)} %fusion.22), channel_id=1, source_target_pairs={{0,8},{4,12},{8,16},{12,20},{16,24},{20,28},{24,0},{28,4},{1,9},{5... | collective-permute-start | bytes 307208 | tf_op jit(solution)/shard_map/ppermute | solution.py:769
  37.6 41.2 %collective-permute-start.4 = (bf16[128,1600]{1,0:T(8,128)(2,1)S(1)}, bf16[128,1600]{1,0:T(8,128)(2,1)S(1)}, u32[]{:S(2)}, u32[]{:S(2)}) collective-permute-start(bf16[128,1600]{1,0:T(8,128)(2,1)S(1)} %pad_maximum_fusion.7.n0), channel_id=1, source_target_pairs={{0,1},{1,0},{2,3},{3,2},{4,5},{5,4},{6,7},{7,6},{8,9},{9,8},{10,11... | collective-permute-start | bytes 1228808 | tf_op jit(solution)/shard_map/ppermute | solution.py:792
  37.7 22.4 %collective-permute-start.3 = (bf16[128,1600]{1,0:T(8,128)(2,1)S(1)}, bf16[128,1600]{1,0:T(8,128)(2,1)S(1)}, u32[]{:S(2)}, u32[]{:S(2)}) collective-permute-start(bf16[128,1600]{1,0:T(8,128)(2,1)S(1)} %pad_maximum_fusion.7.n0), channel_id=1, source_target_pairs={{0,2},{1,3},{2,0},{3,1},{4,6},{5,7},{6,4},{7,5},{8,10},{9,11},{10,... | collective-permute-start | bytes 1228808 | tf_op jit(solution)/shard_map/ppermute | solution.py:791
  43.2 21.0 %collective-permute-start.11 = (bf16[200,992]{1,0:T(8,128)(2,1)S(1)}, bf16[200,992]{1,0:T(8,128)(2,1)S(1)}, u32[]{:S(2)}, u32[]{:S(2)}) collective-permute-start(bf16[200,992]{1,0:T(8,128)(2,1)S(1)} %copy-done.158), channel_id=1, source_target_pairs={{0,16},{4,20},{8,24},{12,28},{16,0},{20,4},{24,8},{28,12},{1,17},{... | collective-permute-start | bytes 1190408 | tf_op jit(solution)/shard_map/ppermute | solution.py:769
  64.3 24.3 %collective-permute-start.15 = (bf16[96,1024]{1,0:T(8,128)(2,1)S(1)}, bf16[96,1024]{1,0:T(8,128)(2,1)S(1)}, u32[]{:S(2)}, u32[]{:S(2)}) collective-permute-start(bf16[96,1024]{1,0:T(8,128)(2,1)S(1)} %slice.518), channel_id=1, source_target_pairs={{0,16},{4,20},{8,24},{12,28},{16,0},{20,4},{24,8},{28,12},{1,17},{... | collective-permute-start | bytes 589832 | tf_op jit(solution)/shard_map/ppermute | solution.py:769
  64.3 24.3 %collective-permute-start.14 = (bf16[200,1024]{1,0:T(8,128)(2,1)}, bf16[200,1024]{1,0:T(8,128)(2,1)S(1)}, u32[]{:S(2)}, u32[]{:S(2)}) collective-permute-start(bf16[200,1024]{1,0:T(8,128)(2,1)} %get-tuple-element.363), channel_id=1, source_target_pairs={{0,24},{4,28},{8,0},{12,4},{16,8},{20,12},{24,16},{28,20},{1,25},{... | collective-permute-start | bytes 1228808 | tf_op jit(solution)/shard_map/ppermute | solution.py:769
  129.9 41.2 %collective-permute-start.40 = (bf16[4,200,1024]{2,1,0:T(8,128)(2,1)S(1)}, bf16[4,200,1024]{2,1,0:T(8,128)(2,1)}, u32[]{:S(2)}, u32[]{:S(2)}) collective-permute-start(bf16[4,200,1024]{2,1,0:T(8,128)(2,1)S(1)} %bitcast_dynamic-update-slice_fusion.23), channel_id=1, source_target_pairs={{0,4},{4,0},{8,12},{12,8},{16,20},{20,16},{24,28},{28,24},{1,5},{5... | collective-permute-start | bytes 4915208 | tf_op jit(solution)/shard_map/ppermute | solution.py:772
  167.5 21.2 %collective-permute-start.38 = (bf16[128,1600]{1,0:T(8,128)(2,1)S(1)}, bf16[128,1600]{1,0:T(8,128)(2,1)S(1)}, u32[]{:S(2)}, u32[]{:S(2)}) collective-permute-start(bf16[128,1600]{1,0:T(8,128)(2,1)S(1)} %pad_maximum_fusion.8.f0), channel_id=1, source_target_pairs={{0,2},{1,3},{2,0},{3,1},{4,6},{5,7},{6,4},{7,5},{8,10},{9,11},{10,... | collective-permute-start | bytes 1228808 | tf_op jit(solution)/shard_map/ppermute | solution.py:791
  216.1 26.8 %collective-permute-start.59 = (bf16[200,992]{1,0:T(8,128)(2,1)S(1)}, bf16[200,992]{1,0:T(8,128)(2,1)S(1)}, u32[]{:S(2)}, u32[]{:S(2)}) collective-permute-start(bf16[200,992]{1,0:T(8,128)(2,1)S(1)} %collective-permute-done.39), channel_id=1, source_target_pairs={{0,4},{4,0},{8,12},{12,8},{16,20},{20,16},{24,28},{28,24},{1,5},{5... | collective-permute-start | bytes 1190408 | tf_op jit(solution)/shard_map/ppermute | solution.py:772
  321.9 37.4 %collective-permute-start.87 = (bf16[4,200,1024]{2,1,0:T(8,128)(2,1)S(1)}, bf16[4,200,1024]{2,1,0:T(8,128)(2,1)S(1)}, u32[]{:S(2)}, u32[]{:S(2)}) collective-permute-start(bf16[4,200,1024]{2,1,0:T(8,128)(2,1)S(1)} %bitcast_dynamic-update-slice_fusion.22), channel_id=1, source_target_pairs={{0,4},{4,0},{8,12},{12,8},{16,20},{20,16},{24,28},{28,24},{1,5},{5... | collective-permute-start | bytes 4915208 | tf_op jit(solution)/shard_map/ppermute | solution.py:772
  420.8 20.6 %collective-permute-start.99 = (bf16[128,1600]{1,0:T(8,128)(2,1)S(1)}, bf16[128,1600]{1,0:T(8,128)(2,1)S(1)}, u32[]{:S(2)}, u32[]{:S(2)}) collective-permute-start(bf16[128,1600]{1,0:T(8,128)(2,1)S(1)} %copy-done.134), channel_id=1, source_target_pairs={{0,1},{1,0},{2,3},{3,2},{4,5},{5,4},{6,7},{7,6},{8,9},{9,8},{10,11... | collective-permute-start | bytes 1228808 | tf_op jit(solution)/shard_map/ppermute | solution.py:803
  454.5 37.4 %collective-permute-start.117 = (bf16[2,200,1024]{2,1,0:T(8,128)(2,1)S(1)}, bf16[2,200,1024]{2,1,0:T(8,128)(2,1)S(1)}, u32[]{:S(2)}, u32[]{:S(2)}) collective-permute-start(bf16[2,200,1024]{2,1,0:T(8,128)(2,1)S(1)} %bitcast.344), channel_id=1, source_target_pairs={{0,4},{4,0},{8,12},{12,8},{16,20},{20,16},{24,28},{28,24},{1,5},{5... | collective-permute-start | bytes 2457608 | tf_op jit(solution)/shard_map/ppermute | solution.py:772
  463.7 28.3 %collective-permute-start.119 = (bf16[128,1600]{1,0:T(8,128)(2,1)S(1)}, bf16[128,1600]{1,0:T(8,128)(2,1)S(1)}, u32[]{:S(2)}, u32[]{:S(2)}) collective-permute-start(bf16[128,1600]{1,0:T(8,128)(2,1)S(1)} %constant_dynamic-update-slice_fusion.4.g0.a0), channel_id=1, source_target_pairs={{0,1},{1,0},{2,3},{3,2},{4,5},{5,4},{6,7},{7,6},{8,9},{9,8},{10,11... | collective-permute-start | bytes 1228808 | tf_op jit(solution)/shard_map/ppermute | solution.py:792
  463.9 28.1 %collective-permute-start.118 = (bf16[128,1600]{1,0:T(8,128)(2,1)S(1)}, bf16[128,1600]{1,0:T(8,128)(2,1)}, u32[]{:S(2)}, u32[]{:S(2)}) collective-permute-start(bf16[128,1600]{1,0:T(8,128)(2,1)S(1)} %constant_dynamic-update-slice_fusion.4.g0.a0), channel_id=1, source_target_pairs={{0,2},{1,3},{2,0},{3,1},{4,6},{5,7},{6,4},{7,5},{8,10},{9,11},{10,... | collective-permute-start | bytes 1228808 | tf_op jit(solution)/shard_map/ppermute | solution.py:791
  464.4 27.6 %collective-permute-start.115 = (bf16[200,1024]{1,0:T(8,128)(2,1)S(1)}, bf16[200,1024]{1,0:T(8,128)(2,1)S(1)}, u32[]{:S(2)}, u32[]{:S(2)}) collective-permute-start(bf16[200,1024]{1,0:T(8,128)(2,1)S(1)} %get-tuple-element.485), channel_id=1, source_target_pairs={{0,8},{4,12},{8,16},{12,20},{16,24},{20,28},{24,0},{28,4},{1,9},{5... | collective-permute-start | bytes 1228808 | tf_op jit(solution)/shard_map/ppermute | solution.py:769
  465.7 26.3 %collective-permute-start.116 = (bf16[200,1024]{1,0:T(8,128)(2,1)S(1)}, bf16[200,1024]{1,0:T(8,128)(2,1)S(1)}, u32[]{:S(2)}, u32[]{:S(2)}) collective-permute-start(bf16[200,1024]{1,0:T(8,128)(2,1)S(1)} %get-tuple-element.486), channel_id=1, source_target_pairs={{0,24},{4,28},{8,0},{12,4},{16,8},{20,12},{24,16},{28,20},{1,25},{... | collective-permute-start | bytes 1228808 | tf_op jit(solution)/shard_map/ppermute | solution.py:769
  549.3 20.8 %collective-permute-start.138 = (bf16[2,200,992]{2,1,0:T(8,128)(2,1)S(1)}, bf16[2,200,992]{2,1,0:T(8,128)(2,1)S(1)}, u32[]{:S(2)}, u32[]{:S(2)}) collective-permute-start(bf16[2,200,992]{2,1,0:T(8,128)(2,1)S(1)} %bitcast.348), channel_id=1, source_target_pairs={{0,4},{4,0},{8,12},{12,8},{16,20},{20,16},{24,28},{28,24},{1,5},{5... | collective-permute-start | bytes 2380808 | tf_op jit(solution)/shard_map/ppermute | solution.py:772
  633.8 22.7 %collective-permute-start.162 = (bf16[2,200,1024]{2,1,0:T(8,128)(2,1)S(1)}, bf16[2,200,1024]{2,1,0:T(8,128)(2,1)S(1)}, u32[]{:S(2)}, u32[]{:S(2)}) collective-permute-start(bf16[2,200,1024]{2,1,0:T(8,128)(2,1)S(1)} %bitcast.346), channel_id=1, source_target_pairs={{0,4},{4,0},{8,12},{12,8},{16,20},{20,16},{24,28},{28,24},{1,5},{5... | collective-permute-start | bytes 2457608 | tf_op jit(solution)/shard_map/ppermute | solution.py:772
  657.6 29.3 %collective-permute-start.166 = (bf16[2,200,1024]{2,1,0:T(8,128)(2,1)S(1)}, bf16[2,200,1024]{2,1,0:T(8,128)(2,1)S(1)}, u32[]{:S(2)}, u32[]{:S(2)}) collective-permute-start(bf16[2,200,1024]{2,1,0:T(8,128)(2,1)S(1)} %bitcast.345), channel_id=1, source_target_pairs={{0,4},{4,0},{8,12},{12,8},{16,20},{20,16},{24,28},{28,24},{1,5},{5... | collective-permute-start | bytes 2457608 | tf_op jit(solution)/shard_map/ppermute | solution.py:772
  658.2 31.7 %collective-permute-start.168 = (bf16[128,1600]{1,0:T(8,128)(2,1)S(1)}, bf16[128,1600]{1,0:T(8,128)(2,1)S(1)}, u32[]{:S(2)}, u32[]{:S(2)}) collective-permute-start(bf16[128,1600]{1,0:T(8,128)(2,1)S(1)} %constant_dynamic-update-slice_fusion.8.g0.a0), channel_id=1, source_target_pairs={{0,1},{1,0},{2,3},{3,2},{4,5},{5,4},{6,7},{7,6},{8,9},{9,8},{10,11... | collective-permute-start | bytes 1228808 | tf_op jit(solution)/shard_map/ppermute | solution.py:792
  658.4 31.6 %collective-permute-start.167 = (bf16[128,1600]{1,0:T(8,128)(2,1)S(1)}, bf16[128,1600]{1,0:T(8,128)(2,1)}, u32[]{:S(2)}, u32[]{:S(2)}) collective-permute-start(bf16[128,1600]{1,0:T(8,128)(2,1)S(1)} %constant_dynamic-update-slice_fusion.8.g0.a0), channel_id=1, source_target_pairs={{0,2},{1,3},{2,0},{3,1},{4,6},{5,7},{6,4},{7,5},{8,10},{9,11},{10,... | collective-permute-start | bytes 1228808 | tf_op jit(solution)/shard_map/ppermute | solution.py:791
  659.2 30.7 %collective-permute-start.163 = (bf16[200,1024]{1,0:T(8,128)(2,1)S(1)}, bf16[200,1024]{1,0:T(8,128)(2,1)}, u32[]{:S(2)}, u32[]{:S(2)}) collective-permute-start(bf16[200,1024]{1,0:T(8,128)(2,1)S(1)} %get-tuple-element.554), channel_id=1, source_target_pairs={{0,8},{4,12},{8,16},{12,20},{16,24},{20,28},{24,0},{28,4},{1,9},{5... | collective-permute-start | bytes 1228808 | tf_op jit(solution)/shard_map/ppermute | solution.py:769
  661.4 28.5 %collective-permute-start.165 = (bf16[200,992]{1,0:T(8,128)(2,1)S(1)}, bf16[200,992]{1,0:T(8,128)(2,1)S(1)}, u32[]{:S(2)}, u32[]{:S(2)}) collective-permute-start(bf16[200,992]{1,0:T(8,128)(2,1)S(1)} %get-tuple-element.558), channel_id=1, source_target_pairs={{0,16},{4,20},{8,24},{12,28},{16,0},{20,4},{24,8},{28,12},{1,17},{... | collective-permute-start | bytes 1190408 | tf_op jit(solution)/shard_map/ppermute | solution.py:769
  730.3 25.2 %collective-permute-start.189 = (bf16[2,200,384]{2,1,0:T(8,128)(2,1)}, bf16[2,200,384]{2,1,0:T(8,128)(2,1)S(1)}, u32[]{:S(2)}, u32[]{:S(2)}) collective-permute-start(bf16[2,200,384]{2,1,0:T(8,128)(2,1)} %collective-permute-done.176.refs_6_), channel_id=1, source_target_pairs={{0,1},{1,0},{2,3},{3,2},{4,5},{5,4},{6,7},{7,6},{8,9},{9,8},{10,11... | collective-permute-start | bytes 921608 | tf_op jit(solution)/shard_map/ppermute | solution.py:1096
  730.7 26.9 %collective-permute-start.188 = (bf16[2,200,384]{2,1,0:T(8,128)(2,1)}, bf16[2,200,384]{2,1,0:T(8,128)(2,1)}, u32[]{:S(2)}, u32[]{:S(2)}) collective-permute-start(bf16[2,200,384]{2,1,0:T(8,128)(2,1)} %collective-permute-done.179.refs_2_), channel_id=1, source_target_pairs={{0,1},{1,0},{2,3},{3,2},{4,5},{5,4},{6,7},{7,6},{8,9},{9,8},{10,11... | collective-permute-start | bytes 921608 | tf_op jit(solution)/shard_map/ppermute | solution.py:1096
  745.6 20.5 %collective-permute-start.190 = (bf16[2,200,992]{2,1,0:T(8,128)(2,1)}, bf16[2,200,992]{2,1,0:T(8,128)(2,1)S(1)}, u32[]{:S(2)}, u32[]{:S(2)}) collective-permute-start(bf16[2,200,992]{2,1,0:T(8,128)(2,1)} %bitcast.349), channel_id=1, source_target_pairs={{0,4},{4,0},{8,12},{12,8},{16,20},{20,16},{24,28},{28,24},{1,5},{5... | collective-permute-start | bytes 2380808 | tf_op jit(solution)/shard_map/ppermute | solution.py:772
  766.4 24.0 %collective-permute-start.193 = (bf16[200,992]{1,0:T(8,128)(2,1)S(1)}, bf16[200,992]{1,0:T(8,128)(2,1)S(1)}, u32[]{:S(2)}, u32[]{:S(2)}) collective-permute-start(bf16[200,992]{1,0:T(8,128)(2,1)S(1)} %get-tuple-element.764), channel_id=1, source_target_pairs={{0,8},{4,12},{8,16},{12,20},{16,24},{20,28},{24,0},{28,4},{1,9},{5... | collective-permute-start | bytes 1190408 | tf_op jit(solution)/shard_map/ppermute | solution.py:769
  769.0 21.4 %collective-permute-start.194 = (bf16[200,992]{1,0:T(8,128)(2,1)S(1)}, bf16[200,992]{1,0:T(8,128)(2,1)S(1)}, u32[]{:S(2)}, u32[]{:S(2)}) collective-permute-start(bf16[200,992]{1,0:T(8,128)(2,1)S(1)} %get-tuple-element.763), channel_id=1, source_target_pairs={{0,24},{4,28},{8,0},{12,4},{16,8},{20,12},{24,16},{28,20},{1,25},{... | collective-permute-start | bytes 1190408 | tf_op jit(solution)/shard_map/ppermute | solution.py:769
  822.3 35.3 %collective-permute-start.210 = (bf16[2,200,384]{2,1,0:T(8,128)(2,1)S(1)}, bf16[2,200,384]{2,1,0:T(8,128)(2,1)}, u32[]{:S(2)}, u32[]{:S(2)}) collective-permute-start(bf16[2,200,384]{2,1,0:T(8,128)(2,1)S(1)} %pad_maximum_fusion.23.refs_5_), channel_id=1, source_target_pairs={{0,1},{1,0},{2,3},{3,2},{4,5},{5,4},{6,7},{7,6},{8,9},{9,8},{10,11... | collective-permute-start | bytes 921608 | tf_op jit(solution)/shard_map/ppermute | solution.py:1095
  828.8 28.8 %collective-permute-start.207 = (bf16[2,200,384]{2,1,0:T(8,128)(2,1)S(1)}, bf16[2,200,384]{2,1,0:T(8,128)(2,1)}, u32[]{:S(2)}, u32[]{:S(2)}) collective-permute-start(bf16[2,200,384]{2,1,0:T(8,128)(2,1)S(1)} %pad_maximum_fusion.22.refs_1_), channel_id=1, source_target_pairs={{0,1},{1,0},{2,3},{3,2},{4,5},{5,4},{6,7},{7,6},{8,9},{9,8},{10,11... | collective-permute-start | bytes 921608 | tf_op jit(solution)/shard_map/ppermute | solution.py:1095
  (343 other events, 3997.6 us)

commit v5 on v4

--- a/solution.py
+++ b/solution.py
@@ -581,28 +581,50 @@
                 d_kv[:, 1, group * HEAD : (group + 1) * HEAD] = total[:, HEAD:]
 
 
-def unpack_channels_kernel(cols, chan, place, pieces, d_ssm, d_in):
-    slow_idx = place[0]
-    for s in range(GROUP):
-        came = lax.rem(slow_idx - s + GROUP, GROUP)
-        mine = slice(s * chan, (s + 1) * chan)
-        d_ssm[:, mine] = pieces[came, :, cols.s : cols.x].astype(F32)
-        d_in[:, 0, mine] = pieces[came, :, cols.x : cols.z].astype(F32)
-        d_in[:, 1, mine] = pieces[came, :, cols.z : cols.end].astype(F32)
-
-
-def unpack_ffn_kernel(units, extra, place, pieces, mix_pieces, gate_up, down):
-    slow_idx = place[0]
-    for s in range(GROUP):
-        came = lax.rem(slow_idx - s + GROUP, GROUP)
-        mine = slice(s * units, (s + 1) * units)
-        last = (s + 1) * units - extra
-        for k in range(2):
-            gate_up[:, k, mine] = pieces[came, :, k * units : (k + 1) * units].astype(F32)
-        down[:, s * units : last] = pieces[came, :, 2 * units :].astype(F32)
-        if extra:
-            columns = mix_pieces.shape[2]
-            down[:, last : last + extra] = mix_pieces[came, :, columns - extra :].astype(F32)
+def by_rows(pieces, number):
+    refs = [pieces[number]] if number < 2 else [pieces[2]] if number == 3 else pieces[3:]
+    low = 0
+    parts = []
+    for ref in refs:
+        parts.append((low, low + ref.shape[0], ref))
+        low = low + ref.shape[0]
+    return parts
+
+
+def unpack_channels_kernel(cols, chan, place, *refs):
+    pieces, (d_ssm, d_in) = refs[:-2], refs[-2:]
+    for slow_idx in range(GROUP):
+
+        @pl.when(place[0] == slow_idx)
+        def _():
+            for s in range(GROUP):
+                mine = slice(s * chan, (s + 1) * chan)
+                for low, high, ref in by_rows(pieces, (slow_idx - s) % GROUP):
+                    d_ssm[low:high, mine] = ref[:, cols.s : cols.x].astype(F32)
+                    d_in[low:high, 0, mine] = ref[:, cols.x : cols.z].astype(F32)
+                    d_in[low:high, 1, mine] = ref[:, cols.z : cols.end].astype(F32)
+
+
+def unpack_ffn_kernel(units, extra, count, place, *refs):
+    pieces, mix_pieces, (gate_up, down) = refs[:count], refs[count:-2], refs[-2:]
+    for slow_idx in range(GROUP):
+
+        @pl.when(place[0] == slow_idx)
+        def _():
+            for s in range(GROUP):
+                number = (slow_idx - s) % GROUP
+                mine = slice(s * units, (s + 1) * units)
+                last = (s + 1) * units - extra
+                for low, high, ref in by_rows(pieces, number):
+                    for k in range(2):
+                        part = ref[:, k * units : (k + 1) * units]
+                        gate_up[low:high, k, mine] = part.astype(F32)
+                    down[low:high, s * units : last] = ref[:, 2 * units :].astype(F32)
+                if extra:
+                    for low, high, ref in by_rows(mix_pieces, number):
+                        columns = ref.shape[1]
+                        few = ref[:, columns - extra :].astype(F32)
+                        down[low:high, last : last + extra] = few
 
 
 def small_grads_kernel(chan, rank, state, place, shared, conv_w, conv_b, step_b, dlog, skip, scan_w, step_w):
@@ -820,8 +842,8 @@
     def sum_far(mine, work=None):
         chunk = tokens // GROUP
         terms = [mine] + [slow(mine, by) for by in range(1, GROUP)]
+        terms = joined(terms, [] if work is None else [work])
         mine = add_low(*[jnp.roll(term, by * chunk, axis=1) for by, term in enumerate(terms)])
-        mine = mine if work is None else after(mine, work)
         theirs = lax.ppermute(mine, "tensor", core_perm)
         return jnp.where(
             core_idx == 0,
@@ -889,12 +911,7 @@
 
     def all_pieces(rows, units_in, tie):
         names = (one, three) + ((two,) if two in units_in else (two_a, two_b))
-        own, first, third, *second = joined([rows[0]] + [units_in[unit] for unit in names], [tie])
-        second = second[0] if len(second) == 1 else jnp.concatenate(second, axis=0)
-        return own, first, second, third
-
-    def stacked(rows, units_in, tie):
-        return jnp.stack(all_pieces(rows, units_in, tie))
+        return joined([rows[0]] + [units_in[unit] for unit in names], [tie])
 
     o_turned = o_weight.swapaxes(1, 2)
     ssm_turned = ssm_weight.swapaxes(1, 2)
@@ -1060,12 +1077,12 @@
         else:
             own = mix_packed[layer + 1]
             mix_got = Fetched(own[0])
-            unit_two = send(own, two, f)
-            f = gather_near(f, [unit_two, ffn_w])
-            mix_got.add(two, unit_two)
+            unit_one = send(own, one, f)
+            f = gather_near(f, [unit_one, ffn_w])
+            mix_got.add(one, unit_one)
         ready = joined(f, [ffn_w])
         if not final:
-            unit_one = send(own, one, ready[0])
+            unit_two = send(own, two_a, ready[0])
         hidden, *ffn_parts = call(
             functools.partial(ffn_forward_kernel, units),
             [f_rows(2 * units)] + part_outs,
@@ -1073,11 +1090,12 @@
             7,
         )
         if not final:
-            ffn_parts = joined(ffn_parts, [unit_one])
-            mix_got.add(one, unit_one)
-            unit_three = send(own, three, ffn_parts[0])
-            total = after(scatter_near(ffn_parts), unit_three)
-            mix_got.add(three, unit_three)
+            ffn_parts = joined(ffn_parts, [unit_two])
+            mix_got.add(two_a, unit_two)
+            last = {unit: send(own, unit, ffn_parts[0]) for unit in (three, two_b)}
+            total = after(scatter_near(ffn_parts), *last.values())
+            for unit, piece in last.items():
+                mix_got.add(unit, piece)
             running = residual + scatter_far(total)
         kept.append((n, pull_input, xi, z, conv, qkv, heads, proj, gated, pull_mix, f, hidden))
 
@@ -1136,7 +1154,7 @@
             blocks,
             after(place, last),
         )
-        pieces = stacked(rows, units_in, tie)
+        pieces = all_pieces(rows, units_in, tie)
         big["mix"] = call_into(
             functools.partial(unpack_channels_kernel, cols, chan),
             layer,
@@ -1145,21 +1163,22 @@
                 out((layers, share, 2, GROUP * chan), F32),
             ],
             big["mix"],
-            [pieces],
+            pieces,
             place,
         )
         return pieces
 
     def finish_ffn(layer, rows, units_in, mix_pieces, tie):
+        pieces = all_pieces(rows, units_in, tie)
         big["ffn"] = call_into(
-            functools.partial(unpack_ffn_kernel, units, extra),
+            functools.partial(unpack_ffn_kernel, units, extra, len(pieces)),
             layer,
             [
                 out((layers, share, 2, GROUP * units), F32),
                 out((layers, share, GROUP * units), F32),
             ],
             big["ffn"],
-            [stacked(rows, units_in, tie), mix_pieces],
+            pieces + mix_pieces,
             place,
         )
 
@@ -1212,8 +1231,13 @@
             (grad_run, d_ffn_in)
         )
         moved = go_round(d_ffn_w[1])
-        d_ssm = gather_far(d_ssm.astype(BF16))
-        d_ssm = gather_near(d_ssm if above is not None else after(d_ssm, out_total))
+        d_ssm = after(gather_far(d_ssm.astype(BF16)), *moved)
+        if above is None:
+            d_ssm = after(d_ssm, out_total)
+        else:
+            odd = heads_blocks((mix_units[one], mix_units[three]), total)
+            d_ssm = after(d_ssm, *odd[1:3])
+        d_ssm = gather_near(d_ssm)
         d_attn = gather_far(after(d_attn.astype(BF16), d_ssm[0]))
         done = [d_attn]
         ffn_rows = add_round(after(d_ffn_w[0], d_ssm[0]), moved, (1, 3))
@@ -1264,8 +1288,6 @@
         d_near = sum_near(d_proj)
         d_proj = sum_far(d_near, d_qkv)
         if above is not None:
-            odd = heads_blocks((mix_units[one], mix_units[three]), d_near)
-            d_proj = after(d_proj, *odd[1:3])
             even = heads_blocks((above[0][0], mix_units[two]), d_proj)
         beside = two_a if above is None else three
         ffn_units[beside] = send(ffn_rows, beside, d_proj)

time: 871 us -> 850 us (0.976)
  waiting for transfers between devices: 358 us -> 337 us
    ppermute x103 -> x104, waiting for transfers between devices: 224 us -> 217 us  [slow(): return lax.ppermute(values, 'dp', slow_perm(by)) if by % GROUP else values]
    ppermute x20 -> x21, starting transfers between devices: 19.7 us -> 26 us  [other_fast(): return lax.ppermute(values, 'dp', fast_perm(by)) if by % fast else values]
    ppermute x103 -> x104, starting transfers between devices: 130 us -> 126 us  [slow(): return lax.ppermute(values, 'dp', slow_perm(by)) if by % GROUP else values]
    ppermute x20 -> x21, waiting for transfers between devices: 49.5 us -> 46.9 us  [other_fast(): return lax.ppermute(values, 'dp', fast_perm(by)) if by % fast else values]
  transfers between devices with their start and end apart: 213 -> 215, of which waited for: 110 -> 106; matrix products, arithmetic and copies ran while one was open for 7% -> 7% of each run, Pallas kernels for 24% -> 25%
where the time goes in v5:
time: 850 us; the launch traced here: 841 us
  waiting for transfers between devices  337 us (40%)
  Pallas kernels  225 us (26%)
  starting transfers between devices  196 us (23%)
  local copies, waits for them, and re-layouts  44.1 us (5%)
  other arithmetic  35.5 us (4%)
    ppermute x104, waiting for transfers between devices, slow(): return lax.ppermute(values, 'dp', slow_perm(by)) if by % GROUP else values  217 us
    pallas_call x24, Pallas kernels, call(): pl.pallas_call(kernel, out_shape=outs, grid=(1,) if layers else (), in_sp...  196 us
    ppermute x104, starting transfers between devices, slow(): return lax.ppermute(values, 'dp', slow_perm(by)) if by % GROUP else values  126 us
    ppermute x21, waiting for transfers between devices, other_fast(): return lax.ppermute(values, 'dp', fast_perm(by)) if by % fast else values  46.9 us
    pallas_call x6, Pallas kernels, call_into(): pl.pallas_call(body, out_shape=outs, grid=(1,), in_specs=specs, out_specs...  29.2 us
    ppermute x10, waiting for transfers between devices, gather_near(): chip = after(lax.ppermute(mine, 'tensor', chip_perm), *beside)  26.8 us
    ppermute x21, starting transfers between devices, other_fast(): return lax.ppermute(values, 'dp', fast_perm(by)) if by % fast else values  26 us
  transfers between devices with their start and end apart: 215, of which 106 were waited for; matrix products, arithmetic and copies ran while one was open for 7% of the time, Pallas kernels for 25%

profile of v5, /device:TPU:0, one launch (start us, length us, event | category | flops | bytes accessed | tf_op | source)
XLA Modules:
  0.0 841.1 jit_solution(4856968543606794987)
XLA Ops:
  15.1 5.9 shard_map.305
  53.3 5.8 shard_map.306
  68.4 8.3 collective-permute-done.12
  80.0 7.8 shard_map.310
  112.6 9.8 %shard_map.311 = (bf16[512,256]{1,0:T(8,128)(2,1)}, bf16[128,1600]{1,0:T(8,128)(2,1)}, bf16[128,1600]{1,0:T(8,128)(2,1)}, bf16[128,1600]{1,0:T(8,128)(2,1)}, bf16[128,1600]{1,0:T(8,128)(2,1)}) custom-call(s32[5]{0:T(128)} %stack.256.place.refs_0_, bf16[144,512]{1,0:T(8,128)(2,1)} %maximum_select_fusion.7.proj, bf16[512,256]{1,0:T(8,128)(2,1)} %get-tuple-element.380.conv, ...), custom_call_target="tpu_custom_call" | custom-call | flops 11000000512 | bytes 1 | tf_op jit(solution)/shard_map/pallas_call | solution.py:58
  159.5 5.7 collective-permute-done.36
  171.1 8.6 %collective-permute-done.39 = bf16[200,992]{1,0:T(8,128)(2,1)} collective-permute-done((bf16[200,992]{1,0:T(8,128)(2,1)}, bf16[200,992]{1,0:T(8,128)(2,1)}, u32[]{:S(2)}, u32[]{:S(2)}) %collective-permute-start.39) | collective-permute-done | bytes 396832 | tf_op jit(solution)/shard_map/ppermute | solution.py:791
  182.5 7.0 shard_map.312
  195.8 8.7 %collective-permute-done.60 = bf16[200,992]{1,0:T(8,128)(2,1)S(1)} collective-permute-done((bf16[200,992]{1,0:T(8,128)(2,1)}, bf16[200,992]{1,0:T(8,128)(2,1)S(1)}, u32[]{:S(2)}, u32[]{:S(2)}) %collective-permute-start.60) | collective-permute-done | bytes 396832 | tf_op jit(solution)/shard_map/ppermute | solution.py:794
  208.2 8.1 collective-permute-done.48
  220.7 6.3 collective-permute-start.49
  255.5 6.0 collective-permute-done.56
  264.1 7.8 shard_map.313
  272.3 6.0 collective-permute-done.64
  302.9 9.8 %shard_map.314 = (bf16[512,256]{1,0:T(8,128)(2,1)}, bf16[128,1600]{1,0:T(8,128)(2,1)}, bf16[128,1600]{1,0:T(8,128)(2,1)}, bf16[128,1600]{1,0:T(8,128)(2,1)}, bf16[128,1600]{1,0:T(8,128)(2,1)}) custom-call(s32[5]{0:T(128)} %stack.256.place.refs_0_, bf16[144,512]{1,0:T(8,128)(2,1)} %maximum_select_fusion.8.proj, bf16[512,256]{1,0:T(8,128)(2,1)} %get-tuple-element.439.conv, ...), custom_call_target="tpu_custom_call" | custom-call | flops 11000000512 | bytes 1 | tf_op jit(solution)/shard_map/pallas_call | solution.py:58
  373.0 9.5 %collective-permute-done.95.d1 = bf16[128,1600]{1,0:T(8,128)(2,1)S(1)} collective-permute-done((bf16[128,1600]{1,0:T(8,128)(2,1)S(1)}, bf16[128,1600]{1,0:T(8,128)(2,1)S(1)}, u32[]{:S(2)}, u32[]{:S(2)}) %collective-permute-start.95) | collective-permute-done | bytes 409632 | tf_op jit(solution)/shard_map/ppermute | solution.py:813
  382.6 7.1 shard_map.315
  390.6 6.9 shard_map.316
  401.5 8.2 shard_map.317
  461.5 23.3 %shard_map.318 = (bf16[144,512]{1,0:T(8,128)(2,1)}, f32[512,256]{1,0:T(8,128)}, bf16[512,256]{1,0:T(8,128)(2,1)}, bf16[32,256]{1,0:T(8,128)(2,1)}, bf16[112,256]{1,0:T(8,128)(2,1)}) custom-call(s32[5]{0:T(128)} %stack.256.place.refs_0_, bf16[128,1600]{1,0:T(8,128)(2,1)} %copy-done.22, bf16[128,1600]{1,0:T(8,128)(2,1)} %copy-done.85, ...), custom_call_target="tpu_custom_call" | custom-call | flops 25999998976 | bytes 1 | tf_op jit(solution)/shard_map/pallas_call | solution.py:58
  505.8 6.1 shard_map.320
  519.4 11.4 %shard_map.321 = (bf16[4,200,992]{2,1,0:T(8,128)(2,1)}, bf16[1,2,200,992]{3,2,1,0:T(8,128)(2,1)}, bf16[1,2,200,992]{3,2,1,0:T(8,128)(2,1)}) custom-call(s32[5]{0:T(128)} %stack.256.place.refs_0_, bf16[128,1600]{1,0:T(8,128)(2,1)} %copy-done.20, bf16[128,1600]{1,0:T(8,128)(2,1)} %copy-done.76, bf16[128,1600]{1,0:T(8,128)(2,1)} %copy-done.77, ...), custom_call_target="tpu_custom_call" | custom-call | flops 7000000000 | bytes 1 | tf_op jit(solution)/shard_map/pallas_call | solution.py:58
  551.2 6.3 collective-permute-done.138
  563.7 5.7 collective-permute-done.144.d1
  572.2 6.9 shard_map.322
  589.2 8.2 shard_map.323
  619.5 7.9 collective-permute-done.156
  647.9 23.2 %shard_map.324 = (bf16[144,512]{1,0:T(8,128)(2,1)}, f32[512,256]{1,0:T(8,128)}, bf16[512,256]{1,0:T(8,128)(2,1)}, bf16[32,256]{1,0:T(8,128)(2,1)}, bf16[112,256]{1,0:T(8,128)(2,1)}) custom-call(s32[5]{0:T(128)} %stack.256.place.refs_0_, bf16[128,1600]{1,0:T(8,128)(2,1)} %copy-done.21, bf16[128,1600]{1,0:T(8,128)(2,1)} %copy-done.80, ...), custom_call_target="tpu_custom_call" | custom-call | flops 25999998976 | bytes 1 | tf_op jit(solution)/shard_map/pallas_call | solution.py:58
  701.7 6.1 shard_map.326
  715.2 11.0 %shard_map.327 = (bf16[4,200,992]{2,1,0:T(8,128)(2,1)}, bf16[1,2,200,992]{3,2,1,0:T(8,128)(2,1)}, bf16[1,2,200,992]{3,2,1,0:T(8,128)(2,1)}) custom-call(s32[5]{0:T(128)} %stack.256.place.refs_0_, bf16[128,1600]{1,0:T(8,128)(2,1)} %copy-done.18, bf16[128,1600]{1,0:T(8,128)(2,1)} %copy-done.72, bf16[128,1600]{1,0:T(8,128)(2,1)} %copy-done.71, ...), custom_call_target="tpu_custom_call" | custom-call | flops 7000000000 | bytes 1 | tf_op jit(solution)/shard_map/pallas_call | solution.py:58
  759.9 10.3 %collective-permute-done.197 = bf16[2,200,992]{2,1,0:T(8,128)(2,1)S(1)} collective-permute-done((bf16[2,200,992]{2,1,0:T(8,128)(2,1)S(1)}, bf16[2,200,992]{2,1,0:T(8,128)(2,1)S(1)}, u32[]{:S(2)}, u32[]{:S(2)}) %collective-permute-start.197) | collective-permute-done | bytes 793632 | tf_op jit(solution)/shard_map/ppermute | solution.py:794
  777.9 14.2 %collective-permute-done.199.refs_4_.refs_9_ = bf16[200,992]{1,0:T(8,128)(2,1)S(1)} collective-permute-done((bf16[200,992]{1,0:T(8,128)(2,1)S(1)}, bf16[200,992]{1,0:T(8,128)(2,1)S(1)}, u32[]{:S(2)}, u32[]{:S(2)}) %collective-permute-start.199) | collective-permute-done | bytes 396832 | tf_op jit(solution)/shard_map/ppermute | solution.py:791
  (923 shorter events, 553.3 us)
Async XLA Ops:
  4.0 29.6 %collective-permute-start.2 = (bf16[32,1600]{1,0:T(8,128)(2,1)S(1)}, bf16[32,1600]{1,0:T(8,128)(2,1)}, u32[]{:S(2)}, u32[]{:S(2)}) collective-permute-start(bf16[32,1600]{1,0:T(8,128)(2,1)S(1)} %fusion.22), channel_id=1, source_target_pairs={{0,24},{4,28},{8,0},{12,4},{16,8},{20,12},{24,16},{28,20},{1,25},{... | collective-permute-start | bytes 307208 | tf_op jit(solution)/shard_map/ppermute | solution.py:791
  9.1 26.0 %collective-permute-start.1 = (bf16[32,1600]{1,0:T(8,128)(2,1)S(1)}, bf16[32,1600]{1,0:T(8,128)(2,1)}, u32[]{:S(2)}, u32[]{:S(2)}) collective-permute-start(bf16[32,1600]{1,0:T(8,128)(2,1)S(1)} %fusion.22), channel_id=1, source_target_pairs={{0,16},{4,20},{8,24},{12,28},{16,0},{20,4},{24,8},{28,12},{1,17},{... | collective-permute-start | bytes 307208 | tf_op jit(solution)/shard_map/ppermute | solution.py:791
  9.1 26.0 %collective-permute-start = (bf16[32,1600]{1,0:T(8,128)(2,1)S(1)}, bf16[32,1600]{1,0:T(8,128)(2,1)}, u32[]{:S(2)}, u32[]{:S(2)}) collective-permute-start(bf16[32,1600]{1,0:T(8,128)(2,1)S(1)} %fusion.22), channel_id=1, source_target_pairs={{0,8},{4,12},{8,16},{12,20},{16,24},{20,28},{24,0},{28,4},{1,9},{5... | collective-permute-start | bytes 307208 | tf_op jit(solution)/shard_map/ppermute | solution.py:791
  36.1 41.9 %collective-permute-start.4 = (bf16[128,1600]{1,0:T(8,128)(2,1)S(1)}, bf16[128,1600]{1,0:T(8,128)(2,1)S(1)}, u32[]{:S(2)}, u32[]{:S(2)}) collective-permute-start(bf16[128,1600]{1,0:T(8,128)(2,1)S(1)} %pad_maximum_fusion.3.n0), channel_id=1, source_target_pairs={{0,1},{1,0},{2,3},{3,2},{4,5},{5,4},{6,7},{7,6},{8,9},{9,8},{10,11... | collective-permute-start | bytes 1228808 | tf_op jit(solution)/shard_map/ppermute | solution.py:814
  36.2 22.9 %collective-permute-start.3 = (bf16[128,1600]{1,0:T(8,128)(2,1)S(1)}, bf16[128,1600]{1,0:T(8,128)(2,1)S(1)}, u32[]{:S(2)}, u32[]{:S(2)}) collective-permute-start(bf16[128,1600]{1,0:T(8,128)(2,1)S(1)} %pad_maximum_fusion.3.n0), channel_id=1, source_target_pairs={{0,2},{1,3},{2,0},{3,1},{4,6},{5,7},{6,4},{7,5},{8,10},{9,11},{10,... | collective-permute-start | bytes 1228808 | tf_op jit(solution)/shard_map/ppermute | solution.py:813
  42.3 21.0 %collective-permute-start.11 = (bf16[200,992]{1,0:T(8,128)(2,1)S(1)}, bf16[200,992]{1,0:T(8,128)(2,1)S(1)}, u32[]{:S(2)}, u32[]{:S(2)}) collective-permute-start(bf16[200,992]{1,0:T(8,128)(2,1)S(1)} %copy-done.112), channel_id=1, source_target_pairs={{0,16},{4,20},{8,24},{12,28},{16,0},{20,4},{24,8},{28,12},{1,17},{... | collective-permute-start | bytes 1190408 | tf_op jit(solution)/shard_map/ppermute | solution.py:791
  63.3 24.5 %collective-permute-start.15 = (bf16[96,1024]{1,0:T(8,128)(2,1)S(1)}, bf16[96,1024]{1,0:T(8,128)(2,1)S(1)}, u32[]{:S(2)}, u32[]{:S(2)}) collective-permute-start(bf16[96,1024]{1,0:T(8,128)(2,1)S(1)} %slice.524), channel_id=1, source_target_pairs={{0,16},{4,20},{8,24},{12,28},{16,0},{20,4},{24,8},{28,12},{1,17},{... | collective-permute-start | bytes 589832 | tf_op jit(solution)/shard_map/ppermute | solution.py:791
  63.3 24.5 %collective-permute-start.14 = (bf16[200,1024]{1,0:T(8,128)(2,1)}, bf16[200,1024]{1,0:T(8,128)(2,1)S(1)}, u32[]{:S(2)}, u32[]{:S(2)}) collective-permute-start(bf16[200,1024]{1,0:T(8,128)(2,1)} %get-tuple-element.372), channel_id=1, source_target_pairs={{0,24},{4,28},{8,0},{12,4},{16,8},{20,12},{24,16},{28,20},{1,25},{... | collective-permute-start | bytes 1228808 | tf_op jit(solution)/shard_map/ppermute | solution.py:791
  128.9 38.3 %collective-permute-start.40 = (bf16[4,200,1024]{2,1,0:T(8,128)(2,1)S(1)}, bf16[4,200,1024]{2,1,0:T(8,128)(2,1)}, u32[]{:S(2)}, u32[]{:S(2)}) collective-permute-start(bf16[4,200,1024]{2,1,0:T(8,128)(2,1)S(1)} %bitcast_dynamic-update-slice_fusion.23), channel_id=1, source_target_pairs={{0,4},{4,0},{8,12},{12,8},{16,20},{20,16},{24,28},{28,24},{1,5},{5... | collective-permute-start | bytes 4915208 | tf_op jit(solution)/shard_map/ppermute | solution.py:794
  206.5 33.9 %collective-permute-start.61 = (bf16[96,992]{1,0:T(8,128)(2,1)}, bf16[96,992]{1,0:T(8,128)(2,1)S(1)}, u32[]{:S(2)}, u32[]{:S(2)}) collective-permute-start(bf16[96,992]{1,0:T(8,128)(2,1)} %collective-permute-done.43), channel_id=1, source_target_pairs={{0,4},{4,0},{8,12},{12,8},{16,20},{20,16},{24,28},{28,24},{1,5},{5... | collective-permute-start | bytes 571400 | tf_op jit(solution)/shard_map/ppermute | solution.py:794
  240.5 21.1 %collective-permute-start.63 = (bf16[104,992]{1,0:T(8,128)(2,1)S(1)}, bf16[104,992]{1,0:T(8,128)(2,1)S(1)}, u32[]{:S(2)}, u32[]{:S(2)}) collective-permute-start(bf16[104,992]{1,0:T(8,128)(2,1)S(1)} %collective-permute-done.48), channel_id=1, source_target_pairs={{0,4},{4,0},{8,12},{12,8},{16,20},{20,16},{24,28},{28,24},{1,5},{5... | collective-permute-start | bytes 619016 | tf_op jit(solution)/shard_map/ppermute | solution.py:794
  319.2 37.7 %collective-permute-start.89 = (bf16[4,200,1024]{2,1,0:T(8,128)(2,1)S(1)}, bf16[4,200,1024]{2,1,0:T(8,128)(2,1)S(1)}, u32[]{:S(2)}, u32[]{:S(2)}) collective-permute-start(bf16[4,200,1024]{2,1,0:T(8,128)(2,1)S(1)} %bitcast_dynamic-update-slice_fusion.20), channel_id=1, source_target_pairs={{0,4},{4,0},{8,12},{12,8},{16,20},{20,16},{24,28},{28,24},{1,5},{5... | collective-permute-start | bytes 4915208 | tf_op jit(solution)/shard_map/ppermute | solution.py:794
  449.3 35.4 %collective-permute-start.119 = (bf16[2,200,1024]{2,1,0:T(8,128)(2,1)}, bf16[2,200,1024]{2,1,0:T(8,128)(2,1)S(1)}, u32[]{:S(2)}, u32[]{:S(2)}) collective-permute-start(bf16[2,200,1024]{2,1,0:T(8,128)(2,1)} %bitcast.77), channel_id=1, source_target_pairs={{0,4},{4,0},{8,12},{12,8},{16,20},{20,16},{24,28},{28,24},{1,5},{5... | collective-permute-start | bytes 2457608 | tf_op jit(solution)/shard_map/ppermute | solution.py:794
  456.4 28.3 %collective-permute-start.121 = (bf16[128,1600]{1,0:T(8,128)(2,1)S(1)}, bf16[128,1600]{1,0:T(8,128)(2,1)S(1)}, u32[]{:S(2)}, u32[]{:S(2)}) collective-permute-start(bf16[128,1600]{1,0:T(8,128)(2,1)S(1)} %constant_dynamic-update-slice_fusion.4.g0.a0), channel_id=1, source_target_pairs={{0,1},{1,0},{2,3},{3,2},{4,5},{5,4},{6,7},{7,6},{8,9},{9,8},{10,11... | collective-permute-start | bytes 1228808 | tf_op jit(solution)/shard_map/ppermute | solution.py:814
  456.6 28.2 %collective-permute-start.120 = (bf16[128,1600]{1,0:T(8,128)(2,1)S(1)}, bf16[128,1600]{1,0:T(8,128)(2,1)}, u32[]{:S(2)}, u32[]{:S(2)}) collective-permute-start(bf16[128,1600]{1,0:T(8,128)(2,1)S(1)} %constant_dynamic-update-slice_fusion.4.g0.a0), channel_id=1, source_target_pairs={{0,2},{1,3},{2,0},{3,1},{4,6},{5,7},{6,4},{7,5},{8,10},{9,11},{10,... | collective-permute-start | bytes 1228808 | tf_op jit(solution)/shard_map/ppermute | solution.py:813
  457.6 27.1 %collective-permute-start.117 = (bf16[200,1024]{1,0:T(8,128)(2,1)S(1)}, bf16[200,1024]{1,0:T(8,128)(2,1)S(1)}, u32[]{:S(2)}, u32[]{:S(2)}) collective-permute-start(bf16[200,1024]{1,0:T(8,128)(2,1)S(1)} %get-tuple-element.496), channel_id=1, source_target_pairs={{0,8},{4,12},{8,16},{12,20},{16,24},{20,28},{24,0},{28,4},{1,9},{5... | collective-permute-start | bytes 1228808 | tf_op jit(solution)/shard_map/ppermute | solution.py:791
  459.8 24.9 %collective-permute-start.118 = (bf16[200,1024]{1,0:T(8,128)(2,1)S(1)}, bf16[200,1024]{1,0:T(8,128)(2,1)}, u32[]{:S(2)}, u32[]{:S(2)}) collective-permute-start(bf16[200,1024]{1,0:T(8,128)(2,1)S(1)} %get-tuple-element.497), channel_id=1, source_target_pairs={{0,24},{4,28},{8,0},{12,4},{16,8},{20,12},{24,16},{28,20},{1,25},{... | collective-permute-start | bytes 1228808 | tf_op jit(solution)/shard_map/ppermute | solution.py:791
  535.1 22.5 %collective-permute-start.140 = (bf16[2,200,992]{2,1,0:T(8,128)(2,1)}, bf16[2,200,992]{2,1,0:T(8,128)(2,1)S(1)}, u32[]{:S(2)}, u32[]{:S(2)}) collective-permute-start(bf16[2,200,992]{2,1,0:T(8,128)(2,1)} %bitcast.321), channel_id=1, source_target_pairs={{0,4},{4,0},{8,12},{12,8},{16,20},{20,16},{24,28},{28,24},{1,5},{5... | collective-permute-start | bytes 2380808 | tf_op jit(solution)/shard_map/ppermute | solution.py:794
  584.5 32.5 %collective-permute-start.168 = (bf16[2,200,992]{2,1,0:T(8,128)(2,1)}, bf16[2,200,992]{2,1,0:T(8,128)(2,1)S(1)}, u32[]{:S(2)}, u32[]{:S(2)}) collective-permute-start(bf16[2,200,992]{2,1,0:T(8,128)(2,1)} %bitcast.91), channel_id=1, source_target_pairs={{0,4},{4,0},{8,12},{12,8},{16,20},{20,16},{24,28},{28,24},{1,5},{5... | collective-permute-start | bytes 2380808 | tf_op jit(solution)/shard_map/ppermute | solution.py:794
  597.4 30.2 %collective-permute-start.158 = (bf16[2,200,1024]{2,1,0:T(8,128)(2,1)}, bf16[2,200,1024]{2,1,0:T(8,128)(2,1)S(1)}, u32[]{:S(2)}, u32[]{:S(2)}) collective-permute-start(bf16[2,200,1024]{2,1,0:T(8,128)(2,1)} %bitcast.319), channel_id=1, source_target_pairs={{0,4},{4,0},{8,12},{12,8},{16,20},{20,16},{24,28},{28,24},{1,5},{5... | collective-permute-start | bytes 2457608 | tf_op jit(solution)/shard_map/ppermute | solution.py:794
  637.0 34.1 %collective-permute-start.170 = (bf16[2,200,1024]{2,1,0:T(8,128)(2,1)S(1)}, bf16[2,200,1024]{2,1,0:T(8,128)(2,1)S(1)}, u32[]{:S(2)}, u32[]{:S(2)}) collective-permute-start(bf16[2,200,1024]{2,1,0:T(8,128)(2,1)S(1)} %bitcast.317), channel_id=1, source_target_pairs={{0,4},{4,0},{8,12},{12,8},{16,20},{20,16},{24,28},{28,24},{1,5},{5... | collective-permute-start | bytes 2457608 | tf_op jit(solution)/shard_map/ppermute | solution.py:794
  644.0 32.0 %collective-permute-start.172 = (bf16[128,1600]{1,0:T(8,128)(2,1)S(1)}, bf16[128,1600]{1,0:T(8,128)(2,1)S(1)}, u32[]{:S(2)}, u32[]{:S(2)}) collective-permute-start(bf16[128,1600]{1,0:T(8,128)(2,1)S(1)} %constant_dynamic-update-slice_fusion.8.g0.a0), channel_id=1, source_target_pairs={{0,1},{1,0},{2,3},{3,2},{4,5},{5,4},{6,7},{7,6},{8,9},{9,8},{10,11... | collective-permute-start | bytes 1228808 | tf_op jit(solution)/shard_map/ppermute | solution.py:814
  644.1 31.8 %collective-permute-start.171 = (bf16[128,1600]{1,0:T(8,128)(2,1)S(1)}, bf16[128,1600]{1,0:T(8,128)(2,1)S(1)}, u32[]{:S(2)}, u32[]{:S(2)}) collective-permute-start(bf16[128,1600]{1,0:T(8,128)(2,1)S(1)} %constant_dynamic-update-slice_fusion.8.g0.a0), channel_id=1, source_target_pairs={{0,2},{1,3},{2,0},{3,1},{4,6},{5,7},{6,4},{7,5},{8,10},{9,11},{10,... | collective-permute-start | bytes 1228808 | tf_op jit(solution)/shard_map/ppermute | solution.py:813
  645.1 30.8 %collective-permute-start.167 = (bf16[200,1024]{1,0:T(8,128)(2,1)S(1)}, bf16[200,1024]{1,0:T(8,128)(2,1)}, u32[]{:S(2)}, u32[]{:S(2)}) collective-permute-start(bf16[200,1024]{1,0:T(8,128)(2,1)S(1)} %get-tuple-element.572), channel_id=1, source_target_pairs={{0,8},{4,12},{8,16},{12,20},{16,24},{20,28},{24,0},{28,4},{1,9},{5... | collective-permute-start | bytes 1228808 | tf_op jit(solution)/shard_map/ppermute | solution.py:791
  647.0 29.0 %collective-permute-start.169 = (bf16[200,992]{1,0:T(8,128)(2,1)S(1)}, bf16[200,992]{1,0:T(8,128)(2,1)S(1)}, u32[]{:S(2)}, u32[]{:S(2)}) collective-permute-start(bf16[200,992]{1,0:T(8,128)(2,1)S(1)} %get-tuple-element.576), channel_id=1, source_target_pairs={{0,16},{4,20},{8,24},{12,28},{16,0},{20,4},{24,8},{28,12},{1,17},{... | collective-permute-start | bytes 1190408 | tf_op jit(solution)/shard_map/ppermute | solution.py:791
  681.0 53.9 %collective-permute-start.191 = (bf16[2,200,384]{2,1,0:T(8,128)(2,1)}, bf16[2,200,384]{2,1,0:T(8,128)(2,1)S(1)}, u32[]{:S(2)}, u32[]{:S(2)}) collective-permute-start(bf16[2,200,384]{2,1,0:T(8,128)(2,1)} %collective-permute-done.159.refs_6_), channel_id=1, source_target_pairs={{0,1},{1,0},{2,3},{3,2},{4,5},{5,4},{6,7},{7,6},{8,9},{9,8},{10,11... | collective-permute-start | bytes 921608 | tf_op jit(solution)/shard_map/ppermute | solution.py:1114
  711.0 24.7 %collective-permute-start.190 = (bf16[2,200,384]{2,1,0:T(8,128)(2,1)S(1)}, bf16[2,200,384]{2,1,0:T(8,128)(2,1)S(1)}, u32[]{:S(2)}, u32[]{:S(2)}) collective-permute-start(bf16[2,200,384]{2,1,0:T(8,128)(2,1)S(1)} %collective-permute-done.181.refs_2_), channel_id=1, source_target_pairs={{0,1},{1,0},{2,3},{3,2},{4,5},{5,4},{6,7},{7,6},{8,9},{9,8},{10,11... | collective-permute-start | bytes 921608 | tf_op jit(solution)/shard_map/ppermute | solution.py:1114
  726.3 20.7 %collective-permute-start.192 = (bf16[2,200,992]{2,1,0:T(8,128)(2,1)}, bf16[2,200,992]{2,1,0:T(8,128)(2,1)S(1)}, u32[]{:S(2)}, u32[]{:S(2)}) collective-permute-start(bf16[2,200,992]{2,1,0:T(8,128)(2,1)} %bitcast.322), channel_id=1, source_target_pairs={{0,4},{4,0},{8,12},{12,8},{16,20},{20,16},{24,28},{28,24},{1,5},{5... | collective-permute-start | bytes 2380808 | tf_op jit(solution)/shard_map/ppermute | solution.py:794
  747.2 23.2 %collective-permute-start.195 = (bf16[200,992]{1,0:T(8,128)(2,1)S(1)}, bf16[200,992]{1,0:T(8,128)(2,1)S(1)}, u32[]{:S(2)}, u32[]{:S(2)}) collective-permute-start(bf16[200,992]{1,0:T(8,128)(2,1)S(1)} %get-tuple-element.782), channel_id=1, source_target_pairs={{0,8},{4,12},{8,16},{12,20},{16,24},{20,28},{24,0},{28,4},{1,9},{5... | collective-permute-start | bytes 1190408 | tf_op jit(solution)/shard_map/ppermute | solution.py:791
  749.8 20.7 %collective-permute-start.196 = (bf16[200,992]{1,0:T(8,128)(2,1)S(1)}, bf16[200,992]{1,0:T(8,128)(2,1)S(1)}, u32[]{:S(2)}, u32[]{:S(2)}) collective-permute-start(bf16[200,992]{1,0:T(8,128)(2,1)S(1)} %get-tuple-element.781), channel_id=1, source_target_pairs={{0,24},{4,28},{8,0},{12,4},{16,8},{20,12},{24,16},{28,20},{1,25},{... | collective-permute-start | bytes 1190408 | tf_op jit(solution)/shard_map/ppermute | solution.py:791
  802.6 32.5 %collective-permute-start.212 = (bf16[2,200,384]{2,1,0:T(8,128)(2,1)S(1)}, bf16[2,200,384]{2,1,0:T(8,128)(2,1)}, u32[]{:S(2)}, u32[]{:S(2)}) collective-permute-start(bf16[2,200,384]{2,1,0:T(8,128)(2,1)S(1)} %pad_maximum_fusion.19.refs_5_), channel_id=1, source_target_pairs={{0,1},{1,0},{2,3},{3,2},{4,5},{5,4},{6,7},{7,6},{8,9},{9,8},{10,11... | collective-permute-start | bytes 921608 | tf_op jit(solution)/shard_map/ppermute | solution.py:1113
  809.3 25.8 %collective-permute-start.209 = (bf16[2,200,384]{2,1,0:T(8,128)(2,1)S(1)}, bf16[2,200,384]{2,1,0:T(8,128)(2,1)S(1)}, u32[]{:S(2)}, u32[]{:S(2)}) collective-permute-start(bf16[2,200,384]{2,1,0:T(8,128)(2,1)S(1)} %pad_maximum_fusion.18.refs_1_), channel_id=1, source_target_pairs={{0,1},{1,0},{2,3},{3,2},{4,5},{5,4},{6,7},{7,6},{8,9},{9,8},{10,11... | collective-permute-start | bytes 921608 | tf_op jit(solution)/shard_map/ppermute | solution.py:1113
  (305 other events, 3206.7 us)
